TPU v7x, 128 devices: a whole 4x4x4 slice. The times are simulated.
128 devices in a mesh: dp: 32 (over z, x_hi, y), tensor: 4 (over x_lo, core).
Axes of the slice: x: 4 (x_hi: 2, x_lo: 2; x = x_hi * 2 + x_lo), y: 4, z: 4, core: 2. Of those that a mesh axis runs over, the one named last changes fastest.
Arguments:
- layer_input: float32 [12288, 2048], P('dp', 'tensor'), may hold values from -6 to 6
- attn_norm: float32 [2048], replicated, may hold values from 0.5 to 1.5
- w_query: bfloat16 [2048, 2048], P(None, 'tensor'), may hold values from -0.125 to 0.125
- w_key: bfloat16 [2048, 2048], P(None, 'tensor'), may hold values from -0.125 to 0.125
- w_value: bfloat16 [2048, 2048], P(None, 'tensor'), may hold values from -0.125 to 0.125
- query_norm: float32 [2048], P('tensor'), may hold values from 0.5 to 1.5
- key_norm: float32 [2048], P('tensor'), may hold values from 0.5 to 1.5
- w_output: bfloat16 [2048, 2048], P('tensor'), may hold values from -0.5 to 0.5
- moe_norm: float32 [2048], replicated, may hold values from 0.5 to 1.5
- w_router: bfloat16 [2048, 64], replicated, may hold values from -0.0625 to 0.0625
- w_gate: bfloat16 [64, 2048, 1024], P('dp', None, 'tensor'), may hold values from -0.125 to 0.125
- w_up: bfloat16 [64, 2048, 1024], P('dp', None, 'tensor'), may hold values from -0.125 to 0.125
- w_down: bfloat16 [64, 1024, 2048], P('dp', 'tensor'), may hold values from -0.5 to 0.5
- segments: int32 [32, 384], P('dp'), may hold values from 0 to 5, never falling along the last dimension, each value on 1 to 192 neighbouring positions
- positions: int32 [32, 384], P('dp'), may hold values from 0 to 1535
- routes: int32 [12288, 8], P('dp'), may hold values from 0 to 63, all different within a row; in each aligned block of 384 rows (0 to 383, 384 to 767, ...) at most 56 rows name the same one
- out_grad: float32 [12288, 2048], P('dp', 'tensor'), may hold values from -6 to 6
Outputs:
- layer_output: float32 [12288, 2048], P('dp', 'tensor')
- input_grad: float32 [12288, 2048], P('dp', 'tensor')
- attn_norm_grad: float32 [2048], replicated
- w_query_grad: float32 [2048, 2048], P(None, 'tensor')
- w_key_grad: float32 [2048, 2048], P(None, 'tensor')
- w_value_grad: float32 [2048, 2048], P(None, 'tensor')
- query_norm_grad: float32 [2048], P('tensor')
- key_norm_grad: float32 [2048], P('tensor')
- w_output_grad: float32 [2048, 2048], P('tensor')
- moe_norm_grad: float32 [2048], replicated
- w_router_grad: float32 [2048, 64], replicated
- w_gate_grad: float32 [64, 2048, 1024], P('dp', None, 'tensor')
- w_up_grad: float32 [64, 2048, 1024], P('dp', None, 'tensor')
- w_down_grad: float32 [64, 1024, 2048], P('dp', 'tensor')
Inputs may be any that keep to these rules, and one draw needn't show every extreme that they name: `routes`: each token names 8 different experts. Among the 384 tokens of one sequence no expert is named more than 56 times, and in some sequence an expert is named exactly 56 times. `segments`: within a sequence the numbers never fall.
All inputs are finite; a program needn't handle non-finite values.
Results may differ from a plain program's by a relative error of at most 0.028.
Values may be sent and summed in bfloat16 or wider, within the bound.
A program may use at most 320 MiB of HBM per device.

v0:
```python
import jax
import jax.numpy as jnp
from jax import lax
from jax.sharding import PartitionSpec as P

HDIM = 128
TOP = 8


EPS = 1e-06
HIGH = lax.Precision.HIGHEST


def inv_rms(value):
    return lax.rsqrt(jnp.mean(value * value, axis=-1, keepdims=True) + EPS)


def rope_angles(places):
    half = HDIM // 2
    frequency = jnp.exp(jnp.arange(half, dtype=jnp.float32) * (-2.0 * jnp.log(10000.0) / HDIM))
    angle = places.astype(jnp.float32)[:, None] * frequency[None, :]
    return (jnp.cos(angle)[:, None, :], jnp.sin(angle)[:, None, :])


def rotate(value, cosine, sine):
    half = value.shape[-1] // 2
    first = value[..., :half]
    second = value[..., half:]
    return jnp.concatenate(
        [first * cosine - second * sine, second * cosine + first * sine], axis=-1
    )


def norm_back(pre, scale_head, gain, grad_normed):
    weighted = grad_normed * gain
    pre_grad = scale_head * weighted - pre * scale_head**3 * jnp.mean(
        weighted * pre, axis=-1, keepdims=True
    )
    gain_grad = jnp.sum(grad_normed * pre * scale_head, axis=0).reshape(-1)
    return (pre_grad, gain_grad)


def send_whole(slots):
    return lax.all_to_all(slots, "dp", split_axis=0, concat_axis=1, tiled=True)


def reduce_rows(term):
    return lax.psum_scatter(term, "tensor", scatter_dimension=2, tiled=True)


def attention_scores(query, key, same):
    raw = jnp.einsum("thd,shd->hts", query, key, preferred_element_type=jnp.float32) * HDIM ** (
        -0.5
    )
    return jnp.where(same, raw, -1e30)


def per_device(
    layer_input,
    attn_norm,
    w_query,
    w_key,
    w_value,
    query_norm,
    key_norm,
    w_output,
    moe_norm,
    w_router,
    w_gate,
    w_up,
    w_down,
    segments,
    positions,
    routes,
    out_grad,
):
    length = layer_input.shape[0]
    quarter = layer_input.shape[1]
    start = lax.axis_index("tensor") * quarter
    experts_all = w_gate.shape[0] * lax.axis_size("dp")
    capacity = (length * TOP * 7 // (experts_all * 6) + 7) // 8 * 8
    local_heads = w_query.shape[1] // HDIM
    scale = HDIM ** (-0.5)
    full_in = lax.all_gather(layer_input, "tensor", axis=1, tiled=True)
    first_scale = inv_rms(full_in)
    normed_in = (full_in * first_scale * attn_norm).astype(jnp.bfloat16)
    cosine, sine = rope_angles(positions[0])
    labels = segments[0]
    same = (labels[:, None] == labels[None, :])[None]
    query_pre = jnp.dot(normed_in, w_query, preferred_element_type=jnp.float32).reshape(
        length, local_heads, HDIM
    )
    key_pre = jnp.dot(normed_in, w_key, preferred_element_type=jnp.float32).reshape(
        length, local_heads, HDIM
    )
    query_scale = inv_rms(query_pre)
    key_scale = inv_rms(key_pre)
    query_gain = query_norm.reshape(local_heads, HDIM)
    key_gain = key_norm.reshape(local_heads, HDIM)
    query = rotate(query_pre * query_scale * query_gain, cosine, sine).astype(jnp.bfloat16)
    key = rotate(key_pre * key_scale * key_gain, cosine, sine).astype(jnp.bfloat16)
    values = (
        jnp.dot(normed_in, w_value, preferred_element_type=jnp.float32)
        .astype(jnp.bfloat16)
        .reshape(length, local_heads, HDIM)
    )
    scores = attention_scores(query, key, same)
    highest = jnp.max(scores, axis=-1, keepdims=True)
    powered = jnp.exp(scores - highest)
    total = jnp.sum(powered, axis=-1, keepdims=True)
    log_total = highest + jnp.log(total)
    mixed = jnp.einsum(
        "hts,shd->thd",
        (powered / total).astype(jnp.bfloat16),
        values,
        preferred_element_type=jnp.float32,
    )
    mixed = mixed.reshape(length, local_heads * HDIM).astype(jnp.bfloat16)
    attn = lax.psum(jnp.dot(mixed, w_output, preferred_element_type=jnp.float32), "tensor")
    mid = full_in + attn
    second_scale = inv_rms(mid)
    normed_mid = (mid * second_scale * moe_norm).astype(jnp.bfloat16)
    logits = jnp.dot(normed_mid, w_router, preferred_element_type=jnp.float32)
    chosen = routes[:, :, None] == jnp.arange(experts_all, dtype=jnp.int32)[None, None, :]
    gates = jax.nn.softmax(jnp.sum(jnp.where(chosen, logits[:, None, :], 0.0), axis=2), axis=-1)
    flat_routes = routes.reshape(-1)
    hits = chosen.reshape(length * TOP, experts_all).astype(jnp.int32)
    rank = jnp.sum(jnp.cumsum(hits, axis=0) * hits, axis=1) - 1
    flat_slot = flat_routes * capacity + rank
    owners = jnp.arange(length * TOP, dtype=jnp.int32) // TOP
    table = jnp.full((experts_all, capacity), length, jnp.int32).at[flat_routes, rank].set(owners)
    gate_table = (
        jnp.zeros((experts_all, capacity), jnp.float32).at[flat_routes, rank].set(gates.reshape(-1))
    )
    outgoing = jnp.concatenate(
        [normed_mid, jnp.zeros((1, normed_mid.shape[1]), jnp.bfloat16)], axis=0
    )[table]
    arrived = send_whole(outgoing)
    gate_pre = jnp.einsum("esd,edf->esf", arrived, w_gate, preferred_element_type=jnp.float32)
    up_pre = jnp.einsum("esd,edf->esf", arrived, w_up, preferred_element_type=jnp.float32)
    hidden = (jax.nn.silu(gate_pre) * up_pre).astype(jnp.bfloat16)
    expert_out = reduce_rows(
        jnp.einsum("esf,efd->esd", hidden, w_down, preferred_element_type=jnp.float32)
    ).astype(jnp.bfloat16)
    returned = lax.all_to_all(expert_out, "dp", split_axis=1, concat_axis=0, tiled=True)
    picked = (
        returned.reshape(experts_all * capacity, quarter)[flat_slot]
        .reshape(length, TOP, quarter)
        .astype(jnp.float32)
    )
    layer_output = lax.dynamic_slice_in_dim(mid, start, quarter, 1) + jnp.sum(
        gates[:, :, None] * picked, axis=1
    )
    gate_grad = lax.psum(jnp.sum(out_grad[:, None, :] * picked, axis=2), "tensor")
    pick_grad = gates * (gate_grad - jnp.sum(gates * gate_grad, axis=1, keepdims=True))
    logit_grad = jnp.sum(jnp.where(chosen, pick_grad[:, :, None], 0.0), axis=1)
    w_router_grad = jnp.einsum(
        "td,te->de", normed_mid.astype(jnp.float32), logit_grad, precision=HIGH
    )
    router_back = jnp.einsum("te,de->td", logit_grad, w_router.astype(jnp.float32), precision=HIGH)
    grad_padded = jnp.concatenate([out_grad, jnp.zeros((1, quarter), jnp.float32)], axis=0)
    slot_grad = (gate_table[:, :, None] * grad_padded[table]).astype(jnp.bfloat16)
    grads_in = send_whole(lax.all_gather(slot_grad, "tensor", axis=2, tiled=True))
    w_down_grad = jnp.einsum("esf,esd->efd", hidden, grads_in, preferred_element_type=jnp.float32)
    hidden_grad = jnp.einsum("esd,efd->esf", grads_in, w_down, preferred_element_type=jnp.float32)
    sigmoid_gate = jax.nn.sigmoid(gate_pre)
    gate_pre_grad = (
        hidden_grad * up_pre * sigmoid_gate * (1.0 + gate_pre * (1.0 - sigmoid_gate))
    ).astype(jnp.bfloat16)
    up_pre_grad = (hidden_grad * gate_pre * sigmoid_gate).astype(jnp.bfloat16)
    w_gate_grad = jnp.einsum(
        "esd,esf->edf", arrived, gate_pre_grad, preferred_element_type=jnp.float32
    )
    w_up_grad = jnp.einsum("esd,esf->edf", arrived, up_pre_grad, preferred_element_type=jnp.float32)
    rows_grad_part = jnp.einsum(
        "esf,edf->esd", gate_pre_grad, w_gate, preferred_element_type=jnp.float32
    )
    rows_grad_part = rows_grad_part + jnp.einsum(
        "esf,edf->esd", up_pre_grad, w_up, preferred_element_type=jnp.float32
    )
    rows_grad = lax.all_to_all(
        reduce_rows(rows_grad_part), "dp", split_axis=1, concat_axis=0, tiled=True
    )
    back_rows = jnp.sum(
        rows_grad.reshape(experts_all * capacity, quarter)[flat_slot].reshape(length, TOP, quarter),
        axis=1,
    )
    expert_back, full_out_grad = (
        lax.all_gather(back_rows, "tensor", axis=1, tiled=True),
        lax.all_gather(out_grad, "tensor", axis=1, tiled=True),
    )
    normed_grad = expert_back + router_back
    moe_norm_grad = jnp.sum(normed_grad * mid * second_scale, axis=0)
    weighted = normed_grad * moe_norm
    mid_grad = (
        full_out_grad
        + second_scale * weighted
        - mid * second_scale**3 * jnp.mean(weighted * mid, axis=-1, keepdims=True)
    )
    attn_grad = mid_grad.astype(jnp.bfloat16)
    w_output_grad = jnp.einsum("tc,td->cd", mixed, attn_grad, preferred_element_type=jnp.float32)
    mixed_grad = jnp.einsum("td,cd->tc", attn_grad, w_output, preferred_element_type=jnp.float32)
    mixed_grad = mixed_grad.astype(jnp.bfloat16).reshape(length, local_heads, HDIM)
    probs = jnp.exp(attention_scores(query, key, same) - log_total)
    value_grad = jnp.einsum(
        "hts,thd->shd", probs.astype(jnp.bfloat16), mixed_grad, preferred_element_type=jnp.float32
    ).astype(jnp.bfloat16)
    prob_grad = jnp.einsum("thd,shd->hts", mixed_grad, values, preferred_element_type=jnp.float32)
    score_grad = (probs * (prob_grad - jnp.sum(probs * prob_grad, axis=-1, keepdims=True))).astype(
        jnp.bfloat16
    )
    query_rot_grad = (
        jnp.einsum("hts,shd->thd", score_grad, key, preferred_element_type=jnp.float32) * scale
    )
    key_rot_grad = (
        jnp.einsum("hts,thd->shd", score_grad, query, preferred_element_type=jnp.float32) * scale
    )
    query_pre_grad, query_norm_grad = norm_back(
        query_pre, query_scale, query_gain, rotate(query_rot_grad, cosine, -sine)
    )
    key_pre_grad, key_norm_grad = norm_back(
        key_pre, key_scale, key_gain, rotate(key_rot_grad, cosine, -sine)
    )
    query_low = query_pre_grad.astype(jnp.bfloat16).reshape(length, local_heads * HDIM)
    key_low = key_pre_grad.astype(jnp.bfloat16).reshape(length, local_heads * HDIM)
    value_low = value_grad.reshape(length, local_heads * HDIM)
    w_query_grad = jnp.einsum("tc,tf->cf", normed_in, query_low, preferred_element_type=jnp.float32)
    w_key_grad = jnp.einsum("tc,tf->cf", normed_in, key_low, preferred_element_type=jnp.float32)
    w_value_grad = jnp.einsum("tc,tf->cf", normed_in, value_low, preferred_element_type=jnp.float32)
    in_part = jnp.einsum("tf,cf->tc", query_low, w_query, preferred_element_type=jnp.float32)
    in_part = in_part + jnp.einsum("tf,cf->tc", key_low, w_key, preferred_element_type=jnp.float32)
    in_part = in_part + jnp.einsum(
        "tf,cf->tc", value_low, w_value, preferred_element_type=jnp.float32
    )
    in_grad = lax.psum(in_part.astype(jnp.bfloat16), "tensor").astype(jnp.float32)
    attn_norm_grad = jnp.sum(in_grad * full_in * first_scale, axis=0)
    weighted_in = in_grad * attn_norm
    input_full = (
        mid_grad
        + first_scale * weighted_in
        - full_in * first_scale**3 * jnp.mean(weighted_in * full_in, axis=-1, keepdims=True)
    )
    input_grad = lax.dynamic_slice_in_dim(input_full, start, quarter, 1)
    summed = (
        lax.psum(attn_norm_grad.astype(jnp.bfloat16), "dp").astype(jnp.float32),
        lax.psum(w_query_grad.astype(jnp.bfloat16), "dp").astype(jnp.float32),
        lax.psum(w_key_grad.astype(jnp.bfloat16), "dp").astype(jnp.float32),
        lax.psum(w_value_grad.astype(jnp.bfloat16), "dp").astype(jnp.float32),
        lax.psum(query_norm_grad.astype(jnp.bfloat16), "dp").astype(jnp.float32),
        lax.psum(key_norm_grad.astype(jnp.bfloat16), "dp").astype(jnp.float32),
        lax.psum(w_output_grad.astype(jnp.bfloat16), "dp").astype(jnp.float32),
        lax.psum(moe_norm_grad.astype(jnp.bfloat16), "dp").astype(jnp.float32),
        lax.psum(w_router_grad.astype(jnp.bfloat16), "dp").astype(jnp.float32),
    )
    return (
        layer_output,
        input_grad,
        summed[0],
        summed[1],
        summed[2],
        summed[3],
        summed[4],
        summed[5],
        summed[6],
        summed[7],
        summed[8],
        w_gate_grad,
        w_up_grad,
        w_down_grad,
    )


def solution(mesh):
    placed = (
        P("dp", "tensor"),
        P(),
        P(None, "tensor"),
        P(None, "tensor"),
        P(None, "tensor"),
        P("tensor"),
        P("tensor"),
        P("tensor", None),
        P(),
        P(),
        P("dp", None, "tensor"),
        P("dp", None, "tensor"),
        P("dp", "tensor", None),
        P("dp", None),
        P("dp", None),
        P("dp", None),
        P("dp", "tensor"),
    )
    return jax.shard_map(
        per_device,
        mesh=mesh,
        in_specs=placed,
        out_specs=(
            P("dp", "tensor"),
            P("dp", "tensor"),
            P(),
            P(None, "tensor"),
            P(None, "tensor"),
            P(None, "tensor"),
            P("tensor"),
            P("tensor"),
            P("tensor", None),
            P(),
            P(),
            P("dp", None, "tensor"),
            P("dp", None, "tensor"),
            P("dp", "tensor", None),
        ),
        check_vma=False,
    )
```

profile of v0, /device:TPU:0, one launch (start us, length us, event | category | flops | bytes accessed | tf_op | source)
XLA Modules:
  0.0 2017.4 jit_solution(16437272370064187151)
XLA Ops:
  11.7 38.0 %all-gather.5.cloned.1.call-done = f32[384,2048]{1,0:T(8,128)} async-done(((f32[384,512]{1,0:T(8,128)}), f32[384,2048]{1,0:T(8,128)}) %all-gather.5.cloned.1.call-update) | async-done | bytes 3145744 | tf_op jit(solution)/shard_map/all_gather | solution.py:84
  77.2 31.9 %reduce-window.6 = s32[64,24,128]{2,1,0:T(8,128)S(1)} reduce-window(s32[64,24,128]{2,1,0:T(8,128)} %fusion.27, s32[]{:T(128)} %constant.66.clone.1), window={size=1x1x128 pad=0_0x0_0x127_0}, to_apply=%region_10.11 | reduce-window | flops 24969216 | bytes 1572868 | tf_op jit(solution)/shard_map/reduce-window
  113.4 12.1 scatter_custom_fusion
  137.1 14.3 all-reduce.8.cloned.1.call-done
  178.5 29.3 %gather_fusion = bf16[3584,2048]{1,0:T(8,128)(2,1)} fusion(bf16[385,2048]{1,0:T(8,128)(2,1)} %concatenate.30, s32[4096]{0:T(1024)S(1)} %pad_clamp_fusion), kind=kCustom, calls=%fused_computation | custom fusion | bytes 29374464 | tf_op jit(solution)/shard_map/gather | solution.py:135
  207.8 265.1 %all_to_all.66 = bf16[64,56,2048]{2,1,0:T(8,128)(2,1)} all-to-all(bf16[64,56,2048]{2,1,0:T(8,128)(2,1)} %bitcast.208), channel_id=1, replica_groups=mesh['dp'=32,'tensor'=4] {'dp'}, dimensions={0} | all-to-all | bytes 29360128 | tf_op jit(solution)/shard_map/all_to_all | solution.py:44
  502.1 194.5 %all-to-all-done.2 = bf16[64,56,2048]{2,1,0:T(8,128)(2,1)} async-done(((bf16[64,56,2048]{2,1,0:T(8,128)(2,1)}), bf16[64,56,2048]{2,1,0:T(8,128)(2,1)}, u32[]{:S(2)}, u32[]{:S(2)}) %all-to-all-start.2) | async-done | bytes 14680096 | tf_op jit(solution)/shard_map/all_to_all | solution.py:44
  696.6 13.7 copy.332
  710.3 15.4 multiply_convert_fusion.1
  725.7 16.0 fusion.56
  741.7 21.7 %convolution_add_fusion = f32[2,1792,2048]{2,1,0:T(8,128)} fusion(f32[2,1792,2048]{2,1,0:T(8,128)} %fusion.56, bf16[2,1792,256]{2,1,0:T(8,128)(2,1)S(1)} %copy-done.38, bf16[2,2048,256]{2,1,0:T(8,128)(2,1)S(1)} %copy-done.27), kind=kOutput, calls=%fused_computation.6 | convolution fusion | flops 3765436416 | bytes 62652416 | tf_op jit(solution)/shard_map/esf,edf->esd/dot_general | solution.py:178
  763.5 13.5 fusion.55
  777.1 264.9 %reduce-scatter.5.cloned.1.call-done = f32[2,1792,512]{2,1,0:T(8,128)} async-done(((f32[2,1792,2048]{2,1,0:T(8,128)}), f32[2,1792,512]{2,1,0:T(8,128)}) %reduce-scatter.5.cloned.1.call-update) | async-done | bytes 7340048 | tf_op jit(solution)/shard_map/reduce_scatter | solution.py:48
  1042.0 13.7 copy.333
  1065.4 164.8 %all-to-all-done.3 = f32[2,1792,512]{2,0,1:T(2,128)} async-done(((f32[2,1792,512]{2,0,1:T(2,128)}), f32[2,1792,512]{2,0,1:T(2,128)}, u32[]{:S(2)}, u32[]{:S(2)}) %all-to-all-start.3) | async-done | bytes 7340064 | tf_op jit(solution)/shard_map/all_to_all | solution.py:181
  1237.8 17.3 gather_fusion.3
  1260.3 111.8 %reduce-scatter.3.cloned.1.call-done = f32[2,1792,512]{2,1,0:T(8,128)} async-done(((f32[2,1792,2048]{2,1,0:T(8,128)}), f32[2,1792,512]{2,1,0:T(8,128)}) %reduce-scatter.3.cloned.1.call-update) | async-done | bytes 7340048 | tf_op jit(solution)/shard_map/reduce_scatter | solution.py:48
  1375.7 16.8 copy.328
  1392.5 14.0 all-to-all-start.1
  1410.6 64.3 %all-to-all-done.1 = bf16[2,1792,512]{2,0,1:T(2,128)(2,1)} async-done(((bf16[2,1792,512]{2,0,1:T(2,128)(2,1)}), bf16[2,1792,512]{2,0,1:T(2,128)(2,1)}, u32[]{:S(2)}, u32[]{:S(2)}) %all-to-all-start.1) | async-done | bytes 3670048 | tf_op jit(solution)/shard_map/all_to_all | solution.py:145
  1479.6 15.9 gather_fusion.1
  1564.9 11.8 fusion.60
  1607.8 183.7 %all-reduce.2 = (bf16[2048]{0:T(1024)(128)(2,1)S(1)}, bf16[512]{0:T(512)(128)(2,1)S(1)}, bf16[512]{0:T(512)(128)(2,1)S(1)}, bf16[2048]{0:T(1024)(128)(2,1)S(1)}) all-reduce(bf16[2048]{0:T(1024)(128)(2,1)S(1)} %get-tuple-element.16, bf16[512]{0:T(512)(128)(2,1)S(1)} %get-tuple-element.36, ...), channel_id=1, replica_groups=mesh['dp'=32,'tensor'=4] {'dp'}, use_global_device_ids=true, to_apply=%region_30.31 | all-reduce | flops 5120 | bytes 20480 | tf_op jit(solution)/shard_map/psum | solution.py:245
  1796.6 199.9 %all-reduce.12.cloned.1.call-done = (bf16[2048,512]{1,0:T(8,128)(2,1)}, bf16[2048,512]{1,0:T(8,128)(2,1)}, bf16[2048,512]{1,0:T(8,128)(2,1)}, bf16[512,2048]{1,0:T(8,128)(2,1)}, bf16[2048,64]{0,1:T(8,128)(2,1)}) async-done(((bf16[2048,512]{1,0:T(8,128)(2,1)}, bf16[2048,512]{1,0:T(8,128)(2,1)}, bf16[2048,512]{1,0:T(8,128)(2,1)}, bf16[512,2048]{1,0:T(8,128)(2,1)}, bf16[2048,64]{0,1:T(8,128)(2,1)}), ...) | async-done | bytes 8650768 | tf_op jit(solution)/shard_map/psum | solution.py:246
  (352 shorter events, 257.4 us)
Async XLA Ops:
  7.2 703.1 %copy-start = (bf16[2,256,2048]{2,1,0:T(8,128)(2,1)S(1)}, bf16[2,256,2048]{2,1,0:T(8,128)(2,1)}, u32[]{:S(2)}) copy-start(bf16[2,256,2048]{2,1,0:T(8,128)(2,1)} %param.29) | copy-start | bytes 6291460
  7.2 45.4 %copy-start.77 = (f32[2048]{0:T(1024)S(1)}, f32[2048]{0:T(1024)}, u32[]{:S(2)}) copy-start(f32[2048]{0:T(1024)} %param.18) | copy-start | bytes 24580
  7.2 42.4 %all-gather.5.cloned.1.call-start = ((), (), s32[]{:S(2)}) async-start(), calls=%async_computation.6 | async-start | bytes 3932160 | tf_op jit(solution)/shard_map/all_gather | solution.py:84
  7.9 143.5 %all-reduce.8.cloned.1.call-start = ((), (), s32[]{:S(2)}) async-start(), calls=%async_computation.7 | async-start | bytes 6291456 | tf_op jit(solution)/shard_map/psum | solution.py:119
  11.7 57.0 %copy-start.40 = (f32[384,64]{1,0:T(8,128)}, f32[384,64]{1,0:T(8,128)S(1)}, u32[]{:S(2)}) copy-start(f32[384,64]{1,0:T(8,128)S(1)} %get-tuple-element.66) | copy-start | bytes 294916
  75.7 397.3 %all-gather.9.cloned.1.call-start = ((), (), s32[]{:S(2)}) async-start(), calls=%async_computation.10 | async-start | bytes 18350080 | tf_op jit(solution)/shard_map/all_gather | solution.py:163
  77.2 36.0 %copy-start.94 = (s32[2]{0:T(128)S(1)}, s32[2]{0:T(128)}, u32[]{:S(2)}) copy-start(s32[2]{0:T(128)} %constant.91) | copy-start | bytes 28
  77.2 36.1 %copy-start.93 = (s32[2]{0:T(128)S(1)}, s32[2]{0:T(128)}, u32[]{:S(2)}) copy-start(s32[2]{0:T(128)} %constant.94) | copy-start | bytes 28
  137.1 18.2 copy-start.64
  472.9 223.7 %all-to-all-start.2 = ((bf16[64,56,2048]{2,1,0:T(8,128)(2,1)}), bf16[64,56,2048]{2,1,0:T(8,128)(2,1)}, u32[]{:S(2)}, u32[]{:S(2)}) async-start(bf16[64,56,2048]{2,1,0:T(8,128)(2,1)} %all-gather.9.cloned.1.call-done), calls=%async_computation.3 | async-start | bytes 29360128 | tf_op jit(solution)/shard_map/all_to_all | solution.py:44
  478.0 564.0 %reduce-scatter.5.cloned.1.call-start = ((), (), s32[]{:S(2)}) async-start(), calls=%async_computation.11 | async-start | bytes 36700160 | tf_op jit(solution)/shard_map/reduce_scatter | solution.py:48
  763.5 608.6 %reduce-scatter.3.cloned.1.call-start = ((), (), s32[]{:S(2)}) async-start(), calls=%async_computation.8 | async-start | bytes 36700160 | tf_op jit(solution)/shard_map/reduce_scatter | solution.py:48
  1055.7 174.5 %all-to-all-start.3 = ((f32[2,1792,512]{2,0,1:T(2,128)}), f32[2,1792,512]{2,0,1:T(2,128)}, u32[]{:S(2)}, u32[]{:S(2)}) async-start(f32[2,1792,512]{2,0,1:T(2,128)} %copy.333), calls=%async_computation.5 | async-start | bytes 14680064 | tf_op jit(solution)/shard_map/all_to_all | solution.py:181
  1065.4 446.0 %all-gather.11.cloned.1.call-start = ((), (), s32[]{:S(2)}) async-start(), calls=%async_computation.12 | async-start | bytes 3932160 | tf_op jit(solution)/shard_map/all_gather | solution.py:189
  1392.4 17.3 copy-start.86
  1392.4 18.1 copy-start.67
  1392.4 18.1 copy-start.84
  1392.5 82.4 %all-to-all-start.1 = ((bf16[2,1792,512]{2,0,1:T(2,128)(2,1)}), bf16[2,1792,512]{2,0,1:T(2,128)(2,1)}, u32[]{:S(2)}, u32[]{:S(2)}) async-start(bf16[2,1792,512]{2,0,1:T(2,128)(2,1)} %copy.328), calls=%async_computation.2 | async-start | bytes 7340032 | tf_op jit(solution)/shard_map/all_to_all | solution.py:145
  1406.4 111.5 %all-gather.7.cloned.1.call-start = ((), (), s32[]{:S(2)}) async-start(), calls=%async_computation.9 | async-start | bytes 3932160 | tf_op jit(solution)/shard_map/all_gather | solution.py:190
  1407.2 195.8 %all-reduce.10.cloned.1.call-start = ((), (), s32[]{:S(2)}) async-start(), calls=%async_computation.13 | async-start | bytes 3145728 | tf_op jit(solution)/shard_map/psum | solution.py:235
  1549.6 446.9 %all-reduce.12.cloned.1.call-start = ((), (), s32[]{:S(2)}) async-start(), calls=%async_computation.14 | async-start | bytes 17301504 | tf_op jit(solution)/shard_map/psum | solution.py:246
  1564.9 23.4 %slice-start = ((s8[14680064]{0:T(1024)(128)(4,1)}), s8[4194304]{0:T(1024)(128)(4,1)S(1)}, s32[]{:S(2)}) async-start(s8[14680064]{0:T(1024)(128)(4,1)} %bitcast.205), calls=%async_computation.15 | async-start | bytes 8388608
  1564.9 23.4 %slice-start.1 = ((s8[14680064]{0:T(1024)(128)(4,1)}), s8[4194304]{0:T(1024)(128)(4,1)S(1)}, s32[]{:S(2)}) async-start(s8[14680064]{0:T(1024)(128)(4,1)} %bitcast.205), calls=%async_computation.16 | async-start | bytes 8388608
  1596.3 197.6 %copy-start.91 = (f32[384]{0:T(512)S(1)}, f32[384]{0:T(512)}, u32[]{:S(2)}) copy-start(f32[384]{0:T(512)} %get-tuple-element.67) | copy-start | bytes 4612
  (87 other events, 498.3 us)
Sparse Core Ops, SparseCore 0:
  9.7 39.8 all-gather.4
  75.8 75.6 all-reduce.7
  175.9 226.2 all-gather.8
  763.6 278.3 reduce-scatter.4
  1044.5 327.5 reduce-scatter.2
  1374.2 53.0 all-gather.10
  1429.0 53.7 all-gather.6
  1549.7 53.2 all-reduce.9
  1606.5 390.0 all-reduce.11
where the time goes:
time: 2030 us; the launch traced here: 2020 us
  waiting for transfers between devices  1060 us (52%)
  blocking collectives  460 us (23%)
  local copies, waits for them, and re-layouts  191 us (9%)
  matrix products  152 us (7%)
  other arithmetic  110 us (5%)
  starting transfers between devices  29.1 us (1%)
    reduce_scatter x2, waiting for transfers between devices, reduce_rows(): return lax.psum_scatter(term, 'tensor', scatter_dimension=2, tiled=True)  377 us
    all_to_all x1, blocking collectives, send_whole(): return lax.all_to_all(slots, 'dp', split_axis=0, concat_axis=1, tiled=True)  265 us
    psum x1, waiting for transfers between devices, per_device(): lax.psum(w_query_grad.astype(jnp.bfloat16), 'dp').astype(jnp.float32)  200 us
    all_to_all x1, waiting for transfers between devices, send_whole(): return lax.all_to_all(slots, 'dp', split_axis=0, concat_axis=1, tiled=True)  194 us
    psum x1, blocking collectives, per_device(): lax.psum(attn_norm_grad.astype(jnp.bfloat16), 'dp').astype(jnp.float32)  184 us
    all_to_all x1, waiting for transfers between devices, per_device(): lax.all_to_all(reduce_rows(rows_grad_part), 'dp', split_axis=1, concat_ax...  165 us
    all_to_all x1, waiting for transfers between devices, per_device(): lax.all_to_all(expert_out, 'dp', split_axis=1, concat_axis=0, tiled=True)  64.3 us
  transfers between devices with their start and end apart: 12, of which 9 were waited for; matrix products, arithmetic and copies ran while one was open for 14% of the time, Pallas kernels for 0%

commit v1 on v0

v1 whole, which is shorter than its diff:
```python
import jax
import jax.numpy as jnp
from jax import lax
from jax.sharding import PartitionSpec as P

HDIM = 128
TOP = 8
SLOTS = 64
HALF = SLOTS // 2
EPS = 1e-06
HIGH = lax.Precision.HIGHEST
F32 = jnp.float32
BF16 = jnp.bfloat16


def dot(a, b, dims, **kw):
    return lax.dot_general(a, b, (dims, ((), ())), preferred_element_type=F32, **kw)


def nn(a, b):
    return dot(a, b, ((1,), (0,)))


def nt(a, b):
    return dot(a, b, ((1,), (1,)))


def tn(a, b):
    return dot(a, b, ((0,), (0,)))


def cross(value):
    return lax.ppermute(value, "tensor", [(0, 2), (2, 0), (1, 3), (3, 1)])


def swap(value):
    return lax.ppermute(value, "tensor", [(0, 1), (1, 0), (2, 3), (3, 2)])


def inv_rms(value):
    return lax.rsqrt(jnp.mean(value * value, axis=-1, keepdims=True) + EPS)


def rope_angles(places):
    half = HDIM // 2
    frequency = jnp.exp(jnp.arange(half, dtype=F32) * (-2.0 * jnp.log(10000.0) / HDIM))
    angle = places.astype(F32)[:, None] * frequency[None, :]
    return (jnp.cos(angle)[:, None, :], jnp.sin(angle)[:, None, :])


def rotate(value, cosine, sine):
    half = value.shape[-1] // 2
    first = value[..., :half]
    second = value[..., half:]
    return jnp.concatenate(
        [first * cosine - second * sine, second * cosine + first * sine], axis=-1
    )


def norm_back(pre, scale_head, gain, grad_normed):
    weighted = grad_normed * gain
    pre_grad = scale_head * weighted - pre * scale_head**3 * jnp.mean(
        weighted * pre, axis=-1, keepdims=True
    )
    gain_grad = jnp.sum(grad_normed * pre * scale_head, axis=0).reshape(-1)
    return (pre_grad, gain_grad)


def attention_scores(query, key, same):
    raw = jnp.einsum("thd,shd->hts", query, key, preferred_element_type=F32) * HDIM ** (-0.5)
    return jnp.where(same, raw, -1e30)


def per_device(
    layer_input,
    attn_norm,
    w_query,
    w_key,
    w_value,
    query_norm,
    key_norm,
    w_output,
    moe_norm,
    w_router,
    w_gate,
    w_up,
    w_down,
    segments,
    positions,
    routes,
    out_grad,
):
    length, quarter = layer_input.shape
    width = 4 * quarter
    rank_t = lax.axis_index("tensor")
    side = rank_t // 2
    core = rank_t % 2
    first_side = side == 0
    first_core = core == 0
    groups = lax.axis_size("dp")
    experts = 2 * groups
    local_heads = w_query.shape[1] // HDIM
    scale = HDIM ** (-0.5)

    def own(vector):
        return lax.dynamic_slice_in_dim(vector, rank_t * quarter, quarter, 0)

    def gather(mine):
        far = cross(mine)
        near = swap(mine)
        near_far = swap(far)
        a = jnp.where(first_side, mine, far)
        b = jnp.where(first_side, far, mine)
        c = jnp.where(first_side, near, near_far)
        d = jnp.where(first_side, near_far, near)
        return jnp.concatenate(
            [
                jnp.where(first_core, a, c),
                jnp.where(first_core, c, a),
                jnp.where(first_core, b, d),
                jnp.where(first_core, d, b),
            ],
            axis=1,
        )

    def scatter_sum(part):
        p0, p1, p2, p3 = (part[:, i * quarter : (i + 1) * quarter] for i in range(4))
        sent = jnp.where(
            first_core, jnp.concatenate([p1, p3], axis=1), jnp.concatenate([p0, p2], axis=1)
        ).astype(BF16)
        got = swap(sent).astype(F32)
        low_half = jnp.where(first_core, p0, p1) + got[:, :quarter]
        high_half = jnp.where(first_core, p2, p3) + got[:, quarter:]
        back = cross(jnp.where(first_side, high_half, low_half).astype(BF16))
        return jnp.where(first_side, low_half, high_half) + back.astype(F32)

    def sum_tensor(value):
        value = value + swap(value)
        return value + cross(value)

    def pick(pair, which):
        return jnp.where(which, pair[0], pair[1])

    quarters = []
    for w in (w_gate, w_up, w_down):
        mine = pick(w, first_side)
        far = cross(pick(w, jnp.logical_not(first_side)))
        quarters.append((mine, far, swap(mine), swap(far)))

    experts_row = jnp.arange(experts, dtype=jnp.int32)
    chosen = jnp.any(routes[:, :, None] == experts_row[None, None, :], axis=1)
    chosen_low = chosen.astype(BF16)
    before = (jnp.arange(length)[:, None] > jnp.arange(length)[None, :]).astype(BF16)
    rank = nn(before, chosen_low).astype(jnp.int32)
    place = jnp.where(chosen, rank, -1).reshape(length, groups, 2)
    place = jnp.where(first_side, place[:, :, 0], place[:, :, 1]).T
    spots = core * HALF + jnp.arange(HALF, dtype=jnp.int32)
    select = (
        (place[:, None, :] == spots[None, :, None]).astype(BF16).reshape(groups * HALF, length)
    )

    def to_experts(rows):
        return lax.all_to_all(
            rows.reshape(groups, HALF, rows.shape[-1]), "dp", split_axis=0, concat_axis=0, tiled=True
        ).reshape(groups * HALF, rows.shape[-1])

    grad_full = gather(out_grad.astype(BF16))
    grad_rows = to_experts(nn(select, grad_full).astype(BF16))

    in_full = gather(layer_input.astype(BF16)).astype(F32)
    first_scale = inv_rms(in_full)
    normed_in = (in_full * first_scale * attn_norm).astype(BF16)
    cosine, sine = rope_angles(positions[0])
    labels = segments[0]
    same = (labels[:, None] == labels[None, :])[None]
    query_pre = nn(normed_in, w_query).reshape(length, local_heads, HDIM)
    key_pre = nn(normed_in, w_key).reshape(length, local_heads, HDIM)
    query_scale = inv_rms(query_pre)
    key_scale = inv_rms(key_pre)
    query_gain = query_norm.reshape(local_heads, HDIM)
    key_gain = key_norm.reshape(local_heads, HDIM)
    query = rotate(query_pre * query_scale * query_gain, cosine, sine).astype(BF16)
    key = rotate(key_pre * key_scale * key_gain, cosine, sine).astype(BF16)
    values = nn(normed_in, w_value).astype(BF16).reshape(length, local_heads, HDIM)
    scores = attention_scores(query, key, same)
    highest = jnp.max(scores, axis=-1, keepdims=True)
    powered = jnp.exp(scores - highest)
    total = jnp.sum(powered, axis=-1, keepdims=True)
    log_total = highest + jnp.log(total)
    mixed = jnp.einsum(
        "hts,shd->thd", (powered / total).astype(BF16), values, preferred_element_type=F32
    )
    mixed = mixed.reshape(length, local_heads * HDIM).astype(BF16)
    mid = layer_input + scatter_sum(nn(mixed, w_output))
    mid_full = gather(mid.astype(BF16)).astype(F32)
    second_scale = inv_rms(mid_full)
    normed_mid = (mid_full * second_scale * moe_norm).astype(BF16)

    logits = nn(normed_mid, w_router)
    masked = jnp.where(chosen, logits, -1e30)
    raised = jnp.where(chosen, jnp.exp(masked - jnp.max(masked, axis=1, keepdims=True)), 0.0)
    gates = raised / jnp.sum(raised, axis=1, keepdims=True)
    gates_side = gates.reshape(length, groups, 2)
    gates_side = jnp.where(first_side, gates_side[:, :, 0], gates_side[:, :, 1])
    select_cube = select.reshape(groups, HALF, length).astype(F32)
    slot_gates = jnp.sum(select_cube * gates_side.T[:, None, :], axis=2)
    rows = to_experts(nn(select, normed_mid).astype(BF16))
    slot_gates = lax.all_to_all(slot_gates, "dp", split_axis=0, concat_axis=0, tiled=True)
    slot_gates = slot_gates.reshape(groups * HALF, 1)

    expert_out = 0.0
    saved = []
    for i in range(4):
        gate_w, up_w, down_w = (w[i] for w in quarters)
        gate_pre = nn(rows, gate_w)
        up_pre = nn(rows, up_w)
        hidden = jax.nn.silu(gate_pre) * up_pre
        expert_out = expert_out + nn(hidden.astype(BF16), down_w)
        saved.append((gate_pre, up_pre, hidden))
    expert_out = expert_out.astype(BF16)
    slot_grad = jnp.sum(grad_rows.astype(F32) * expert_out.astype(F32), axis=1)
    rows_grad = 0.0
    weight_grads = []
    for i in range(4):
        gate_w, up_w, down_w = (w[i] for w in quarters)
        gate_pre, up_pre, hidden = saved[i]
        hidden_grad = slot_gates * nt(grad_rows, down_w)
        sig = jax.nn.sigmoid(gate_pre)
        gate_pre_grad = (hidden_grad * up_pre * sig * (1.0 + gate_pre * (1.0 - sig))).astype(BF16)
        up_pre_grad = (hidden_grad * gate_pre * sig).astype(BF16)
        rows_grad = rows_grad + nt(gate_pre_grad, gate_w) + nt(up_pre_grad, up_w)
        weight_grads.append(
            (
                tn(rows, gate_pre_grad),
                tn(rows, up_pre_grad),
                tn((slot_gates * hidden).astype(BF16), grad_rows),
            )
        )

    def from_experts(value):
        return lax.all_to_all(
            value.astype(BF16).reshape(groups, HALF, width), "dp", split_axis=0, concat_axis=0, tiled=True
        ).reshape(groups * HALF, width)

    slot_grad = lax.all_to_all(
        slot_grad.reshape(groups, HALF), "dp", split_axis=0, concat_axis=0, tiled=True
    )
    back_rows = from_experts(rows_grad)
    returned = from_experts(expert_out)

    expert_grads = []
    for i in range(3):
        mine, far, near, near_far = (weight_grads[j][i] for j in range(4))
        mine = mine + swap(near.astype(BF16)).astype(F32)
        far = far + swap(near_far.astype(BF16)).astype(F32)
        other = cross(far.astype(BF16)).astype(F32)
        expert_grads.append(
            jnp.stack([jnp.where(first_side, mine, other), jnp.where(first_side, other, mine)])
        )

    gate_grad = jnp.sum(select_cube * slot_grad[:, :, None], axis=1).T
    zero = jnp.zeros_like(gate_grad)
    gate_grad = jnp.stack(
        [jnp.where(first_side, gate_grad, zero), jnp.where(first_side, zero, gate_grad)], axis=2
    ).reshape(length, experts)
    gate_grad = sum_tensor(gate_grad)
    logit_grad = gates * (gate_grad - jnp.sum(gates * gate_grad, axis=1, keepdims=True))
    normed_mid_own = lax.dynamic_slice_in_dim(normed_mid, rank_t * quarter, quarter, 1)
    w_router_own = lax.dynamic_slice_in_dim(w_router, rank_t * quarter, quarter, 0)
    w_router_grad = dot(
        normed_mid_own.astype(F32), logit_grad, ((0,), (0,)), precision=HIGH
    )
    router_back = dot(logit_grad, w_router_own.astype(F32), ((1,), (1,)), precision=HIGH)
    normed_grad = scatter_sum(tn(select, back_rows)) + router_back
    moe_norm_grad = jnp.sum(
        normed_grad * mid * second_scale, axis=0
    )
    normed_grad_full = gather(normed_grad.astype(BF16)).astype(F32)
    weighted_full = normed_grad_full * moe_norm
    shrink = second_scale**3 * jnp.mean(weighted_full * mid_full, axis=-1, keepdims=True)
    attn_grad = (
        grad_full.astype(F32) + second_scale * weighted_full - mid_full * shrink
    ).astype(BF16)
    mid_grad = out_grad + second_scale * (normed_grad * own(moe_norm)) - mid * shrink

    select_gated = (select_cube * gates_side.T[:, None, :]).reshape(groups * HALF, length)
    layer_output = mid + scatter_sum(tn(select_gated.astype(BF16), returned))

    w_output_grad = tn(mixed, attn_grad)
    mixed_grad = nt(attn_grad, w_output).astype(BF16).reshape(length, local_heads, HDIM)
    probs = jnp.exp(scores - log_total)
    value_grad = jnp.einsum(
        "hts,thd->shd", probs.astype(BF16), mixed_grad, preferred_element_type=F32
    ).astype(BF16)
    prob_grad = jnp.einsum("thd,shd->hts", mixed_grad, values, preferred_element_type=F32)
    score_grad = (probs * (prob_grad - jnp.sum(probs * prob_grad, axis=-1, keepdims=True))).astype(
        BF16
    )
    query_rot_grad = jnp.einsum("hts,shd->thd", score_grad, key, preferred_element_type=F32) * scale
    key_rot_grad = jnp.einsum("hts,thd->shd", score_grad, query, preferred_element_type=F32) * scale
    query_pre_grad, query_norm_grad = norm_back(
        query_pre, query_scale, query_gain, rotate(query_rot_grad, cosine, -sine)
    )
    key_pre_grad, key_norm_grad = norm_back(
        key_pre, key_scale, key_gain, rotate(key_rot_grad, cosine, -sine)
    )
    query_low = query_pre_grad.astype(BF16).reshape(length, local_heads * HDIM)
    key_low = key_pre_grad.astype(BF16).reshape(length, local_heads * HDIM)
    value_low = value_grad.reshape(length, local_heads * HDIM)
    w_query_grad = tn(normed_in, query_low)
    w_key_grad = tn(normed_in, key_low)
    w_value_grad = tn(normed_in, value_low)
    in_part = nt(query_low, w_query) + nt(key_low, w_key) + nt(value_low, w_value)
    in_grad = scatter_sum(in_part)
    attn_norm_grad = jnp.sum(in_grad * layer_input * first_scale, axis=0)
    weighted_in = in_grad * own(attn_norm)
    mean_in = sum_tensor(jnp.sum(weighted_in * layer_input, axis=-1, keepdims=True)) / width
    input_grad = mid_grad + first_scale * weighted_in - layer_input * first_scale**3 * mean_in

    stacked = jnp.concatenate(
        [w_output_grad[:, i * quarter : (i + 1) * quarter] for i in range(4)]
        + [w_query_grad, w_key_grad, w_value_grad, w_router_grad.T]
        + [jnp.stack([attn_norm_grad, moe_norm_grad, query_norm_grad, key_norm_grad])],
        axis=0,
    ).astype(BF16)
    n_rows = stacked.shape[0]
    piece = -(-n_rows // (groups * 16)) * 16
    stacked = jnp.pad(stacked, ((0, groups * piece - n_rows), (0, 0)))
    pieces = lax.all_to_all(
        stacked.reshape(groups, piece, quarter), "dp", split_axis=0, concat_axis=0, tiled=True
    )
    whole = jnp.sum(pieces.astype(F32), axis=0).astype(BF16)
    big = lax.all_gather(whole, "dp", axis=0, tiled=True)
    base = width + 3 * w_query.shape[0]
    small = big[base : base + experts + 4]
    everywhere = lax.all_gather(small[: experts + 2], "tensor", axis=1, tiled=True).astype(F32)
    rows_w = w_query.shape[0]
    rows_o = w_output.shape[0]
    summed = [big[width + i * rows_w : width + (i + 1) * rows_w].astype(F32) for i in range(3)]
    output_grad = jnp.concatenate(
        [big[i * rows_o : (i + 1) * rows_o] for i in range(4)], axis=1
    ).astype(F32)
    return (
        layer_output,
        input_grad,
        everywhere[experts],
        summed[0],
        summed[1],
        summed[2],
        small[experts + 2].astype(F32),
        small[experts + 3].astype(F32),
        output_grad,
        everywhere[experts + 1],
        everywhere[:experts].T,
        expert_grads[0],
        expert_grads[1],
        expert_grads[2],
    )


def solution(mesh):
    placed = (
        P("dp", "tensor"),
        P(),
        P(None, "tensor"),
        P(None, "tensor"),
        P(None, "tensor"),
        P("tensor"),
        P("tensor"),
        P("tensor", None),
        P(),
        P(),
        P("dp", None, "tensor"),
        P("dp", None, "tensor"),
        P("dp", "tensor", None),
        P("dp", None),
        P("dp", None),
        P("dp", None),
        P("dp", "tensor"),
    )
    return jax.shard_map(
        per_device,
        mesh=mesh,
        in_specs=placed,
        out_specs=(
            P("dp", "tensor"),
            P("dp", "tensor"),
            P(),
            P(None, "tensor"),
            P(None, "tensor"),
            P(None, "tensor"),
            P("tensor"),
            P("tensor"),
            P("tensor", None),
            P(),
            P(),
            P("dp", None, "tensor"),
            P("dp", None, "tensor"),
            P("dp", "tensor", None),
        ),
        check_vma=False,
    )
```

time: 2030 us -> 925 us (0.46)
  waiting for transfers between devices: 1060 us -> 263 us
  blocking collectives: 460 us -> 185 us
  local copies, waits for them, and re-layouts: 191 us -> 74.5 us
  matrix products: 152 us -> 236 us
  other arithmetic: 110 us -> 76.7 us
  starting transfers between devices: 29.1 us -> 61.9 us
    all_to_all x3 -> x4, waiting for transfers between devices: 424 us -> 23.9 us  [the longest x2 14.3 us: to_experts(): lax.all_to_all(rows.reshape(groups, HALF, rows.shape[-1]), 'dp', split_ax...]
    reduce_scatter x2 -> x0, waiting for transfers between devices: 377 us -> none  [reduce_rows(): return lax.psum_scatter(term, 'tensor', scatter_dimension=2, tiled=True)]
    ppermute x0 -> x42, waiting for transfers between devices: none -> 237 us  [the longest x16 235 us: cross(): return lax.ppermute(value, 'tensor', [(0, 2), (2, 0), (1, 3), (3, 1)])]
    psum x3 -> x0, waiting for transfers between devices: 221 us -> none  [the longest x1 200 us: per_device(): lax.psum(w_query_grad.astype(jnp.bfloat16), 'dp').astype(jnp.float32)]
    psum x2 -> x0, blocking collectives: 194 us -> none  [the longest x1 184 us: per_device(): lax.psum(attn_norm_grad.astype(jnp.bfloat16), 'dp').astype(jnp.float32)]
    all_to_all x1 -> x3, blocking collectives: 265 us -> 179 us  [the longest x1 114 us: per_device(): lax.all_to_all(stacked.reshape(groups, piece, quarter), 'dp', split_axis=...]
    dot_general x30 -> x62, matrix products: 152 us -> 236 us  [the longest x56 229 us: dot(): lax.dot_general(a, b, (dims, ((), ())), preferred_element_type=F32, **kw)]
    gather x4 -> x0, local copies, waits for them, and re-layouts: 72.7 us -> none  [the longest x1 29.3 us: per_device(): jnp.concatenate([normed_mid, jnp.zeros((1, normed_mid.shape[1]), jnp.bflo...]
  transfers between devices with their start and end apart: 12 -> 47, of which waited for: 9 -> 19; matrix products, arithmetic and copies ran while one was open for 14% -> 20% of each run, Pallas kernels for 0% -> 0%
where the time goes in v1:
time: 925 us; the launch traced here: 913 us
  waiting for transfers between devices  263 us (28%)
  matrix products  236 us (26%)
  blocking collectives  185 us (20%)
  other arithmetic  76.7 us (8%)
  local copies, waits for them, and re-layouts  74.5 us (8%)
  starting transfers between devices  61.9 us (7%)
  between operations  16.7 us (2%)
    ppermute x16, waiting for transfers between devices, cross(): return lax.ppermute(value, 'tensor', [(0, 2), (2, 0), (1, 3), (3, 1)])  235 us
    dot_general x56, matrix products, dot(): lax.dot_general(a, b, (dims, ((), ())), preferred_element_type=F32, **kw)  229 us
    all_to_all x1, blocking collectives, per_device(): lax.all_to_all(stacked.reshape(groups, piece, quarter), 'dp', split_axis=...  114 us
    all_to_all x1, blocking collectives, from_experts(): lax.all_to_all(value.astype(BF16).reshape(groups, HALF, width), 'dp', spl...  52.1 us
    concatenate x1, local copies, waits for them, and re-layouts, per_device(): jnp.concatenate([w_output_grad[:, i * quarter:(i + 1) * quarter] for i in...  36.9 us
    ppermute x16, starting transfers between devices, cross(): return lax.ppermute(value, 'tensor', [(0, 2), (2, 0), (1, 3), (3, 1)])  22.2 us
    all_to_all x2, starting transfers between devices, to_experts(): lax.all_to_all(rows.reshape(groups, HALF, rows.shape[-1]), 'dp', split_ax...  20.6 us
  transfers between devices with their start and end apart: 47, of which 19 were waited for; matrix products, arithmetic and copies ran while one was open for 20% of the time, Pallas kernels for 0%

profile of v1, /device:TPU:0, one launch (start us, length us, event | category | flops | bytes accessed | tf_op | source)
XLA Modules:
  0.0 913.3 jit_solution(4266409601305887784)
XLA Ops:
  11.7 7.6 collective-permute-done
  51.3 9.6 %collective-permute-done.4 = bf16[384,512]{1,0:T(8,128)(2,1)S(1)} collective-permute-done((bf16[384,512]{1,0:T(8,128)(2,1)S(1)}, bf16[384,512]{1,0:T(8,128)(2,1)S(1)}, u32[]{:S(2)}, u32[]{:S(2)}) %collective-permute-start.4) | collective-permute-done | bytes 393248 | tf_op jit(solution)/shard_map/ppermute | solution.py:33
  64.1 8.5 collective-permute-done.5
  81.6 11.2 %all-to-all-start = ((bf16[32,32,2048]{2,1,0:T(8,128)(2,1)}), bf16[32,32,2048]{2,1,0:T(8,128)(2,1)}, u32[]{:S(2)}, u32[]{:S(2)}) async-start(bf16[32,32,2048]{2,1,0:T(8,128)(2,1)} %bitcast.277), calls=%async_computation | async-start | bytes 8388608 | tf_op jit(solution)/shard_map/all_to_all | solution.py:163
  102.0 51.2 %collective-permute-done.19 = bf16[384,512]{1,0:T(8,128)(2,1)} collective-permute-done((bf16[384,512]{1,0:T(8,128)(2,1)}, bf16[384,512]{1,0:T(8,128)(2,1)}, u32[]{:S(2)}, u32[]{:S(2)}) %collective-permute-start.19) | collective-permute-done | bytes 393248 | tf_op jit(solution)/shard_map/ppermute | solution.py:33
  164.2 9.5 %all-to-all-start.3 = ((bf16[32,32,2048]{2,1,0:T(8,128)(2,1)}), bf16[32,32,2048]{2,1,0:T(8,128)(2,1)}, u32[]{:S(2)}, u32[]{:S(2)}) async-start(bf16[32,32,2048]{2,1,0:T(8,128)(2,1)} %bitcast.278), calls=%async_computation.3 | async-start | bytes 8388608 | tf_op jit(solution)/shard_map/all_to_all | solution.py:163
  181.6 16.6 %collective-permute-done.8 = bf16[2048,256]{1,0:T(8,128)(2,1)} collective-permute-done((bf16[2048,256]{1,0:T(8,128)(2,1)}, bf16[2048,256]{1,0:T(8,128)(2,1)}, u32[]{:S(2)}, u32[]{:S(2)}) %collective-permute-start.8) | collective-permute-done | bytes 1048608 | tf_op jit(solution)/shard_map/ppermute | solution.py:33
  206.3 14.4 %collective-permute-done.10 = bf16[256,2048]{1,0:T(8,128)(2,1)} collective-permute-done((bf16[256,2048]{1,0:T(8,128)(2,1)}, bf16[256,2048]{1,0:T(8,128)(2,1)}, u32[]{:S(2)}, u32[]{:S(2)}) %collective-permute-start.10) | collective-permute-done | bytes 1048608 | tf_op jit(solution)/shard_map/ppermute | solution.py:33
  254.1 14.3 %all-to-all-done.3 = bf16[32,32,2048]{2,1,0:T(8,128)(2,1)} async-done(((bf16[32,32,2048]{2,1,0:T(8,128)(2,1)}), bf16[32,32,2048]{2,1,0:T(8,128)(2,1)}, u32[]{:S(2)}, u32[]{:S(2)}) %all-to-all-start.3) | async-done | bytes 4194336 | tf_op jit(solution)/shard_map/all_to_all | solution.py:163
  268.3 14.6 %multiply_reduce_fusion = (f32[1024]{0:T(1024)S(1)}, bf16[1024,2048]{1,0:T(8,128)(2,1)}) fusion(bf16[32,32,2048]{2,1,0:T(8,128)(2,1)} %all-to-all-done.3, bf16[256,2048]{1,0:T(8,128)(2,1)} %collective-permute-done.16, f32[1024,256]{1,0:T(8,128)} %fusion.104, f32[1024,256]{1,0:T(8,128)} %fusion.103, f32[1024,2048]{1,0:T(8,128)} %fusion.55, ...), kind=kOutput, calls=%fused_computation | convolution fusion | flops 1092090880 | bytes 36704256 | tf_op jit(solution)/shard_map/dot_general | solution.py:17
  283.7 7.0 all-to-all-start.5
  290.7 9.6 %all-to-all-done.5 = f32[32,1,32]{2,1,0:T(1,128)S(1)} async-done(((f32[32,1,32]{2,1,0:T(1,128)}), f32[32,1,32]{2,1,0:T(1,128)S(1)}, u32[]{:S(2)}, u32[]{:S(2)}) %all-to-all-start.5) | async-done | bytes 4128 | tf_op jit(solution)/shard_map/all_to_all | solution.py:245
  301.6 13.1 %all_to_all.43 = f32[32,1,32]{2,1,0:T(1,128)S(1)} all-to-all(f32[32,1,32]{2,1,0:T(1,128)S(1)} %bitcast.298), channel_id=1, replica_groups=mesh['dp'=32,'tensor'=4] {'dp'}, dimensions={0} | all-to-all | bytes 8192 | tf_op jit(solution)/shard_map/all_to_all | solution.py:208
  320.6 6.3 fusion.106
  374.5 19.5 %add_convert_fusion = bf16[1024,2048]{1,0:T(8,128)(2,1)S(1)} fusion(f32[1024,2048]{1,0:T(8,128)} %fusion.111, f32[1024,2048]{1,0:T(8,128)} %fusion.110, f32[1024,2048]{1,0:T(8,128)} %fusion.109, f32[1024,2048]{1,0:T(8,128)} %fusion.108, f32[1024,2048]{1,0:T(8,128)} %fusion.107, f32[1024,2048]{1,0:T(8,128)} %fusion.105, f32[1024,2048]{1,0:T(8,128)} %fusion.106, ...), kind=kOutput, calls=%fused_computation.1 | convolution fusion | flops 1090519040 | bytes 64487424 | tf_op jit(solution)/shard_map/dot_general | solution.py:17
  394.0 52.1 %all_to_all.44 = bf16[32,32,2048]{2,1,0:T(8,128)(2,1)} all-to-all(bf16[32,32,2048]{2,1,0:T(8,128)(2,1)S(1)} %bitcast.276), channel_id=1, replica_groups=mesh['dp'=32,'tensor'=4] {'dp'}, dimensions={0} | all-to-all | bytes 8388608 | tf_op jit(solution)/shard_map/all_to_all | solution.py:241
  475.3 27.9 %collective-permute-done.25 = f32[384,64]{0,1:T(8,128)} collective-permute-done((f32[384,64]{0,1:T(8,128)S(1)}, f32[384,64]{0,1:T(8,128)}, u32[]{:S(2)}, u32[]{:S(2)}) %collective-permute-start.25) | collective-permute-done | bytes 98336 | tf_op jit(solution)/shard_map/ppermute | solution.py:33
  563.4 9.8 %collective-permute-done.30 = bf16[384,512]{1,0:T(8,128)(2,1)S(1)} collective-permute-done((bf16[384,512]{1,0:T(8,128)(2,1)S(1)}, bf16[384,512]{1,0:T(8,128)(2,1)S(1)}, u32[]{:S(2)}, u32[]{:S(2)}) %collective-permute-start.30) | collective-permute-done | bytes 393248 | tf_op jit(solution)/shard_map/ppermute | solution.py:33
  581.7 36.9 %concatenate.79 = bf16[8260,512]{1,0:T(8,128)(2,1)} concatenate(bf16[512,512]{1,0:T(8,128)(2,1)} %get-tuple-element.73, bf16[512,512]{1,0:T(8,128)(2,1)S(1)} %get-tuple-element.72, bf16[512,512]{1,0:T(8,128)(2,1)S(1)} %get-tuple-element.71, bf16[512,512]{1,0:T(8,128)(2,1)S(1)} %get-tuple-element.70, bf16[2048,512]{1,0:T(8,128)(2,1)} %convolution_convert_fusion.4, ...), dimensions={0} | concatenate | bytes 16916480 | tf_op jit(solution)/shard_map/concatenate | solution.py:320
  618.6 6.4 pad.4
  625.0 113.6 %all_to_all.45 = bf16[32,272,512]{2,1,0:T(8,128)(2,1)} all-to-all(bf16[32,272,512]{2,1,0:T(8,128)(2,1)S(1)} %bitcast.274), channel_id=1, replica_groups=mesh['dp'=32,'tensor'=4] {'dp'}, dimensions={0} | all-to-all | bytes 17825792 | tf_op jit(solution)/shard_map/all_to_all | solution.py:329
  792.7 12.6 %collective-permute-done.41 = bf16[256,2048]{1,0:T(8,128)(2,1)S(1)} collective-permute-done((bf16[256,2048]{1,0:T(8,128)(2,1)S(1)}, bf16[256,2048]{1,0:T(8,128)(2,1)S(1)}, u32[]{:S(2)}, u32[]{:S(2)}) %collective-permute-start.41) | collective-permute-done | bytes 1048608 | tf_op jit(solution)/shard_map/ppermute | solution.py:33
  808.3 40.9 %collective-permute-done.38 = bf16[2048,256]{1,0:T(8,128)(2,1)S(1)} collective-permute-done((bf16[2048,256]{1,0:T(8,128)(2,1)S(1)}, bf16[2048,256]{1,0:T(8,128)(2,1)S(1)}, u32[]{:S(2)}, u32[]{:S(2)}) %collective-permute-start.38) | collective-permute-done | bytes 1048608 | tf_op jit(solution)/shard_map/ppermute | solution.py:33
  851.9 30.1 %collective-permute-done.35 = bf16[2048,256]{1,0:T(8,128)(2,1)S(1)} collective-permute-done((bf16[2048,256]{1,0:T(8,128)(2,1)S(1)}, bf16[2048,256]{1,0:T(8,128)(2,1)S(1)}, u32[]{:S(2)}, u32[]{:S(2)}) %collective-permute-start.35) | collective-permute-done | bytes 1048608 | tf_op jit(solution)/shard_map/ppermute | solution.py:33
  (552 shorter events, 353.4 us)
Async XLA Ops:
  81.6 82.6 %all-to-all-start = ((bf16[32,32,2048]{2,1,0:T(8,128)(2,1)}), bf16[32,32,2048]{2,1,0:T(8,128)(2,1)}, u32[]{:S(2)}, u32[]{:S(2)}) async-start(bf16[32,32,2048]{2,1,0:T(8,128)(2,1)} %bitcast.277), calls=%async_computation | async-start | bytes 8388608 | tf_op jit(solution)/shard_map/all_to_all | solution.py:163
  94.7 58.5 %collective-permute-start.19 = (bf16[384,512]{1,0:T(8,128)(2,1)}, bf16[384,512]{1,0:T(8,128)(2,1)}, u32[]{:S(2)}, u32[]{:S(2)}) collective-permute-start(bf16[384,512]{1,0:T(8,128)(2,1)} %convert_element_type.335), channel_id=1, source_target_pairs={{0,2},{2,0},{1,3},{3,1},{4,6},{6,4},{5,7},{7,5},{8,10},{10,8},{9,1... | collective-permute-start | bytes 1179656 | tf_op jit(solution)/shard_map/ppermute | solution.py:33
  95.3 61.8 %collective-permute-start.20 = (bf16[384,512]{1,0:T(8,128)(2,1)}, bf16[384,512]{1,0:T(8,128)(2,1)}, u32[]{:S(2)}, u32[]{:S(2)}) collective-permute-start(bf16[384,512]{1,0:T(8,128)(2,1)} %convert_element_type.335), channel_id=1, source_target_pairs={{0,1},{1,0},{2,3},{3,2},{4,5},{5,4},{6,7},{7,6},{8,9},{9,8},{10,11... | collective-permute-start | bytes 1179656 | tf_op jit(solution)/shard_map/ppermute | solution.py:37
  98.5 103.5 %collective-permute-start.9 = (bf16[2048,256]{1,0:T(8,128)(2,1)}, bf16[2048,256]{1,0:T(8,128)(2,1)}, u32[]{:S(2)}, u32[]{:S(2)}) collective-permute-start(bf16[2048,256]{1,0:T(8,128)(2,1)} %get-tuple-element.84), channel_id=1, source_target_pairs={{0,2},{2,0},{1,3},{3,1},{4,6},{6,4},{5,7},{7,5},{8,10},{10,8},{9,1... | collective-permute-start | bytes 3145736 | tf_op jit(solution)/shard_map/ppermute | solution.py:33
  101.4 96.7 %collective-permute-start.8 = (bf16[2048,256]{1,0:T(8,128)(2,1)}, bf16[2048,256]{1,0:T(8,128)(2,1)}, u32[]{:S(2)}, u32[]{:S(2)}) collective-permute-start(bf16[2048,256]{1,0:T(8,128)(2,1)} %get-tuple-element.82), channel_id=1, source_target_pairs={{0,2},{2,0},{1,3},{3,1},{4,6},{6,4},{5,7},{7,5},{8,10},{10,8},{9,1... | collective-permute-start | bytes 3145736 | tf_op jit(solution)/shard_map/ppermute | solution.py:33
  154.7 66.0 %collective-permute-start.10 = (bf16[256,2048]{1,0:T(8,128)(2,1)}, bf16[256,2048]{1,0:T(8,128)(2,1)}, u32[]{:S(2)}, u32[]{:S(2)}) collective-permute-start(bf16[256,2048]{1,0:T(8,128)(2,1)} %get-tuple-element.86), channel_id=1, source_target_pairs={{0,2},{2,0},{1,3},{3,1},{4,6},{6,4},{5,7},{7,5},{8,10},{10,8},{9,1... | collective-permute-start | bytes 3145736 | tf_op jit(solution)/shard_map/ppermute | solution.py:33
  157.2 63.5 %collective-permute-start.11 = (bf16[2048,256]{1,0:T(8,128)(2,1)}, bf16[2048,256]{1,0:T(8,128)(2,1)}, u32[]{:S(2)}, u32[]{:S(2)}) collective-permute-start(bf16[2048,256]{1,0:T(8,128)(2,1)} %get-tuple-element.83), channel_id=1, source_target_pairs={{0,1},{1,0},{2,3},{3,2},{4,5},{5,4},{6,7},{7,6},{8,9},{9,8},{10,11... | collective-permute-start | bytes 3145736 | tf_op jit(solution)/shard_map/ppermute | solution.py:37
  157.4 67.7 %collective-permute-start.12 = (bf16[2048,256]{1,0:T(8,128)(2,1)}, bf16[2048,256]{1,0:T(8,128)(2,1)}, u32[]{:S(2)}, u32[]{:S(2)}) collective-permute-start(bf16[2048,256]{1,0:T(8,128)(2,1)} %get-tuple-element.85), channel_id=1, source_target_pairs={{0,1},{1,0},{2,3},{3,2},{4,5},{5,4},{6,7},{7,6},{8,9},{9,8},{10,11... | collective-permute-start | bytes 3145736 | tf_op jit(solution)/shard_map/ppermute | solution.py:37
  164.2 104.1 %all-to-all-start.3 = ((bf16[32,32,2048]{2,1,0:T(8,128)(2,1)}), bf16[32,32,2048]{2,1,0:T(8,128)(2,1)}, u32[]{:S(2)}, u32[]{:S(2)}) async-start(bf16[32,32,2048]{2,1,0:T(8,128)(2,1)} %bitcast.278), calls=%async_computation.3 | async-start | bytes 8388608 | tf_op jit(solution)/shard_map/all_to_all | solution.py:163
  198.2 51.3 %collective-permute-start.13 = (bf16[256,2048]{1,0:T(8,128)(2,1)S(1)}, bf16[256,2048]{1,0:T(8,128)(2,1)S(1)}, u32[]{:S(2)}, u32[]{:S(2)}) collective-permute-start(bf16[256,2048]{1,0:T(8,128)(2,1)S(1)} %copy-done.22), channel_id=1, source_target_pairs={{0,1},{1,0},{2,3},{3,2},{4,5},{5,4},{6,7},{7,6},{8,9},{9,8},{10,11... | collective-permute-start | bytes 3145736 | tf_op jit(solution)/shard_map/ppermute | solution.py:37
  201.9 32.0 %collective-permute-start.14 = (bf16[2048,256]{1,0:T(8,128)(2,1)}, bf16[2048,256]{1,0:T(8,128)(2,1)S(1)}, u32[]{:S(2)}, u32[]{:S(2)}) collective-permute-start(bf16[2048,256]{1,0:T(8,128)(2,1)} %collective-permute-done.8), channel_id=1, source_target_pairs={{0,1},{1,0},{2,3},{3,2},{4,5},{5,4},{6,7},{7,6},{8,9},{9,8},{10,11... | collective-permute-start | bytes 3145736 | tf_op jit(solution)/shard_map/ppermute | solution.py:37
  220.6 33.4 %collective-permute-start.16 = (bf16[256,2048]{1,0:T(8,128)(2,1)}, bf16[256,2048]{1,0:T(8,128)(2,1)}, u32[]{:S(2)}, u32[]{:S(2)}) collective-permute-start(bf16[256,2048]{1,0:T(8,128)(2,1)} %collective-permute-done.10), channel_id=1, source_target_pairs={{0,1},{1,0},{2,3},{3,2},{4,5},{5,4},{6,7},{7,6},{8,9},{9,8},{10,11... | collective-permute-start | bytes 3145736 | tf_op jit(solution)/shard_map/ppermute | solution.py:37
  446.1 66.7 %all-to-all-start.1 = ((bf16[32,32,2048]{2,1,0:T(8,128)(2,1)}), bf16[32,32,2048]{2,1,0:T(8,128)(2,1)}, u32[]{:S(2)}, u32[]{:S(2)}) async-start(bf16[32,32,2048]{2,1,0:T(8,128)(2,1)} %bitcast.275), calls=%async_computation.1 | async-start | bytes 8388608 | tf_op jit(solution)/shard_map/all_to_all | solution.py:241
  452.1 434.2 %all-gather.2.cloned.1.call-start = ((), (), s32[]{:S(2)}) async-start(), calls=%async_computation.7 | async-start | bytes 9191424 | tf_op jit(solution)/shard_map/all_gather | solution.py:333
  463.7 39.5 %collective-permute-start.25 = (f32[384,64]{0,1:T(8,128)S(1)}, f32[384,64]{0,1:T(8,128)}, u32[]{:S(2)}, u32[]{:S(2)}) collective-permute-start(f32[384,64]{0,1:T(8,128)S(1)} %add.274), channel_id=1, source_target_pairs={{0,2},{2,0},{1,3},{3,1},{4,6},{6,4},{5,7},{7,5},{8,10},{10,8},{9,1... | collective-permute-start | bytes 294920 | tf_op jit(solution)/shard_map/ppermute | solution.py:33
  469.6 37.9 %collective-permute-start.23 = (bf16[384,512]{1,0:T(8,128)(2,1)}, bf16[384,512]{1,0:T(8,128)(2,1)}, u32[]{:S(2)}, u32[]{:S(2)}) collective-permute-start(bf16[384,512]{1,0:T(8,128)(2,1)} %get-tuple-element.24), channel_id=1, source_target_pairs={{0,2},{2,0},{1,3},{3,1},{4,6},{6,4},{5,7},{7,5},{8,10},{10,8},{9,1... | collective-permute-start | bytes 1179656 | tf_op jit(solution)/shard_map/ppermute | solution.py:33
  520.3 30.9 %collective-permute-start.17 = (bf16[384,1024]{1,0:T(8,128)(2,1)}, bf16[384,1024]{1,0:T(8,128)(2,1)}, u32[]{:S(2)}, u32[]{:S(2)}) collective-permute-start(bf16[384,1024]{1,0:T(8,128)(2,1)} %fusion.22), channel_id=1, source_target_pairs={{0,1},{1,0},{2,3},{3,2},{4,5},{5,4},{6,7},{7,6},{8,9},{9,8},{10,11... | collective-permute-start | bytes 2359304 | tf_op jit(solution)/shard_map/ppermute | solution.py:37
  553.2 26.9 %collective-permute-start.18 = (bf16[384,512]{1,0:T(8,128)(2,1)S(1)}, bf16[384,512]{1,0:T(8,128)(2,1)S(1)}, u32[]{:S(2)}, u32[]{:S(2)}) collective-permute-start(bf16[384,512]{1,0:T(8,128)(2,1)S(1)} %get-tuple-element.27), channel_id=1, source_target_pairs={{0,2},{2,0},{1,3},{3,1},{4,6},{6,4},{5,7},{7,5},{8,10},{10,8},{9,1... | collective-permute-start | bytes 1179656 | tf_op jit(solution)/shard_map/ppermute | solution.py:33
  748.1 27.2 %collective-permute-start.40 = (bf16[256,2048]{1,0:T(8,128)(2,1)S(1)}, bf16[256,2048]{1,0:T(8,128)(2,1)S(1)}, u32[]{:S(2)}, u32[]{:S(2)}) collective-permute-start(bf16[256,2048]{1,0:T(8,128)(2,1)S(1)} %convolution_convert_fusion.6), channel_id=1, source_target_pairs={{0,1},{1,0},{2,3},{3,2},{4,5},{5,4},{6,7},{7,6},{8,9},{9,8},{10,11... | collective-permute-start | bytes 3145736 | tf_op jit(solution)/shard_map/ppermute | solution.py:37
  766.5 26.0 %collective-permute-start.39 = (bf16[256,2048]{1,0:T(8,128)(2,1)S(1)}, bf16[256,2048]{1,0:T(8,128)(2,1)S(1)}, u32[]{:S(2)}, u32[]{:S(2)}) collective-permute-start(bf16[256,2048]{1,0:T(8,128)(2,1)S(1)} %convolution_convert_fusion.7), channel_id=1, source_target_pairs={{0,1},{1,0},{2,3},{3,2},{4,5},{5,4},{6,7},{7,6},{8,9},{9,8},{10,11... | collective-permute-start | bytes 3145736 | tf_op jit(solution)/shard_map/ppermute | solution.py:37
  779.0 26.3 %collective-permute-start.41 = (bf16[256,2048]{1,0:T(8,128)(2,1)S(1)}, bf16[256,2048]{1,0:T(8,128)(2,1)S(1)}, u32[]{:S(2)}, u32[]{:S(2)}) collective-permute-start(bf16[256,2048]{1,0:T(8,128)(2,1)S(1)} %add_convert_fusion.2), channel_id=1, source_target_pairs={{0,2},{2,0},{1,3},{3,1},{4,6},{6,4},{5,7},{7,5},{8,10},{10,8},{9,1... | collective-permute-start | bytes 3145736 | tf_op jit(solution)/shard_map/ppermute | solution.py:33
  782.9 69.0 %collective-permute-start.33 = (bf16[2048,256]{1,0:T(8,128)(2,1)S(1)}, bf16[2048,256]{1,0:T(8,128)(2,1)S(1)}, u32[]{:S(2)}, u32[]{:S(2)}) collective-permute-start(bf16[2048,256]{1,0:T(8,128)(2,1)S(1)} %convolution_convert_fusion.11), channel_id=1, source_target_pairs={{0,1},{1,0},{2,3},{3,2},{4,5},{5,4},{6,7},{7,6},{8,9},{9,8},{10,11... | collective-permute-start | bytes 3145736 | tf_op jit(solution)/shard_map/ppermute | solution.py:37
  786.9 62.3 %collective-permute-start.38 = (bf16[2048,256]{1,0:T(8,128)(2,1)S(1)}, bf16[2048,256]{1,0:T(8,128)(2,1)S(1)}, u32[]{:S(2)}, u32[]{:S(2)}) collective-permute-start(bf16[2048,256]{1,0:T(8,128)(2,1)S(1)} %add_convert_fusion.3), channel_id=1, source_target_pairs={{0,2},{2,0},{1,3},{3,1},{4,6},{6,4},{5,7},{7,5},{8,10},{10,8},{9,1... | collective-permute-start | bytes 3145736 | tf_op jit(solution)/shard_map/ppermute | solution.py:33
  792.5 89.4 %collective-permute-start.35 = (bf16[2048,256]{1,0:T(8,128)(2,1)S(1)}, bf16[2048,256]{1,0:T(8,128)(2,1)S(1)}, u32[]{:S(2)}, u32[]{:S(2)}) collective-permute-start(bf16[2048,256]{1,0:T(8,128)(2,1)S(1)} %add_convert_fusion.4), channel_id=1, source_target_pairs={{0,2},{2,0},{1,3},{3,1},{4,6},{6,4},{5,7},{7,5},{8,10},{10,8},{9,1... | collective-permute-start | bytes 3145736 | tf_op jit(solution)/shard_map/ppermute | solution.py:33
  (167 other events, 1408.1 us)
Sparse Core Ops, SparseCore 0:
  744.6 141.6 all-gather.1

commit v2 on v1

v2 whole, which is shorter than its diff:
```python
import functools

import jax
import jax.numpy as jnp
from jax import lax
from jax.experimental import pallas as pl
from jax.experimental.pallas import tpu as pltpu
from jax.sharding import PartitionSpec as P

HDIM = 128
TOP = 8
SLOTS = 64
HALF = SLOTS // 2
EPS = 1e-06
HIGH = lax.Precision.HIGHEST
F32 = jnp.float32
BF16 = jnp.bfloat16
MESH = pl.DeviceIdType.MESH
SMALL = 80
LANES = 128


def dot(a, b, dims, **kw):
    return lax.dot_general(a, b, (dims, ((), ())), preferred_element_type=F32, **kw)


def nn(a, b):
    return dot(a, b, ((1,), (0,)))


def nt(a, b):
    return dot(a, b, ((1,), (1,)))


def tn(a, b):
    return dot(a, b, ((0,), (0,)))


def cross(value):
    return lax.ppermute(value, "tensor", [(0, 2), (2, 0), (1, 3), (3, 1)])


def swap(value):
    return lax.ppermute(value, "tensor", [(0, 1), (1, 0), (2, 3), (3, 2)])


def inv_rms(value):
    return lax.rsqrt(jnp.mean(value * value, axis=-1, keepdims=True) + EPS)


def rope_angles(places):
    half = HDIM // 2
    frequency = jnp.exp(jnp.arange(half, dtype=F32) * (-2.0 * jnp.log(10000.0) / HDIM))
    angle = places.astype(F32)[:, None] * frequency[None, :]
    cosine, sine = jnp.cos(angle), jnp.sin(angle)
    return (
        jnp.concatenate([cosine, cosine], axis=1),
        jnp.concatenate([-sine, sine], axis=1),
    )


def two_parts(column):
    high = column.astype(BF16)
    rest = (column - high.astype(F32)).astype(BF16)
    lane = lax.broadcasted_iota(jnp.int32, (column.shape[0], LANES), 1)
    return jnp.where(
        lane == 0, high.astype(F32), jnp.where(lane == 1, rest.astype(F32), 0.0)
    ).astype(BF16)


def one_column(pair):
    wide = pair.astype(F32)
    return wide[:, 0:1] + wide[:, 1:2]


def expert_body(
    rows_in, og_in, wg_all, wu_all, wd_all,
    out_ref, back_in, kept_g, kept_u, kept_d, got_g, got_u, got_d,
    rows_s, og_s, wgu_s, wd_s, back_s, gu_s, hid_s, keep_s, move_s, down_keep, down_move,
    rs_sem, og_sem, w_sem, bs, br, ls, ks, ms, mr,
):
    plane = Plane()
    swap = (plane.dp, lax.axis_index("tensor") + 1 - 2 * plane.core)
    groups, slots, more = rows_s.shape
    width = og_s.shape[2]
    hidden = hid_s.shape[1]
    span = hidden // 4
    per = groups // 4
    tile = per * slots

    def load(e, _):
        g = plane.entry(e)
        pltpu.make_async_copy(rows_in.at[g], rows_s.at[e], rs_sem.at[e // per]).start()
        pltpu.make_async_copy(og_in.at[g], og_s.at[e], og_sem.at[e // per]).start()
        return 0

    lax.fori_loop(0, per, load, 0)
    w_copies = []
    for i in range(4):
        at = slice(i * span, (i + 1) * span)
        high = slice(hidden + i * span, hidden + (i + 1) * span)
        w_copies.append(pltpu.make_async_copy(wg_all.at[i], wgu_s.at[:, at], w_sem.at[0, i]))
        w_copies.append(pltpu.make_async_copy(wu_all.at[i], wgu_s.at[:, high], w_sem.at[1, i]))
    for i in range(4):
        at = slice(i * span, (i + 1) * span)
        w_copies.append(pltpu.make_async_copy(wd_all.at[i], wd_s.at[at], w_sem.at[2, i]))
    for c in w_copies:
        c.start()
    lax.fori_loop(per, groups, load, 0)

    barrier = pltpu.get_barrier_semaphore()

    plane.greet(barrier)
    pl.semaphore_signal(barrier, inc=1, device_id=swap, device_id_type=MESH)
    pl.semaphore_wait(barrier, groups)

    def back_copy(e):
        g = plane.entry(e)
        return pltpu.make_async_remote_copy(
            src_ref=back_s.at[e],
            dst_ref=back_in.at[plane.dp],
            send_sem=bs.at[e],
            recv_sem=br.at[e],
            device_id=plane.device(g),
            device_id_type=MESH,
        )

    own_back = pltpu.make_async_copy(back_s.at[groups - 1], back_in.at[plane.dp], ls.at[0])

    def one_tile(k, _):
        first = pl.multiple_of(k * per, per)
        here = pl.ds(pl.multiple_of(k * tile, tile), tile)
        part = pl.ds(first, per)
        pltpu.make_async_copy(rows_in.at[pl.ds(0, per)], rows_s.at[part], rs_sem.at[k]).wait()

        @pl.when(k == 0)
        def _():
            for c in w_copies[:8]:
                c.wait()

        mine = rows_s[part].reshape(tile, more)
        rows = mine[:, :width]
        gate = one_column(mine[:, width:])
        both = nn(rows, wgu_s[...])
        gp = both[:, :hidden]
        up = both[:, hidden:]
        sig = jax.nn.sigmoid(gp)
        act = gp * sig
        hid = act * up
        hid_s[here, :] = (gate * hid).astype(BF16)

        @pl.when(k == 0)
        def _():
            for c in w_copies[8:]:
                c.wait()

        low = nn(hid.astype(BF16), wd_s[...]).astype(BF16)
        out_ref[part] = low.reshape(per, slots, width)
        pltpu.make_async_copy(og_in.at[pl.ds(0, per)], og_s.at[part], og_sem.at[k]).wait()
        grads = og_s[part].reshape(tile, width)
        slot = jnp.sum(grads.astype(F32) * low.astype(F32), axis=1, keepdims=True)
        back_s[part, :, width:] = two_parts(slot).reshape(per, slots, more - width)
        hidden_grad = gate * nt(grads, wd_s[...])
        gu_s[here, :hidden] = (hidden_grad * up * sig * (1.0 + gp * (1.0 - sig))).astype(BF16)
        gu_s[here, hidden:] = (hidden_grad * act).astype(BF16)
        back = nt(gu_s[here, :], wgu_s[...]).astype(BF16)
        back_s[part, :, :width] = back.reshape(per, slots, width)

        def send(j, _):
            e = first + j

            @pl.when(e < groups - 1)
            def _():
                back_copy(e).start()

            @pl.when(e == groups - 1)
            def _():
                own_back.start()

            return 0

        lax.fori_loop(0, per, send, 0)
        return 0

    lax.fori_loop(0, 4, one_tile, 0)

    half = hidden // 2
    wide_block = keep_s.shape[1]

    def column_copies(i, slot):
        at = pl.ds(pl.multiple_of(i * wide_block, wide_block), wide_block)
        local = [
            pltpu.make_async_copy(keep_s.at[slot, :, :half], kept_g.at[at], ks.at[slot, 0]),
            pltpu.make_async_copy(keep_s.at[slot, :, half:], kept_u.at[at], ks.at[slot, 1]),
        ]
        far = [
            pltpu.make_async_remote_copy(
                src_ref=move_s.at[slot, :, side],
                dst_ref=target.at[at],
                send_sem=ms.at[slot, n],
                recv_sem=mr.at[i, n],
                device_id=swap,
                device_id_type=MESH,
            )
            for n, (side, target) in enumerate(
                ((slice(0, half), got_g), (slice(half, hidden), got_u))
            )
        ]
        return local + far

    def columns(i, _):
        slot = lax.rem(i, 2)

        @pl.when(i >= 2)
        def _():
            for c in column_copies(i - 2, slot):
                c.wait()

        at = pl.ds(pl.multiple_of(i * wide_block, wide_block), wide_block)
        rows = rows_s[:, :, at].reshape(groups * slots, wide_block)
        grad = tn(rows, gu_s[...])
        keep_s[slot, :, :half] = grad[:, :half]
        keep_s[slot, :, half:] = grad[:, hidden : hidden + half]
        move_s[slot, :, :half] = grad[:, half:hidden].astype(BF16)
        move_s[slot, :, half:] = grad[:, hidden + half :].astype(BF16)
        for c in column_copies(i, slot):
            c.start()
        return 0

    steps = width // wide_block
    lax.fori_loop(0, steps, columns, 0)
    downs = []
    for i in range(4):
        at = slice(i * span, (i + 1) * span)
        grad = tn(hid_s[:, at], og_s[...].reshape(groups * slots, width))
        if i < 2:
            down_keep[at] = grad
            downs.append(pltpu.make_async_copy(down_keep.at[at], kept_d.at[at], ls.at[1 + i]))
        else:
            at = slice((i - 2) * span, (i - 1) * span)
            down_move[at] = grad.astype(BF16)
            downs.append(
                pltpu.make_async_remote_copy(
                    src_ref=down_move.at[at],
                    dst_ref=got_d.at[at],
                    send_sem=ms.at[2, i - 2],
                    recv_sem=mr.at[steps, i - 2],
                    device_id=swap,
                    device_id_type=MESH,
                )
            )
        downs[-1].start()
    for i in (steps - 2, steps - 1):
        for c in column_copies(i, i % 2):
            c.wait()
    for c in downs:
        c.wait()

    def finish(e, _):
        back_copy(e).wait()
        return 0

    lax.fori_loop(0, groups - 1, finish, 0)
    own_back.wait()


def run_experts(rows, grads, weights):
    groups, slots, more = rows.shape
    width = grads.shape[2]
    hidden = 4 * weights[0].shape[2]
    half = hidden // 2
    count = groups * slots
    block = 256
    whole = pl.BlockSpec(memory_space=pltpu.VMEM)
    free = pl.BlockSpec(memory_space=pl.ANY)
    f = jax.ShapeDtypeStruct
    vm = pltpu.VMEM
    dma = pltpu.SemaphoreType.DMA
    return pl.pallas_call(
        expert_body,
        in_specs=[free] * 5,
        out_specs=[whole] + [free] * 7,
        out_shape=[
            f((groups, slots, width), BF16),
            f((groups, slots, more), BF16),
            f((width, half), F32),
            f((width, half), F32),
            f((half, width), F32),
            f((width, half), BF16),
            f((width, half), BF16),
            f((half, width), BF16),
        ],
        scratch_shapes=[
            vm((groups, slots, more), BF16),
            vm((groups, slots, width), BF16),
            vm((width, 2 * hidden), BF16),
            vm((hidden, width), BF16),
            vm((groups, slots, more), BF16),
            vm((count, 2 * hidden), BF16),
            vm((count, hidden), BF16),
            vm((2, block, hidden), F32),
            vm((2, block, hidden), BF16),
            vm((half, width), F32),
            vm((half, width), BF16),
            dma((4,)),
            dma((4,)),
            dma((3, 4)),
            dma((31,)),
            dma((31,)),
            dma((3,)),
            dma((2, 2)),
            dma((3, 2)),
            dma((width // block + 1, 2)),
        ],
        compiler_params=pltpu.CompilerParams(
            collective_id=2, has_side_effects=True, vmem_limit_bytes=61 << 20
        ),
        name="experts",
    )(rows, grads, *weights)


def head_scale(pre):
    return lax.rsqrt(jnp.mean(pre * pre, axis=1, keepdims=True) + EPS)


def turn(value, cosine, sine):
    return value * cosine + pltpu.roll(value, HDIM // 2, 1) * sine


def softmax_rows(query, key, same):
    raw = nt(query, key) * HDIM ** (-0.5)
    raw = jnp.where(same, raw, -1e30)
    powered = jnp.exp(raw - jnp.max(raw, axis=1, keepdims=True))
    return powered / jnp.sum(powered, axis=1, keepdims=True)


class Near:
    def __init__(self, send_sems, recv_sems):
        self.dp = lax.axis_index("dp")
        self.t = lax.axis_index("tensor")
        self.core = lax.rem(self.t, 2)
        self.first_core = self.core == 0
        self.low_x = self.t < 2
        self.far = lax.rem(self.t + 2, 4)
        self.swap = (self.dp, self.t + 1 - 2 * self.core)
        self.cross = (self.dp, self.far)
        self.diag = (self.dp, self.far + 1 - 2 * self.core)
        self.sems = (send_sems, recv_sems)
        self.used = 0

    def send(self, source, target, device):
        k = self.used
        self.used = k + 1
        c = pltpu.make_async_remote_copy(
            src_ref=source,
            dst_ref=target,
            send_sem=self.sems[0].at[k],
            recv_sem=self.sems[1].at[k],
            device_id=device,
            device_id_type=MESH,
        )
        c.start()
        return c

    def gather_start(self, buf):
        here = buf.at[self.t]
        return [self.send(here, here, self.cross), self.send(here, here, self.swap)]

    def gather_relay(self, buf, copies):
        copies[0].wait()
        there = buf.at[self.far]
        copies.append(self.send(there, there, self.swap))

    def split(self, part, low_s, high_s, sent):
        quarter = part.shape[1] // 4
        p = [part[:, i * quarter : (i + 1) * quarter] for i in range(4)]
        low_s[...] = jnp.where(self.first_core, p[0], p[1])
        high_s[...] = jnp.where(self.first_core, p[2], p[3])
        sent[:, :quarter] = jnp.where(self.first_core, p[1], p[0]).astype(BF16)
        sent[:, quarter:] = jnp.where(self.first_core, p[3], p[2]).astype(BF16)

    def sum_parts(self, low_s, high_s, sent, got, go, back):
        quarter = go.shape[1]
        self.send(sent, got, self.swap).wait()
        low = low_s[...] + got[:, :quarter].astype(F32)
        high = high_s[...] + got[:, quarter:].astype(F32)
        go[...] = jnp.where(self.low_x, high, low).astype(BF16)
        self.send(go, back, self.cross).wait()
        return jnp.where(self.low_x, low, high) + back[...].astype(F32)


class Plane:
    def __init__(self):
        self.dp = lax.axis_index("dp")
        t = lax.axis_index("tensor")
        self.y = lax.rem(self.dp, 4)
        self.xh = lax.rem(self.dp // 4, 2)
        self.z = self.dp // 8
        self.core = lax.rem(t, 2)
        self.side = lax.rem(t // 2 + self.xh, 2)

    def at(self, dz, dx, dy):
        return (lax.rem(self.z + dz, 4) * 2 + lax.rem(self.xh + dx, 2)) * 4 + lax.rem(
            self.y + dy, 4
        )

    def device(self, group):
        return (group, lax.rem(self.side + lax.rem(group // 4, 2), 2) * 2 + self.core)

    def entry(self, e):
        o = jnp.where(e == 31, 0, lax.rem(11 * e + 5, 31) + 1)
        return self.at(o // 8, lax.rem(o // 4, 2), lax.rem(o, 4))

    def greet(self, barrier):
        def one(e, _):
            pl.semaphore_signal(
                barrier, inc=1, device_id=self.device(self.entry(e)), device_id_type=MESH
            )
            return 0

        lax.fori_loop(0, 31, one, 0)

    def exchange(self, source, target, send_sems, recv_sems, local_sem, ordered):
        def copy(e):
            group = self.entry(e)
            return pltpu.make_async_remote_copy(
                src_ref=source.at[e if ordered else group],
                dst_ref=target.at[self.dp],
                send_sem=send_sems.at[e],
                recv_sem=recv_sems.at[e],
                device_id=self.device(group),
                device_id_type=MESH,
            )

        def start(e, _):
            copy(e).start()
            return 0

        def finish(e, _):
            copy(e).wait()
            return 0

        own = pltpu.make_async_copy(source.at[31 if ordered else self.dp], target.at[self.dp], local_sem)
        lax.fori_loop(0, 31, start, 0)
        own.start()

        def wait():
            lax.fori_loop(0, 31, finish, 0)
            own.wait()

        return wait


def wide(buf):
    return jnp.concatenate([buf[i] for i in range(4)], axis=1)


def front_body(
    x_ref, og_ref, gain1_ref, gain2_ref, wq_ref, wk_ref, wv_ref, wo_ref, qn_ref, kn_ref, cos_ref,
    sin_ref, col_ref, row_ref, routes_ref, ids_ref, router_ref, wg_ref, wu_ref, wd_ref,
    normed_ref, fs_ref, qpre_ref, kpre_ref, q_ref, k_ref, v_ref, mixed_ref, mid_ref, mids_ref, ogs_ref,
    nm_ref, gates_ref, place_ref, rows_in, og_in, wg_all, wu_all, wd_all,
    xs, low_s, high_s, sent, got, go, back, og_out, rows_out,
    ts, tr, as_, ar, bs, br, ls,
):
    near = Near(ts, tr)
    plane = Plane()
    side = plane.side
    barrier = pltpu.get_barrier_semaphore()
    plane.greet(barrier)
    pl.semaphore_signal(barrier, inc=1, device_id=near.swap, device_id_type=MESH)
    pl.semaphore_signal(barrier, inc=1, device_id=near.cross, device_id_type=MESH)
    pl.semaphore_wait(barrier, 33)
    t = near.t
    length = x_ref.shape[0]
    quarter = x_ref.shape[1]
    width = 4 * quarter

    ogs_ref[t] = og_ref[...].astype(BF16)
    og_copies = near.gather_start(ogs_ref)
    xs[t] = x_ref[...].astype(BF16)
    x_copies = near.gather_start(xs)
    weights = ((wg_ref, wg_all), (wu_ref, wu_all), (wd_ref, wd_all))
    kept = [
        pltpu.make_async_copy(w.at[side], w_all.at[0], ls.at[2 + i])
        for i, (w, w_all) in enumerate(weights)
    ]
    w_cross = [near.send(wg_ref.at[1 - side], wg_all.at[1], near.cross)]

    chosen = routes_ref[0:1, :] == ids_ref[...]
    for k in range(1, TOP):
        chosen = jnp.logical_or(chosen, routes_ref[k : k + 1, :] == ids_ref[...])
    mask = jnp.where(chosen, 1.0, 0.0)
    earlier = lax.broadcasted_iota(jnp.int32, (length, length), 0) < lax.broadcasted_iota(
        jnp.int32, (length, length), 1
    )
    rank = nn(mask.astype(BF16), jnp.where(earlier, 1.0, 0.0).astype(BF16))
    rank = jnp.where(chosen, rank, -1.0).astype(jnp.int32)
    experts = rank.shape[0] // 2
    place_ref[...] = jnp.where(side == 0, rank[:experts], rank[experts:])
    base = near.core * HALF

    def hits(i):
        place = place_ref[i * 8 : (i + 1) * 8, :]
        spots = lax.broadcasted_iota(jnp.int32, (8, HALF, length), 1) + base
        return jnp.broadcast_to(place[:, None, :], (8, HALF, length)) == spots

    near.gather_relay(ogs_ref, og_copies)
    near.gather_relay(xs, x_copies)
    for c in og_copies[1:]:
        c.wait()
    og = wide(ogs_ref)
    for i in range(experts // 8):
        select = jnp.where(hits(i), 1.0, 0.0).reshape(8 * HALF, length).astype(BF16)
        og_out[i * 8 : (i + 1) * 8] = nn(select, og).astype(BF16).reshape(8, HALF, width)
    og_wait = plane.exchange(og_out, og_in, as_, ar, ls.at[0], False)
    for c in kept:
        c.start()
    w_swap = [near.send(w.at[side], w_all.at[2], near.swap) for w, w_all in weights]

    for c in x_copies[1:]:
        c.wait()
    x = wide(xs).astype(F32)
    scale = lax.rsqrt(jnp.mean(x * x, axis=1, keepdims=True) + EPS)
    fs_ref[...] = scale
    normed = (x * scale * gain1_ref[...]).astype(BF16)
    normed_ref[...] = normed
    qpre = nn(normed, wq_ref[...])
    kpre = nn(normed, wk_ref[...])
    qpre_ref[...] = qpre
    kpre_ref[...] = kpre
    v_ref[...] = nn(normed, wv_ref[...]).astype(BF16)
    cosine = cos_ref[...]
    sine = sin_ref[...]
    same = col_ref[...] == row_ref[...]
    for h in range(q_ref.shape[1] // HDIM):
        at = slice(h * HDIM, (h + 1) * HDIM)
        qh = qpre[:, at]
        kh = kpre[:, at]
        query = turn(qh * head_scale(qh) * qn_ref[:, at], cosine, sine).astype(BF16)
        key = turn(kh * head_scale(kh) * kn_ref[:, at], cosine, sine).astype(BF16)
        q_ref[:, at] = query
        k_ref[:, at] = key
        probs = softmax_rows(query, key, same).astype(BF16)
        mixed_ref[:, at] = nn(probs, v_ref[:, at]).astype(BF16)
    near.split(nn(mixed_ref[...], wo_ref[...]), low_s, high_s, sent)
    mid = x_ref[...] + near.sum_parts(low_s, high_s, sent, got, go, back)
    mid_ref[...] = mid
    mids_ref[t] = mid.astype(BF16)
    mid_copies = near.gather_start(mids_ref)
    w_cross.append(near.send(wu_ref.at[1 - side], wu_all.at[1], near.cross))
    w_cross.append(near.send(wd_ref.at[1 - side], wd_all.at[1], near.cross))
    near.gather_relay(mids_ref, mid_copies)
    for c in mid_copies[1:]:
        c.wait()
    mid = wide(mids_ref).astype(F32)
    scale = lax.rsqrt(jnp.mean(mid * mid, axis=1, keepdims=True) + EPS)
    normed = (mid * scale * gain2_ref[...]).astype(BF16)
    nm_ref[...] = normed

    logits = nt(router_ref[...], normed)
    masked = jnp.where(chosen, logits, -1e30)
    raised = jnp.where(chosen, jnp.exp(masked - jnp.max(masked, axis=0, keepdims=True)), 0.0)
    gates = raised / jnp.sum(raised, axis=0, keepdims=True)
    gates_ref[...] = gates
    gates_side = jnp.where(side == 0, gates[:experts], gates[experts:])
    for i in range(experts // 8):
        hit = hits(i)
        select = jnp.where(hit, 1.0, 0.0).reshape(8 * HALF, length).astype(BF16)
        rows_out[i * 8 : (i + 1) * 8, :, :width] = (
            nn(select, normed).astype(BF16).reshape(8, HALF, width)
        )
        gate = jnp.broadcast_to(gates_side[i * 8 : (i + 1) * 8][:, None, :], (8, HALF, length))
        column = jnp.sum(
            jnp.where(hit, gate, 0.0).reshape(8 * HALF, length), axis=1, keepdims=True
        )
        rows_out[i * 8 : (i + 1) * 8, :, width:] = two_parts(column).reshape(8, HALF, LANES)
    rows_wait = plane.exchange(rows_out, rows_in, bs, br, ls.at[1], False)
    for c, (w, w_all) in zip(w_cross, weights):
        c.wait()
        w_swap.append(near.send(w_all.at[1], w_all.at[3], near.swap))
    og_wait()
    rows_wait()
    for c in w_swap + kept:
        c.wait()


def run_front(
    x, og, gain1, gain2, wq, wk, wv, wo, qn, kn, cosine, sine, labels, routes, ids, router, wg, wu,
    wd, groups,
):
    length, quarter = x.shape
    width = 4 * quarter
    inner = wq.shape[1]
    whole = pl.BlockSpec(memory_space=pltpu.VMEM)
    free = pl.BlockSpec(memory_space=pl.ANY)
    f = jax.ShapeDtypeStruct
    vm = pltpu.VMEM
    dma = pltpu.SemaphoreType.DMA
    return pl.pallas_call(
        front_body,
        in_specs=[whole] * 17 + [free] * 3,
        out_specs=[whole] * 14 + [free] * 5,
        out_shape=[
            f((length, width), BF16),
            f((length, 1), F32),
            f((length, inner), F32),
            f((length, inner), F32),
            f((length, inner), BF16),
            f((length, inner), BF16),
            f((length, inner), BF16),
            f((length, inner), BF16),
            f((length, quarter), F32),
            f((4, length, quarter), BF16),
            f((4, length, quarter), BF16),
            f((length, width), BF16),
            f((2 * groups, length), F32),
            f((groups, length), jnp.int32),
            f((groups, HALF, width + LANES), BF16),
            f((groups, HALF, width), BF16),
            f((4,) + wg.shape[1:], BF16),
            f((4,) + wu.shape[1:], BF16),
            f((4,) + wd.shape[1:], BF16),
        ],
        scratch_shapes=[
            vm((4, length, quarter), BF16),
            vm((length, quarter), F32),
            vm((length, quarter), F32),
            vm((length, 2 * quarter), BF16),
            vm((length, 2 * quarter), BF16),
            vm((length, quarter), BF16),
            vm((length, quarter), BF16),
            vm((groups, HALF, width), BF16),
            vm((groups, HALF, width + LANES), BF16),
            dma((20,)),
            dma((20,)),
            dma((31,)),
            dma((31,)),
            dma((31,)),
            dma((31,)),
            dma((5,)),
        ],
        compiler_params=pltpu.CompilerParams(
            collective_id=1, has_side_effects=True, vmem_limit_bytes=60 << 20
        ),
        name="front",
    )(
        x, og, gain1, gain2, wq, wk, wv, wo, qn, kn, cosine, sine, labels[:, None], labels[None, :],
        routes, ids, router, wg, wu, wd,
    )


def middle_body(
    rows_ref, out_rows, place_ref, gates_ref, nm_ref, router_ref, mid_ref, og_ref, mids_ref, ogs_ref,
    gain_ref, normed_ref, wq_ref, wk_ref, wv_ref, wo_ref, qn_ref, kn_ref, cos_ref, sin_ref, col_ref,
    row_ref, qpre_ref, kpre_ref, q_ref, k_ref, v_ref, mixed_ref,
    stack_ref, small_ref, mid_grad_ref, keep_ref, sent_ref, returned,
    low_s, low_f, high_f, sent, got, go, back, ngs, gg_s, ts, tr, os, orr, ls,
):
    near = Near(ts, tr)
    plane = Plane()
    side = plane.side
    t = near.t
    groups, slots, more = rows_ref.shape
    length, width = normed_ref.shape
    quarter = width // 4
    inner = q_ref.shape[1]

    barrier = pltpu.get_barrier_semaphore()

    plane.greet(barrier)
    pl.semaphore_signal(barrier, inc=1, device_id=near.swap, device_id_type=MESH)
    pl.semaphore_signal(barrier, inc=1, device_id=near.cross, device_id_type=MESH)
    pl.semaphore_wait(barrier, groups + 1)

    out_wait = plane.exchange(out_rows, returned, os, orr, ls.at[0], True)

    base = near.core * slots
    part = None
    for i in range(groups // 8):
        at = slice(i * 8, (i + 1) * 8)
        spots = lax.broadcasted_iota(jnp.int32, (8, slots, length), 1) + base
        hit = jnp.broadcast_to(place_ref[at, :][:, None, :], (8, slots, length)) == spots
        select = jnp.where(hit, 1.0, 0.0).reshape(8 * slots, length)
        tile = rows_ref[at].reshape(8 * slots, more)
        column = one_column(tile[:, width:])
        gg_s[0, at] = jnp.sum((select * column).reshape(8, slots, length), axis=1)
        term = tn(select.astype(BF16), tile[:, :width])
        part = term if part is None else part + term
    gate_swap = near.send(gg_s.at[0], gg_s.at[1], near.swap)
    near.split(part, low_f, high_f, sent)
    swapped = near.send(sent, got, near.swap)
    gate_swap.wait()
    gg_s[2] = gg_s[0] + gg_s[1]
    gate_cross = near.send(gg_s.at[2], gg_s.at[3], near.cross)
    swapped.wait()
    low = low_f[...] + got[:, :quarter].astype(F32)
    high = high_f[...] + got[:, quarter:].astype(F32)
    go[...] = jnp.where(near.low_x, high, low).astype(BF16)
    crossed = near.send(go, back, near.cross)
    gate_cross.wait()
    own, other = gg_s[2], gg_s[3]
    gate_grad = jnp.concatenate(
        [jnp.where(side == 0, own, other), jnp.where(side == 0, other, own)], axis=0
    )
    gates = gates_ref[...]
    logit_grad = gates * (gate_grad - jnp.sum(gates * gate_grad, axis=0, keepdims=True))
    mine = pl.ds(pl.multiple_of(t * quarter, quarter), quarter)
    router_back = dot(
        logit_grad, router_ref[:, mine].astype(F32), ((0,), (0,)), precision=HIGH
    )
    experts = gates.shape[0]
    small_ref[:experts, :] = dot(
        logit_grad, nm_ref[:, mine].astype(F32), ((1,), (0,)), precision=HIGH
    ).astype(BF16)
    mid = wide(mids_ref).astype(F32)
    scale = lax.rsqrt(jnp.mean(mid * mid, axis=1, keepdims=True) + EPS)
    mid_own = mid_ref[...]
    crossed.wait()
    ng = jnp.where(near.low_x, low, high) + back[...].astype(F32) + router_back
    ngs[t] = ng.astype(BF16)
    ng_copies = near.gather_start(ngs)
    moe = jnp.sum(ng * mid_own * scale, axis=0, keepdims=True)
    near.gather_relay(ngs, ng_copies)
    for c in ng_copies[1:]:
        c.wait()

    weighted = wide(ngs).astype(F32) * gain_ref[...]
    shrink = scale * scale * scale * jnp.mean(weighted * mid, axis=1, keepdims=True)
    mid_grad_ref[...] = og_ref[...] + scale * (ng * gain_ref[:, mine]) - mid_own * shrink
    attn_grad = (wide(ogs_ref).astype(F32) + scale * weighted - mid * shrink).astype(BF16)

    wo_grad = tn(mixed_ref[...], attn_grad).astype(BF16)
    for i in range(4):
        stack_ref[i * inner : (i + 1) * inner, :] = wo_grad[:, i * quarter : (i + 1) * quarter]
    mixed_grad = nt(attn_grad, wo_ref[...]).astype(BF16)
    cosine = cos_ref[...]
    sine = sin_ref[...]
    same = col_ref[...] == row_ref[...]
    factor = HDIM ** (-0.5)

    def norm_back(pre, gain, rotated):
        grad = rotated * cosine - pltpu.roll(rotated, HDIM // 2, 1) * sine
        head = head_scale(pre)
        weighted = grad * gain
        mean = jnp.mean(weighted * pre, axis=1, keepdims=True)
        low = (head * weighted - pre * (head * head * head * mean)).astype(BF16)
        return low, jnp.sum(grad * pre * head, axis=0, keepdims=True)

    q_sums, k_sums = [], []
    for h in range(inner // HDIM):
        at = slice(h * HDIM, (h + 1) * HDIM)
        query = q_ref[:, at]
        key = k_ref[:, at]
        mg = mixed_grad[:, at]
        probs = softmax_rows(query, key, same)
        low_s[:, 2 * inner + h * HDIM : 2 * inner + (h + 1) * HDIM] = tn(
            probs.astype(BF16), mg
        ).astype(BF16)
        prob_grad = nt(mg, v_ref[:, at])
        weighted_p = probs * prob_grad
        score = (weighted_p - probs * jnp.sum(weighted_p, axis=1, keepdims=True)).astype(BF16)
        low_q, total = norm_back(qpre_ref[:, at], qn_ref[:, at], nn(score, key) * factor)
        low_s[:, h * HDIM : (h + 1) * HDIM] = low_q
        q_sums.append(total)
        low_k, total = norm_back(kpre_ref[:, at], kn_ref[:, at], tn(score, query) * factor)
        low_s[:, inner + h * HDIM : inner + (h + 1) * HDIM] = low_k
        k_sums.append(total)
    row = lax.broadcasted_iota(jnp.int32, (small_ref.shape[0] - experts, quarter), 0)
    rest = jnp.zeros(row.shape, F32)
    for i, value in enumerate(
        (moe, jnp.concatenate(q_sums, axis=1), jnp.concatenate(k_sums, axis=1))
    ):
        rest = jnp.where(row == i + 1, jnp.broadcast_to(value, row.shape), rest)
    small_ref[experts:, :] = rest.astype(BF16)
    part = None
    for i, w in enumerate((wq_ref, wk_ref, wv_ref)):
        term = nt(low_s[:, i * inner : (i + 1) * inner], w[...])
        part = term if part is None else part + term
    near.split(part, low_f, high_f, sent_ref)
    keep_ref[:, :quarter] = low_f[...]
    keep_ref[:, quarter:] = high_f[...]
    normed = normed_ref[...]
    for i in range(3):
        stack_ref[(i + 1) * width : (i + 2) * width, :] = tn(
            normed, low_s[:, i * inner : (i + 1) * inner]
        ).astype(BF16)

    out_wait()


def run_middle(
    rows, out_rows, place, gates, nm, router, mid, og, mids, ogs, gain, normed, wq, wk, wv, wo, qn,
    kn, cosine, sine, labels, qpre, kpre, q, k, v, mixed,
):
    length, width = normed.shape
    quarter = width // 4
    groups = place.shape[0]
    inner = wq.shape[1]
    whole = pl.BlockSpec(memory_space=pltpu.VMEM)
    free = pl.BlockSpec(memory_space=pl.ANY)
    f = jax.ShapeDtypeStruct
    vm = pltpu.VMEM
    dma = pltpu.SemaphoreType.DMA
    return pl.pallas_call(
        middle_body,
        in_specs=[whole, free] + [whole] * 26,
        out_specs=[whole] * 5 + [free],
        out_shape=[
            f((4 * width, quarter), BF16),
            f((SMALL, quarter), BF16),
            f((length, quarter), F32),
            f((length, 2 * quarter), F32),
            f((length, 2 * quarter), BF16),
            f(out_rows.shape, BF16),
        ],
        scratch_shapes=[
            vm((length, 3 * inner), BF16),
            vm((length, quarter), F32),
            vm((length, quarter), F32),
            vm((length, 2 * quarter), BF16),
            vm((length, 2 * quarter), BF16),
            vm((length, quarter), BF16),
            vm((length, quarter), BF16),
            vm((4, length, quarter), BF16),
            vm((4, groups, length), F32),
            dma((8,)),
            dma((8,)),
            dma((31,)),
            dma((31,)),
            dma((1,)),
        ],
        compiler_params=pltpu.CompilerParams(
            collective_id=3, has_side_effects=True, vmem_limit_bytes=61 << 20
        ),
        name="middle",
    )(
        rows, out_rows, place, gates, nm, router, mid, og, mids, ogs, gain, normed, wq, wk, wv, wo,
        qn, kn, cosine, sine, labels[:, None], labels[None, :], qpre, kpre, q, k, v, mixed,
    )


def tail_body(
    stack_ref, small_ref, keep_ref, sent_ref, x_ref, mid_grad_ref, fs_ref, gain_ref, mid_ref,
    ret_ref, sel_ref, kept_g, kept_u, kept_d, got_g, got_u, got_d,
    out_ref, small_out_ref, input_ref, layer_ref, mine_g, mine_u, mine_d, other_g, other_u, other_d,
    recv1, buf1, recv2, buf2, recv3, small_in, got, out_sent, out_got, go, back, out_go, out_back,
    mean_in, kb, gb, nb, kd, gd, far_g, far_u, far_d, ss, rs, sss, srs, ts, tr, ws,
):
    dp = lax.axis_index("dp")
    t = lax.axis_index("tensor")
    y = lax.rem(dp, 4)
    xh = lax.rem(dp // 4, 2)
    z = dp // 8
    core = lax.rem(t, 2)
    first_core = core == 0
    low_x = t < 2
    half = stack_ref.shape[0] // 2
    n1, n2, n3 = half // 4, half // 16, half // 32
    quarter = x_ref.shape[1]

    def at_z(k):
        return ((lax.rem(z + k, 4) * 2 + xh) * 4 + y, t)

    def at_y(k):
        return ((z * 2 + xh) * 4 + lax.rem(y + k, 4), t)

    at_x = ((z * 2 + 1 - xh) * 4 + y, t)
    at_swap = (dp, t + 1 - 2 * core)
    at_cross = (dp, lax.rem(t + 2, 4))
    at_diag = (dp, lax.rem(t + 2, 4) + 1 - 2 * core)

    barrier = pltpu.get_barrier_semaphore()
    for k in range(1, 4):
        pl.semaphore_signal(barrier, inc=1, device_id=at_z(k), device_id_type=MESH)
        pl.semaphore_signal(barrier, inc=1, device_id=at_y(k), device_id_type=MESH)
    for there in (at_x, at_swap, at_cross, at_diag):
        pl.semaphore_signal(barrier, inc=1, device_id=there, device_id_type=MESH)
    pl.semaphore_wait(barrier, 10)

    def send(source, target, sems, device):
        c = pltpu.make_async_remote_copy(
            src_ref=source,
            dst_ref=target,
            send_sem=sems[0],
            recv_sem=sems[1],
            device_id=device,
            device_id_type=MESH,
        )
        c.start()
        return c

    def copy(source, target, phase, h, k, device):
        return send(source, target, (ss.at[phase, h, k], rs.at[phase, h, k]), device)

    def small_copy(slot, k, device):
        return send(small_in.at[slot], small_in.at[slot], (sss.at[k], srs.at[k]), device)

    def near(source, target, k, device):
        return send(source, target, (ts.at[k], tr.at[k]), device)

    def rows_at(start, size):
        return pl.ds(pl.multiple_of(start, 128), size)

    ways = (((z, at_z), (y, at_y)), ((y, at_y), (z, at_z)))
    first, second, third = [], [], []
    for h in range(2):
        pos, at = ways[h][0]
        for k in range(1, 4):
            there = rows_at(h * half + lax.rem(pos + k, 4) * n1, n1)
            first.append(copy(stack_ref.at[there], recv1.at[h, k - 1], 0, h, k - 1, at(k)))

    swapped = near(sent_ref, got, 0, at_swap)
    part = tn(sel_ref[...], ret_ref[...])
    p = [part[:, i * quarter : (i + 1) * quarter] for i in range(4)]
    out_sent[:, :quarter] = jnp.where(first_core, p[1], p[0]).astype(BF16)
    out_sent[:, quarter:] = jnp.where(first_core, p[3], p[2]).astype(BF16)
    out_low = jnp.where(first_core, p[0], p[1])
    out_high = jnp.where(first_core, p[2], p[3])
    out_swapped = near(out_sent, out_got, 1, at_swap)
    swapped.wait()
    low_half = keep_ref[:, :quarter] + got[:, :quarter].astype(F32)
    high_half = keep_ref[:, quarter:] + got[:, quarter:].astype(F32)
    go[...] = jnp.where(low_x, high_half, low_half).astype(BF16)
    crossed = near(go, back, 2, at_cross)
    in_mine = jnp.where(low_x, low_half, high_half)
    out_swapped.wait()
    out_low = out_low + out_got[:, :quarter].astype(F32)
    out_high = out_high + out_got[:, quarter:].astype(F32)
    out_go[...] = jnp.where(low_x, out_high, out_low).astype(BF16)
    crossed.wait()
    in_grad = in_mine + back[...].astype(F32)
    x = x_ref[...]
    fs = fs_ref[...]
    weighted = in_grad * gain_ref[...]
    mean = jnp.sum(weighted * x, axis=1, keepdims=True)
    mean_in[0] = jnp.broadcast_to(mean, mean_in.shape[1:])
    mean_swap = near(mean_in.at[0], mean_in.at[1], 3, at_swap)
    row = lax.broadcasted_iota(jnp.int32, (16, quarter), 0)
    norm_row = jnp.sum(in_grad * x * fs, axis=0, keepdims=True)
    small_in[z] = small_ref[...]
    last = small_ref.shape[0] - 16
    small_in[z, last:, :] = jnp.where(
        row == 0, jnp.broadcast_to(norm_row, (16, quarter)), small_ref[last:, :].astype(F32)
    ).astype(BF16)
    small = [small_copy(z, k - 1, at_z(k)) for k in range(1, 4)]
    mean_swap.wait()
    mean_in[2] = mean_in[0] + mean_in[1]
    mean_cross = near(mean_in.at[2], mean_in.at[3], 4, at_cross)
    out_crossed = near(out_go, out_back, 5, at_cross)
    mean_cross.wait()
    mean = (mean_in[2] + mean_in[3])[:, 0:1] / (4 * quarter)
    input_ref[...] = mid_grad_ref[...] + fs * weighted - x * (fs * fs * fs * mean)
    out_crossed.wait()
    layer_ref[...] = mid_ref[...] + (jnp.where(low_x, out_low, out_high) + out_back[...].astype(F32))

    block = kb.shape[1]
    loads = []
    for kept, gotten in ((kept_g, got_g), (kept_u, got_u)):
        for i in range(kept_g.shape[0] // block):
            slot = len(loads) % 2
            at = slice(i * block, (i + 1) * block)
            loads.append(
                (
                    pltpu.make_async_copy(kept.at[at], kb.at[slot], ws.at[slot, 0]),
                    pltpu.make_async_copy(gotten.at[at], gb.at[slot], ws.at[slot, 1]),
                )
            )
    span = far_d.shape[0]
    down_loads = [
        (
            pltpu.make_async_copy(kept_d.at[at], kd.at[i], ws.at[2 + i, 0]),
            pltpu.make_async_copy(got_d.at[at], gd.at[i], ws.at[2 + i, 1]),
        )
        for i, at in enumerate((slice(0, span), slice(span, 2 * span)))
    ]
    for c in loads[0] + down_loads[0] + down_loads[1]:
        c.start()
    stores = []
    for n, pair in enumerate(loads):
        if n + 1 < len(loads):
            for c in loads[n + 1]:
                c.start()
        for c in pair:
            c.wait()
        slot = n % 2
        per = len(loads) // 2
        far, mine = ((far_g, mine_g), (far_u, mine_u))[n // per]
        at = slice((n % per) * block, (n % per + 1) * block)
        total = kb[slot] + gb[slot].astype(F32)
        if n >= 2:
            stores[n - 2].wait()
        nb[slot] = total[:, :span]
        far[at, :] = total[:, span:].astype(BF16)
        stores.append(pltpu.make_async_copy(nb.at[slot], mine.at[at], ws.at[slot, 2]))
        stores[-1].start()
        if n == per - 1:
            others = [near(far_g, other_g, 6, at_cross)]
    for pair in down_loads:
        for c in pair:
            c.wait()
    kd[0] = kd[0] + gd[0].astype(F32)
    far_d[...] = (kd[1] + gd[1].astype(F32)).astype(BF16)
    stores.append(pltpu.make_async_copy(kd.at[0], mine_d, ws.at[2, 2]))
    stores[-1].start()
    for c in stores[-3:]:
        c.wait()

    def small_total(start, count):
        total = small_in[start].astype(F32)
        for i in range(start + 1, start + count):
            total = total + small_in[i].astype(F32)
        return total.astype(BF16)

    bases = []
    for h in range(2):
        pos, _ = ways[h][0]
        for c in first[3 * h : 3 * h + 3]:
            c.wait()
        base = h * half + pos * n1
        step = n1 // 4

        def add_first(i, _, h=h, base=base):
            here = rows_at(i * step, step)
            total = stack_ref[rows_at(base + i * step, step), :].astype(F32)
            for k in range(3):
                total = total + recv1[h, k, here, :].astype(F32)
            buf1[h, here, :] = total.astype(BF16)
            return 0

        lax.fori_loop(0, n1 // step, add_first, 0)
        pos2, at2 = ways[h][1]
        for k in range(1, 4):
            there = rows_at(lax.rem(pos2 + k, 4) * n2, n2)
            second.append(copy(buf1.at[h, there], recv2.at[h, k - 1], 1, h, k - 1, at2(k)))
        bases.append(base)
    for c in small:
        c.wait()
    small_in[4 + y] = small_total(0, 4)
    small = [small_copy(4 + y, 3 + k - 1, at_y(k)) for k in range(1, 4)]
    for h in range(2):
        pos2, _ = ways[h][1]
        for c in second[3 * h : 3 * h + 3]:
            c.wait()
        total = buf1[h, rows_at(pos2 * n2, n2), :].astype(F32)
        for k in range(3):
            total = total + recv2[h, k].astype(F32)
        buf2[h] = total.astype(BF16)
        third.append(
            copy(buf2.at[h, rows_at((1 - xh) * n3, n3)], recv3.at[h], 2, h, 0, at_x)
        )
        bases[h] = bases[h] + pos2 * n2
    for c in small:
        c.wait()
    small_in[8 + xh] = small_total(4, 4)
    small = small_copy(8 + xh, 6, at_x)
    ahead = []
    for h in range(2):
        third[h].wait()
        total = buf2[h, rows_at(xh * n3, n3), :].astype(F32) + recv3[h].astype(F32)
        here = rows_at(bases[h] + xh * n3, n3)
        out_ref[here, :] = total.astype(BF16)
        ahead.append(copy(out_ref.at[here], out_ref.at[here], 3, h, 0, at_x))
    later = []
    for c in ahead:
        c.wait()
    others.append(near(far_u, other_u, 7, at_cross))
    others.append(near(far_d, other_d, 8, at_cross))
    for h in range(2):
        _, at2 = ways[h][1]
        here = rows_at(bases[h], n2)
        for k in range(1, 4):
            later.append(copy(out_ref.at[here], out_ref.at[here], 4, h, k - 1, at2(k)))
    small.wait()
    small_out_ref[t] = small_total(8, 2)
    small = [
        near(small_out_ref.at[t], small_out_ref.at[t], 9 + i, there)
        for i, there in enumerate((at_swap, at_cross, at_diag))
    ]
    ended = []
    for h in range(2):
        for c in later[3 * h : 3 * h + 3]:
            c.wait()
        pos, at = ways[h][0]
        here = rows_at(h * half + pos * n1, n1)
        for k in range(1, 4):
            ended.append(copy(out_ref.at[here], out_ref.at[here], 5, h, k - 1, at(k)))
    for c in small + others + ended:
        c.wait()


def run_tail(
    stack, small, keep, sent, x, mid_grad, fs, gain, mid, returned, select, pieces
):
    rows, cols = stack.shape
    half = rows // 2
    length = x.shape[0]
    deep, wide_half = pieces[0].shape
    span = wide_half // 2
    shapes = [(deep, span), (deep, span), (span, deep)]
    whole = pl.BlockSpec(memory_space=pltpu.VMEM)
    free = pl.BlockSpec(memory_space=pl.ANY)
    f = jax.ShapeDtypeStruct
    vm = pltpu.VMEM
    return pl.pallas_call(
        tail_body,
        in_specs=[whole] * 11 + [free] * 6,
        out_specs=[whole] * 4 + [free] * 6,
        out_shape=[
            f(stack.shape, BF16),
            f((4,) + small.shape, BF16),
            f(x.shape, F32),
            f(x.shape, F32),
        ]
        + [f(shape, F32) for shape in shapes]
        + [f(shape, BF16) for shape in shapes],
        scratch_shapes=[
            vm((2, 3, half // 4, cols), BF16),
            vm((2, half // 4, cols), BF16),
            vm((2, 3, half // 16, cols), BF16),
            vm((2, half // 16, cols), BF16),
            vm((2, half // 32, cols), BF16),
            vm((10,) + small.shape, BF16),
            vm((length, 2 * cols), BF16),
            vm((length, 2 * cols), BF16),
            vm((length, 2 * cols), BF16),
            vm((length, cols), BF16),
            vm((length, cols), BF16),
            vm((length, cols), BF16),
            vm((length, cols), BF16),
            vm((4, length, LANES), F32),
            vm((2, 512, wide_half), F32),
            vm((2, 512, wide_half), BF16),
            vm((2, 512, span), F32),
            vm((2, span, deep), F32),
            vm((2, span, deep), BF16),
            vm((deep, span), BF16),
            vm((deep, span), BF16),
            vm((span, deep), BF16),
            pltpu.SemaphoreType.DMA((6, 2, 3)),
            pltpu.SemaphoreType.DMA((6, 2, 3)),
            pltpu.SemaphoreType.DMA((7,)),
            pltpu.SemaphoreType.DMA((7,)),
            pltpu.SemaphoreType.DMA((12,)),
            pltpu.SemaphoreType.DMA((12,)),
            pltpu.SemaphoreType.DMA((4, 3)),
        ],
        compiler_params=pltpu.CompilerParams(
            collective_id=0, has_side_effects=True, vmem_limit_bytes=62 << 20
        ),
        cost_estimate=pl.CostEstimate(flops=0, bytes_accessed=500_000_000, transcendentals=0),
        name="sum_over_dp",
    )(stack, small, keep, sent, x, mid_grad, fs, gain, mid, returned, select, *pieces)


def per_device(
    layer_input,
    attn_norm,
    w_query,
    w_key,
    w_value,
    query_norm,
    key_norm,
    w_output,
    moe_norm,
    w_router,
    w_gate,
    w_up,
    w_down,
    segments,
    positions,
    routes,
    out_grad,
):
    length, quarter = layer_input.shape
    width = 4 * quarter
    rank_t = lax.axis_index("tensor")
    core = rank_t % 2
    low_x = rank_t // 2 == 0
    high_group = (lax.axis_index("dp") // 4) % 2 == 1
    first_side = jnp.logical_xor(low_x, high_group)
    groups = lax.axis_size("dp")
    experts = 2 * groups

    def own(vector):
        return lax.dynamic_slice_in_dim(vector, rank_t * quarter, quarter, 0)

    cosine, sine = rope_angles(positions[0])
    labels = segments[0]
    gain_q = query_norm[None, :]
    gain_k = key_norm[None, :]
    gain_1 = attn_norm[None, :]
    gain_2 = moe_norm[None, :]
    by_side = jnp.arange(experts, dtype=jnp.int32).reshape(groups, 2).T.reshape(experts, 1)
    router_by_side = w_router.reshape(width, groups, 2).transpose(2, 1, 0).reshape(experts, width)
    (
        normed_in, first_scale, qpre, kpre, query, key, values, mixed, mid, mids, grads_full, normed_mid, gates,
        place, rows, grad_rows, *expert_weights,
    ) = run_front(
        layer_input, out_grad, gain_1, gain_2, w_query, w_key, w_value, w_output, gain_q, gain_k,
        cosine, sine, labels, routes.T, by_side, router_by_side, w_gate, w_up, w_down, groups,
    )

    gates_side = jnp.where(first_side, gates[:groups], gates[groups:])
    spots = core * HALF + jnp.arange(HALF, dtype=jnp.int32)
    select_gated = (
        jnp.where(place[:, None, :] == spots[None, :, None], gates_side[:, None, :], 0.0)
        .astype(BF16)
        .reshape(groups * HALF, length)
    )

    expert_out, back_rows, *pieces = run_experts(rows, grad_rows, expert_weights)

    stack, small, mid_grad, keep, sent, returned = run_middle(
        back_rows, expert_out, place, gates, normed_mid, router_by_side, mid, out_grad, mids,
        grads_full, gain_2, normed_in, w_query, w_key, w_value, w_output, gain_q, gain_k, cosine,
        sine, labels, qpre, kpre, query, key, values, mixed,
    )

    big, everywhere, input_grad, layer_output, *halves = run_tail(
        stack, small, keep, sent, layer_input, mid_grad, first_scale, own(attn_norm)[None, :], mid,
        returned.reshape(groups * HALF, width), select_gated, pieces,
    )
    kept, others = halves[:3], halves[3:]
    expert_grads = []
    for mine, other in zip(kept, others):
        other = other.astype(F32)
        expert_grads.append(
            jnp.stack([jnp.where(first_side, mine, other), jnp.where(first_side, other, mine)])
        )
    small = lax.dynamic_index_in_dim(everywhere, rank_t, 0, keepdims=False)
    everywhere = everywhere.astype(F32)
    rows_w = w_query.shape[0]
    rows_o = w_output.shape[0]
    summed = [big[width + i * rows_w : width + (i + 1) * rows_w].astype(F32) for i in range(3)]
    output_grad = jnp.concatenate(
        [big[i * rows_o : (i + 1) * rows_o] for i in range(4)], axis=1
    ).astype(F32)
    return (
        layer_output,
        input_grad,
        everywhere[:, experts].reshape(width),
        summed[0],
        summed[1],
        summed[2],
        small[experts + 2].astype(F32),
        small[experts + 3].astype(F32),
        output_grad,
        everywhere[:, experts + 1].reshape(width),
        everywhere[:, :experts]
        .reshape(4, 2, groups, quarter)
        .transpose(0, 3, 2, 1)
        .reshape(width, experts),
        expert_grads[0],
        expert_grads[1],
        expert_grads[2],
    )


def solution(mesh):
    placed = (
        P("dp", "tensor"),
        P(),
        P(None, "tensor"),
        P(None, "tensor"),
        P(None, "tensor"),
        P("tensor"),
        P("tensor"),
        P("tensor", None),
        P(),
        P(),
        P("dp", None, "tensor"),
        P("dp", None, "tensor"),
        P("dp", "tensor", None),
        P("dp", None),
        P("dp", None),
        P("dp", None),
        P("dp", "tensor"),
    )
    return jax.shard_map(
        per_device,
        mesh=mesh,
        in_specs=placed,
        out_specs=(
            P("dp", "tensor"),
            P("dp", "tensor"),
            P(),
            P(None, "tensor"),
            P(None, "tensor"),
            P(None, "tensor"),
            P("tensor"),
            P("tensor"),
            P("tensor", None),
            P(),
            P(),
            P("dp", None, "tensor"),
            P("dp", None, "tensor"),
            P("dp", "tensor", None),
        ),
        check_vma=False,
    )
```

time: 925 us -> 508 us (0.55)
  the two profiles are of different devices: /device:TPU:0 before, /device:TPU:2 now
where the time goes in v2:
time: 508 us; the launch traced here: 499 us
  Pallas kernels  463 us (91%)
  other arithmetic  22.1 us (4%)
  local copies, waits for them, and re-layouts  13 us (3%)
    pallas_call x1, Pallas kernels, run_tail(): pl.pallas_call(tail_body, in_specs=[whole] * 11 + [free] * 6, out_specs=[...  158 us
    pallas_call x1, Pallas kernels, run_front(): pl.pallas_call(front_body, in_specs=[whole] * 17 + [free] * 3, out_specs=...  148 us
    pallas_call x1, Pallas kernels, run_middle(): pl.pallas_call(middle_body, in_specs=[whole, free] + [whole] * 26, out_sp...  82.9 us
    pallas_call x1, Pallas kernels, run_experts(): pl.pallas_call(expert_body, in_specs=[free] * 5, out_specs=[whole] + [fre...  74 us
    another operation x6, other arithmetic, per_device(): jnp.stack([jnp.where(first_side, mine, other), jnp.where(first_side, othe...  10.2 us

profile of v2, /device:TPU:2, one launch (start us, length us, event | category | flops | bytes accessed | tf_op | source)
XLA Modules:
  0.0 499.0 jit_solution(12953331834406091415)
XLA Ops:
  1.4 0.8 fusion.7
  2.1 0.9 pad_maximum_fusion.3
  3.1 1.1 reshape.113
  4.2 0.8 copy.34
  5.0 0.8 copy.35.col_ref
  6.5 147.8 %front.1 = (bf16[384,2048]{1,0:T(8,128)(2,1)}, f32[384,1]{1,0:T(8,128)}, f32[384,512]{1,0:T(8,128)}, f32[384,512]{1,0:T(8,128)}, bf16[384,512]{1,0:T(8,128)(2,1)...) custom-call(f32[384,512]{1,0:T(8,128)} %x_ref.3, ...), custom_call_target="tpu_custom_call" | custom-call | tf_op jit(solution)/shard_map/front/pallas_call | solution.py:600
  154.3 74.0 %experts.1 = (bf16[32,32,2048]{2,1,0:T(8,128)(2,1)}, bf16[32,32,2176]{2,1,0:T(8,128)(2,1)}, f32[2048,512]{1,0:T(8,128)}, f32[2048,512]{1,0:T(8,128)}, f32[512,20...) custom-call(bf16[32,32,2176]{2,1,0:T(8,128)(2,1)} %get-tuple-element.57.rows_in, ...), custom_call_target="tpu_custom_call" | custom-call | tf_op jit(solution)/shard_map/experts/pallas_call | solution.py:279
  228.4 82.9 %middle.1 = (bf16[8192,512]{1,0:T(8,128)(2,1)}, bf16[80,512]{1,0:T(8,128)(2,1)}, f32[384,512]{1,0:T(8,128)}, f32[384,1024]{1,0:T(8,128)}, bf16[384,1024]{1,0:T(8,128)(2,1)}, /*index=5*/bf16[32,32,2048]{2,1,0:T(8,128)(2,1)}) custom-call(bf16[32,32,2176]{2,1,0:T(8,128)(2,1)} %get-tuple-element.62.rows_ref, bf16[32,32,2048]{2,1,0:T(8,128)(2,1)} %get-tuple-element.63.out_rows, ...), custom_call_target="tpu_custom_call" | custom-call | tf_op jit(solution)/shard_map/middle/pallas_call | solution.py:805
  311.5 1.1 fusion.6.sel_ref
  312.6 1.3 dynamic_slice.7
  313.9 157.8 %sum_over_dp.1 = (bf16[8192,512]{1,0:T(8,128)(2,1)}, bf16[4,80,512]{2,1,0:T(8,128)(2,1)}, f32[384,512]{1,0:T(8,128)}, f32[384,512]{1,0:T(8,128)}, f32[2048,256]{...) custom-call(bf16[8192,512]{1,0:T(8,128)(2,1)} %get-tuple-element.77., ...), custom_call_target="tpu_custom_call" | custom-call | bytes 500000000 | tf_op jit(solution)/shard_map/sum_over_dp/pallas_call | solution.py:1105
  471.7 2.4 fusion.4
  474.1 2.4 pad_maximum_fusion.2
  476.5 0.9 copy-done.3
  477.8 2.4 pad_maximum_fusion.1
  480.2 0.9 copy-done.2
  481.5 2.4 pad_maximum_fusion
  483.9 0.9 slice-done
  484.9 1.4 slice-done.1
  486.4 2.6 maximum_convert_fusion
  488.9 5.2 %slice_convert_fusion = (f32[2048,512]{1,0:T(8,128)}, f32[2048,512]{1,0:T(8,128)}, f32[2048,512]{1,0:T(8,128)}) fusion(bf16[8192,512]{1,0:T(8,128)(2,1)S(1)} %bitcast.46), kind=kLoop, calls=%fused_computation.16 | loop fusion | flops 3145728 | bytes 18874368 | tf_op jit(solution)/shard_map/convert_element_type | solution.py:1235
  494.6 1.0 copy.39
  496.8 0.9 copy.42
  497.7 0.9 copy.43
  (36 shorter events, 3.9 us)
Async XLA Ops:
  0.6 4.3 copy-start.9
  228.4 83.0 %copy-start.7 = (f32[64,384]{1,0:T(8,128)S(1)}, f32[64,384]{1,0:T(8,128)}, u32[]{:S(2)}) copy-start(f32[64,384]{1,0:T(8,128)} %get-tuple-element.65.gates_ref) | copy-start | bytes 294916
  228.4 83.1 %copy-start.8 = (s32[32,384]{1,0:T(8,128)S(1)}, s32[32,384]{1,0:T(8,128)}, u32[]{:S(2)}) copy-start(s32[32,384]{1,0:T(8,128)} %get-tuple-element.64.place_ref) | copy-start | bytes 147460
  474.1 2.4 copy-start.1
  474.1 3.4 copy-start.3
  477.8 2.4 copy-start
  477.8 3.4 copy-start.2
  481.2 3.7 slice-start
  481.5 4.7 slice-start.1
  488.9 5.3 %copy-start.4 = (bf16[4,80,512]{2,1,0:T(8,128)(2,1)S(1)}, bf16[4,80,512]{2,1,0:T(8,128)(2,1)}, u32[]{:S(2)}) copy-start(bf16[4,80,512]{2,1,0:T(8,128)(2,1)} %get-tuple-element.92) | copy-start | bytes 983044
  494.2 2.6 copy-start.6
  494.3 3.4 copy-start.5

commit v3 on v2

--- a/solution.py
+++ b/solution.py
@@ -18,6 +18,7 @@
 MESH = pl.DeviceIdType.MESH
 SMALL = 80
 LANES = 128
+LATE = 8
 
 
 def dot(a, b, dims, **kw):
@@ -74,10 +75,10 @@
 
 
 def expert_body(
-    rows_in, og_in, wg_all, wu_all, wd_all,
+    rows_in, rows_late, og_in, wg_all, wu_all, wd_all,
     out_ref, back_in, kept_g, kept_u, kept_d, got_g, got_u, got_d,
     rows_s, og_s, wgu_s, wd_s, back_s, gu_s, hid_s, keep_s, move_s, down_keep, down_move,
-    rs_sem, og_sem, w_sem, bs, br, ls, ks, ms, mr,
+    rs_sem, og_sem, w_sem, bs, br, ls, ks, ms, mr, late_s, late_r,
 ):
     plane = Plane()
     swap = (plane.dp, lax.axis_index("tensor") + 1 - 2 * plane.core)
@@ -88,9 +89,16 @@
     per = groups // 4
     tile = per * slots
 
+    late = rows_late.shape[0]
+    early = groups - late
+
     def load(e, _):
-        g = plane.entry(e)
-        pltpu.make_async_copy(rows_in.at[g], rows_s.at[e], rs_sem.at[e // per]).start()
+        g = plane.source(e)
+
+        @pl.when(e < early)
+        def _():
+            pltpu.make_async_copy(rows_in.at[g], rows_s.at[e], rs_sem.at[e // per]).start()
+
         pltpu.make_async_copy(og_in.at[g], og_s.at[e], og_sem.at[e // per]).start()
         return 0
 
@@ -114,8 +122,26 @@
     pl.semaphore_signal(barrier, inc=1, device_id=swap, device_id_type=MESH)
     pl.semaphore_wait(barrier, groups)
 
+    def late_copy(i):
+        return pltpu.make_async_remote_copy(
+            src_ref=rows_late.at[i],
+            dst_ref=rows_s.at[early + i],
+            send_sem=late_s.at[i],
+            recv_sem=late_r.at[i],
+            device_id=plane.device(plane.entry(early + i)),
+            device_id_type=MESH,
+        )
+
+    def late_start(i, _):
+        late_copy(i).start()
+        return 0
+
+    lax.fori_loop(0, late - 1, late_start, 0)
+    own_rows = pltpu.make_async_copy(rows_late.at[late - 1], rows_s.at[groups - 1], ls.at[3])
+    own_rows.start()
+
     def back_copy(e):
-        g = plane.entry(e)
+        g = plane.source(e)
         return pltpu.make_async_remote_copy(
             src_ref=back_s.at[e],
             dst_ref=back_in.at[plane.dp],
@@ -131,7 +157,27 @@
         first = pl.multiple_of(k * per, per)
         here = pl.ds(pl.multiple_of(k * tile, tile), tile)
         part = pl.ds(first, per)
-        pltpu.make_async_copy(rows_in.at[pl.ds(0, per)], rows_s.at[part], rs_sem.at[k]).wait()
+
+        @pl.when(k < early // per)
+        def _():
+            pltpu.make_async_copy(rows_in.at[pl.ds(0, per)], rows_s.at[part], rs_sem.at[k]).wait()
+
+        @pl.when(k >= early // per)
+        def _():
+            def arrive(j, _):
+                i = first + j - early
+
+                @pl.when(i < late - 1)
+                def _():
+                    late_copy(i).wait()
+
+                @pl.when(i == late - 1)
+                def _():
+                    own_rows.wait()
+
+                return 0
+
+            lax.fori_loop(0, per, arrive, 0)
 
         @pl.when(k == 0)
         def _():
@@ -264,7 +310,7 @@
     own_back.wait()
 
 
-def run_experts(rows, grads, weights):
+def run_experts(rows, late, grads, weights):
     groups, slots, more = rows.shape
     width = grads.shape[2]
     hidden = 4 * weights[0].shape[2]
@@ -278,7 +324,7 @@
     dma = pltpu.SemaphoreType.DMA
     return pl.pallas_call(
         expert_body,
-        in_specs=[free] * 5,
+        in_specs=[free] * 6,
         out_specs=[whole] + [free] * 7,
         out_shape=[
             f((groups, slots, width), BF16),
@@ -307,16 +353,18 @@
             dma((3, 4)),
             dma((31,)),
             dma((31,)),
-            dma((3,)),
+            dma((4,)),
             dma((2, 2)),
             dma((3, 2)),
             dma((width // block + 1, 2)),
+            dma((late.shape[0],)),
+            dma((late.shape[0],)),
         ],
         compiler_params=pltpu.CompilerParams(
             collective_id=2, has_side_effects=True, vmem_limit_bytes=61 << 20
         ),
         name="experts",
-    )(rows, grads, *weights)
+    )(rows, late, grads, *weights)
 
 
 def head_scale(pre):
@@ -411,6 +459,10 @@
         o = jnp.where(e == 31, 0, lax.rem(11 * e + 5, 31) + 1)
         return self.at(o // 8, lax.rem(o // 4, 2), lax.rem(o, 4))
 
+    def source(self, e):
+        o = jnp.where(e == 31, 0, lax.rem(11 * e + 5, 31) + 1)
+        return self.at(4 - o // 8, 2 - lax.rem(o // 4, 2), 4 - lax.rem(o, 4))
+
     def greet(self, barrier):
         def one(e, _):
             pl.semaphore_signal(
@@ -420,11 +472,11 @@
 
         lax.fori_loop(0, 31, one, 0)
 
-    def exchange(self, source, target, send_sems, recv_sems, local_sem, ordered):
+    def exchange(self, source, target, send_sems, recv_sems, local_sem, back, count=32):
         def copy(e):
-            group = self.entry(e)
+            group = self.source(e) if back else self.entry(e)
             return pltpu.make_async_remote_copy(
-                src_ref=source.at[e if ordered else group],
+                src_ref=source.at[e if back else group],
                 dst_ref=target.at[self.dp],
                 send_sem=send_sems.at[e],
                 recv_sem=recv_sems.at[e],
@@ -440,13 +492,17 @@
             copy(e).wait()
             return 0
 
-        own = pltpu.make_async_copy(source.at[31 if ordered else self.dp], target.at[self.dp], local_sem)
-        lax.fori_loop(0, 31, start, 0)
-        own.start()
+        lax.fori_loop(0, min(count, 31), start, 0)
+        if count == 32:
+            own = pltpu.make_async_copy(
+                source.at[31 if back else self.dp], target.at[self.dp], local_sem
+            )
+            own.start()
 
         def wait():
-            lax.fori_loop(0, 31, finish, 0)
-            own.wait()
+            lax.fori_loop(0, min(count, 31), finish, 0)
+            if count == 32:
+                own.wait()
 
         return wait
 
@@ -459,9 +515,9 @@
     x_ref, og_ref, gain1_ref, gain2_ref, wq_ref, wk_ref, wv_ref, wo_ref, qn_ref, kn_ref, cos_ref,
     sin_ref, col_ref, row_ref, routes_ref, ids_ref, router_ref, wg_ref, wu_ref, wd_ref,
     normed_ref, fs_ref, qpre_ref, kpre_ref, q_ref, k_ref, v_ref, mixed_ref, mid_ref, mids_ref, ogs_ref,
-    nm_ref, gates_ref, place_ref, rows_in, og_in, wg_all, wu_all, wd_all,
+    nm_ref, gates_ref, place_ref, rows_in, rows_late, og_in, wg_all, wu_all, wd_all,
     xs, low_s, high_s, sent, got, go, back, og_out, rows_out,
-    ts, tr, as_, ar, bs, br, ls,
+    ts, tr, as_, ar, bs, br, ls, late_sem,
 ):
     near = Near(ts, tr)
     plane = Plane()
@@ -575,12 +631,29 @@
             jnp.where(hit, gate, 0.0).reshape(8 * HALF, length), axis=1, keepdims=True
         )
         rows_out[i * 8 : (i + 1) * 8, :, width:] = two_parts(column).reshape(8, HALF, LANES)
-    rows_wait = plane.exchange(rows_out, rows_in, bs, br, ls.at[1], False)
+    early = 32 - rows_late.shape[0]
+    rows_wait = plane.exchange(rows_out, rows_in, bs, br, ls.at[1], False, early)
+
+    def late_copy(i):
+        return pltpu.make_async_copy(
+            rows_out.at[plane.entry(early + i)], rows_late.at[i], late_sem.at[i]
+        )
+
+    def late_start(i, _):
+        late_copy(i).start()
+        return 0
+
+    def late_wait(i, _):
+        late_copy(i).wait()
+        return 0
+
+    lax.fori_loop(0, 32 - early, late_start, 0)
     for c, (w, w_all) in zip(w_cross, weights):
         c.wait()
         w_swap.append(near.send(w_all.at[1], w_all.at[3], near.swap))
     og_wait()
     rows_wait()
+    lax.fori_loop(0, 32 - early, late_wait, 0)
     for c in w_swap + kept:
         c.wait()
 
@@ -600,7 +673,7 @@
     return pl.pallas_call(
         front_body,
         in_specs=[whole] * 17 + [free] * 3,
-        out_specs=[whole] * 14 + [free] * 5,
+        out_specs=[whole] * 14 + [free] * 6,
         out_shape=[
             f((length, width), BF16),
             f((length, 1), F32),
@@ -617,6 +690,7 @@
             f((2 * groups, length), F32),
             f((groups, length), jnp.int32),
             f((groups, HALF, width + LANES), BF16),
+            f((LATE, HALF, width + LANES), BF16),
             f((groups, HALF, width), BF16),
             f((4,) + wg.shape[1:], BF16),
             f((4,) + wu.shape[1:], BF16),
@@ -639,6 +713,7 @@
             dma((31,)),
             dma((31,)),
             dma((5,)),
+            dma((LATE,)),
         ],
         compiler_params=pltpu.CompilerParams(
             collective_id=1, has_side_effects=True, vmem_limit_bytes=60 << 20
@@ -652,13 +727,28 @@
 
 def middle_body(
     rows_ref, out_rows, place_ref, gates_ref, nm_ref, router_ref, mid_ref, og_ref, mids_ref, ogs_ref,
-    gain_ref, normed_ref, wq_ref, wk_ref, wv_ref, wo_ref, qn_ref, kn_ref, cos_ref, sin_ref, col_ref,
+    gain_ref, normed_in, wq_in, wk_in, wv_in, wo_in, qn_ref, kn_ref, cos_ref, sin_ref, col_ref,
     row_ref, qpre_ref, kpre_ref, q_ref, k_ref, v_ref, mixed_ref,
     stack_ref, small_ref, mid_grad_ref, keep_ref, sent_ref, returned,
-    low_s, low_f, high_f, sent, got, go, back, ngs, gg_s, ts, tr, os, orr, ls,
+    low_s, low_f, high_f, sent, got, go, back, ngs, gg_s, probs_s, normed_ref, wq_ref, wk_ref, wv_ref,
+    wo_ref, ts, tr, os, orr, ls,
 ):
     near = Near(ts, tr)
     plane = Plane()
+    loads = [
+        pltpu.make_async_copy(source, target, ls.at[1 + i])
+        for i, (source, target) in enumerate(
+            (
+                (wo_in, wo_ref),
+                (wq_in, wq_ref),
+                (wk_in, wk_ref),
+                (wv_in, wv_ref),
+                (normed_in, normed_ref),
+            )
+        )
+    ]
+    for c in loads:
+        c.start()
     side = plane.side
     t = near.t
     groups, slots, more = rows_ref.shape
@@ -716,11 +806,22 @@
     mid = wide(mids_ref).astype(F32)
     scale = lax.rsqrt(jnp.mean(mid * mid, axis=1, keepdims=True) + EPS)
     mid_own = mid_ref[...]
+    same = col_ref[...] == row_ref[...]
+    heads = inner // HDIM
+
+    def attention_probs(h):
+        at = slice(h * HDIM, (h + 1) * HDIM)
+        probs_s[h] = softmax_rows(q_ref[:, at], k_ref[:, at], same)
+
+    for h in range(heads // 2):
+        attention_probs(h)
     crossed.wait()
     ng = jnp.where(near.low_x, low, high) + back[...].astype(F32) + router_back
     ngs[t] = ng.astype(BF16)
     ng_copies = near.gather_start(ngs)
     moe = jnp.sum(ng * mid_own * scale, axis=0, keepdims=True)
+    for h in range(heads // 2, heads):
+        attention_probs(h)
     near.gather_relay(ngs, ng_copies)
     for c in ng_copies[1:]:
         c.wait()
@@ -730,13 +831,14 @@
     mid_grad_ref[...] = og_ref[...] + scale * (ng * gain_ref[:, mine]) - mid_own * shrink
     attn_grad = (wide(ogs_ref).astype(F32) + scale * weighted - mid * shrink).astype(BF16)
 
+    for c in loads:
+        c.wait()
     wo_grad = tn(mixed_ref[...], attn_grad).astype(BF16)
     for i in range(4):
         stack_ref[i * inner : (i + 1) * inner, :] = wo_grad[:, i * quarter : (i + 1) * quarter]
     mixed_grad = nt(attn_grad, wo_ref[...]).astype(BF16)
     cosine = cos_ref[...]
     sine = sin_ref[...]
-    same = col_ref[...] == row_ref[...]
     factor = HDIM ** (-0.5)
 
     def norm_back(pre, gain, rotated):
@@ -753,7 +855,7 @@
         query = q_ref[:, at]
         key = k_ref[:, at]
         mg = mixed_grad[:, at]
-        probs = softmax_rows(query, key, same)
+        probs = probs_s[h]
         low_s[:, 2 * inner + h * HDIM : 2 * inner + (h + 1) * HDIM] = tn(
             probs.astype(BF16), mg
         ).astype(BF16)
@@ -804,7 +906,7 @@
     dma = pltpu.SemaphoreType.DMA
     return pl.pallas_call(
         middle_body,
-        in_specs=[whole, free] + [whole] * 26,
+        in_specs=[whole, free] + [whole] * 9 + [free] * 5 + [whole] * 12,
         out_specs=[whole] * 5 + [free],
         out_shape=[
             f((4 * width, quarter), BF16),
@@ -824,11 +926,17 @@
             vm((length, quarter), BF16),
             vm((4, length, quarter), BF16),
             vm((4, groups, length), F32),
+            vm((inner // HDIM, length, length), F32),
+            vm(normed.shape, BF16),
+            vm(wq.shape, BF16),
+            vm(wk.shape, BF16),
+            vm(wv.shape, BF16),
+            vm(wo.shape, BF16),
             dma((8,)),
             dma((8,)),
             dma((31,)),
             dma((31,)),
-            dma((1,)),
+            dma((6,)),
         ],
         compiler_params=pltpu.CompilerParams(
             collective_id=3, has_side_effects=True, vmem_limit_bytes=61 << 20
@@ -844,8 +952,8 @@
     stack_ref, small_ref, keep_ref, sent_ref, x_ref, mid_grad_ref, fs_ref, gain_ref, mid_ref,
     ret_ref, sel_ref, kept_g, kept_u, kept_d, got_g, got_u, got_d,
     out_ref, small_out_ref, input_ref, layer_ref, mine_g, mine_u, mine_d, other_g, other_u, other_d,
-    recv1, buf1, recv2, buf2, recv3, small_in, got, out_sent, out_got, go, back, out_go, out_back,
-    mean_in, kb, gb, nb, kd, gd, far_g, far_u, far_d, ss, rs, sss, srs, ts, tr, ws,
+    own_s, ret_s, recv1, buf1, recv2, buf2, recv3, small_in, got, out_sent, out_got, go, back, out_go, out_back,
+    mean_in, kb, gb, nb, kd, gd, far_g, far_u, far_d, ss, rs, sss, srs, ts, tr, ws, ls,
 ):
     dp = lax.axis_index("dp")
     t = lax.axis_index("tensor")
@@ -856,8 +964,11 @@
     first_core = core == 0
     low_x = t < 2
     half = stack_ref.shape[0] // 2
-    n1, n2, n3 = half // 4, half // 16, half // 32
+    size = half // 2
+    n1, n2, n3 = size // 4, size // 16, size // 32
     quarter = x_ref.shape[1]
+    ret_load = pltpu.make_async_copy(ret_ref, ret_s, ls.at[4])
+    ret_load.start()
 
     def at_z(k):
         return ((lax.rem(z + k, 4) * 2 + xh) * 4 + y, t)
@@ -900,18 +1011,25 @@
         return send(source, target, (ts.at[k], tr.at[k]), device)
 
     def rows_at(start, size):
-        return pl.ds(pl.multiple_of(start, 128), size)
+        return pl.ds(pl.multiple_of(start, 64), size)
 
     ways = (((z, at_z), (y, at_y)), ((y, at_y), (z, at_z)))
-    first, second, third = [], [], []
-    for h in range(2):
-        pos, at = ways[h][0]
+    streams = [(ways[h], h * half + s * size) for s in range(2) for h in range(2)]
+    first, second, third, ahead, later, ended, own_loads, bases = [], [], [], [], [], [], [], []
+    for n, (((pos, at), _), start) in enumerate(streams):
         for k in range(1, 4):
-            there = rows_at(h * half + lax.rem(pos + k, 4) * n1, n1)
-            first.append(copy(stack_ref.at[there], recv1.at[h, k - 1], 0, h, k - 1, at(k)))
+            there = rows_at(start + lax.rem(pos + k, 4) * n1, n1)
+            first.append(copy(stack_ref.at[there], recv1.at[n, k - 1], 0, n, k - 1, at(k)))
+        bases.append(start + pos * n1)
+    for n, base in enumerate(bases):
+        own_loads.append(
+            pltpu.make_async_copy(stack_ref.at[rows_at(base, n1)], own_s.at[n], ls.at[n])
+        )
+        own_loads[-1].start()
 
     swapped = near(sent_ref, got, 0, at_swap)
-    part = tn(sel_ref[...], ret_ref[...])
+    ret_load.wait()
+    part = tn(sel_ref[...], ret_s[...])
     p = [part[:, i * quarter : (i + 1) * quarter] for i in range(4)]
     out_sent[:, :quarter] = jnp.where(first_core, p[1], p[0]).astype(BF16)
     out_sent[:, quarter:] = jnp.where(first_core, p[3], p[2]).astype(BF16)
@@ -955,56 +1073,60 @@
     layer_ref[...] = mid_ref[...] + (jnp.where(low_x, out_low, out_high) + out_back[...].astype(F32))
 
     block = kb.shape[1]
-    loads = []
-    for kept, gotten in ((kept_g, got_g), (kept_u, got_u)):
-        for i in range(kept_g.shape[0] // block):
-            slot = len(loads) % 2
+    span = far_d.shape[0]
+
+    def column_sums(kept, gotten, far, mine):
+        loads, stores = [], []
+        count = kept.shape[0] // block
+        for i in range(count):
             at = slice(i * block, (i + 1) * block)
             loads.append(
                 (
-                    pltpu.make_async_copy(kept.at[at], kb.at[slot], ws.at[slot, 0]),
-                    pltpu.make_async_copy(gotten.at[at], gb.at[slot], ws.at[slot, 1]),
+                    pltpu.make_async_copy(kept.at[at], kb.at[i % 2], ws.at[i % 2, 0]),
+                    pltpu.make_async_copy(gotten.at[at], gb.at[i % 2], ws.at[i % 2, 1]),
                 )
             )
-    span = far_d.shape[0]
-    down_loads = [
-        (
-            pltpu.make_async_copy(kept_d.at[at], kd.at[i], ws.at[2 + i, 0]),
-            pltpu.make_async_copy(got_d.at[at], gd.at[i], ws.at[2 + i, 1]),
-        )
-        for i, at in enumerate((slice(0, span), slice(span, 2 * span)))
-    ]
-    for c in loads[0] + down_loads[0] + down_loads[1]:
-        c.start()
-    stores = []
-    for n, pair in enumerate(loads):
-        if n + 1 < len(loads):
-            for c in loads[n + 1]:
+        for c in loads[0]:
+            c.start()
+        for i in range(count):
+            if i + 1 < count:
+                for c in loads[i + 1]:
+                    c.start()
+            for c in loads[i]:
+                c.wait()
+            slot = i % 2
+            at = slice(i * block, (i + 1) * block)
+            total = kb[slot] + gb[slot].astype(F32)
+            if i >= 2:
+                stores[i - 2].wait()
+            nb[slot] = total[:, :span]
+            far[at, :] = total[:, span:].astype(BF16)
+            stores.append(pltpu.make_async_copy(nb.at[slot], mine.at[at], ws.at[slot, 2]))
+            stores[-1].start()
+        for c in stores[-2:]:
+            c.wait()
+
+    def row_sums():
+        loads = [
+            (
+                pltpu.make_async_copy(kept_d.at[at], kd.at[i], ws.at[2 + i, 0]),
+                pltpu.make_async_copy(got_d.at[at], gd.at[i], ws.at[2 + i, 1]),
+            )
+            for i, at in enumerate((slice(span, 2 * span), slice(0, span)))
+        ]
+        for pair in loads:
+            for c in pair:
                 c.start()
-        for c in pair:
+        for c in loads[0]:
             c.wait()
-        slot = n % 2
-        per = len(loads) // 2
-        far, mine = ((far_g, mine_g), (far_u, mine_u))[n // per]
-        at = slice((n % per) * block, (n % per + 1) * block)
-        total = kb[slot] + gb[slot].astype(F32)
-        if n >= 2:
-            stores[n - 2].wait()
-        nb[slot] = total[:, :span]
-        far[at, :] = total[:, span:].astype(BF16)
-        stores.append(pltpu.make_async_copy(nb.at[slot], mine.at[at], ws.at[slot, 2]))
-        stores[-1].start()
-        if n == per - 1:
-            others = [near(far_g, other_g, 6, at_cross)]
-    for pair in down_loads:
-        for c in pair:
+        far_d[...] = (kd[0] + gd[0].astype(F32)).astype(BF16)
+        others.append(near(far_d, other_d, 8, at_cross))
+        for c in loads[1]:
             c.wait()
-    kd[0] = kd[0] + gd[0].astype(F32)
-    far_d[...] = (kd[1] + gd[1].astype(F32)).astype(BF16)
-    stores.append(pltpu.make_async_copy(kd.at[0], mine_d, ws.at[2, 2]))
-    stores[-1].start()
-    for c in stores[-3:]:
-        c.wait()
+        kd[1] = kd[1] + gd[1].astype(F32)
+        store = pltpu.make_async_copy(kd.at[1], mine_d, ws.at[2, 2])
+        store.start()
+        return store
 
     def small_total(start, count):
         total = small_in[start].astype(F32)
@@ -1012,79 +1134,93 @@
             total = total + small_in[i].astype(F32)
         return total.astype(BF16)
 
-    bases = []
-    for h in range(2):
-        pos, _ = ways[h][0]
-        for c in first[3 * h : 3 * h + 3]:
+    def first_sum(n):
+        for c in first[3 * n : 3 * n + 3]:
             c.wait()
-        base = h * half + pos * n1
-        step = n1 // 4
-
-        def add_first(i, _, h=h, base=base):
-            here = rows_at(i * step, step)
-            total = stack_ref[rows_at(base + i * step, step), :].astype(F32)
-            for k in range(3):
-                total = total + recv1[h, k, here, :].astype(F32)
-            buf1[h, here, :] = total.astype(BF16)
-            return 0
-
-        lax.fori_loop(0, n1 // step, add_first, 0)
-        pos2, at2 = ways[h][1]
+        own_loads[n].wait()
+        total = own_s[n].astype(F32)
+        for k in range(3):
+            total = total + recv1[n, k].astype(F32)
+        buf1[n] = total.astype(BF16)
+        _, (pos, at) = streams[n][0]
         for k in range(1, 4):
-            there = rows_at(lax.rem(pos2 + k, 4) * n2, n2)
-            second.append(copy(buf1.at[h, there], recv2.at[h, k - 1], 1, h, k - 1, at2(k)))
-        bases.append(base)
+            there = rows_at(lax.rem(pos + k, 4) * n2, n2)
+            second.append(copy(buf1.at[n, there], recv2.at[n, k - 1], 1, n, k - 1, at(k)))
+        bases[n] = bases[n] + pos * n2
+
+    def second_sum(n):
+        for c in second[3 * n : 3 * n + 3]:
+            c.wait()
+        _, (pos, _) = streams[n][0]
+        total = buf1[n, rows_at(pos * n2, n2), :].astype(F32)
+        for k in range(3):
+            total = total + recv2[n, k].astype(F32)
+        buf2[n] = total.astype(BF16)
+        third.append(
+            copy(buf2.at[n, rows_at((1 - xh) * n3, n3)], recv3.at[n], 2, n, 0, at_x)
+        )
+
+    def third_sum(n):
+        third[n].wait()
+        total = buf2[n, rows_at(xh * n3, n3), :].astype(F32) + recv3[n].astype(F32)
+        here = rows_at(bases[n] + xh * n3, n3)
+        out_ref[here, :] = total.astype(BF16)
+        ahead.append(copy(out_ref.at[here], out_ref.at[here], 3, n, 0, at_x))
+
+    def share_second(n):
+        ahead[n].wait()
+        here = rows_at(bases[n], n2)
+        _, (_, at) = streams[n][0]
+        for k in range(1, 4):
+            later.append(copy(out_ref.at[here], out_ref.at[here], 4, n, k - 1, at(k)))
+
+    def share_first(n):
+        for c in later[3 * n : 3 * n + 3]:
+            c.wait()
+        ((pos, at), _), start = streams[n]
+        here = rows_at(start + pos * n1, n1)
+        for k in range(1, 4):
+            ended.append(copy(out_ref.at[here], out_ref.at[here], 5, n, k - 1, at(k)))
+
+    column_sums(kept_g, got_g, far_g, mine_g)
+    others = [near(far_g, other_g, 6, at_cross)]
+    first_sum(0)
+    first_sum(1)
+    column_sums(kept_u, got_u, far_u, mine_u)
+    first_sum(2)
+    first_sum(3)
     for c in small:
         c.wait()
     small_in[4 + y] = small_total(0, 4)
     small = [small_copy(4 + y, 3 + k - 1, at_y(k)) for k in range(1, 4)]
-    for h in range(2):
-        pos2, _ = ways[h][1]
-        for c in second[3 * h : 3 * h + 3]:
-            c.wait()
-        total = buf1[h, rows_at(pos2 * n2, n2), :].astype(F32)
-        for k in range(3):
-            total = total + recv2[h, k].astype(F32)
-        buf2[h] = total.astype(BF16)
-        third.append(
-            copy(buf2.at[h, rows_at((1 - xh) * n3, n3)], recv3.at[h], 2, h, 0, at_x)
-        )
-        bases[h] = bases[h] + pos2 * n2
+    second_sum(0)
+    second_sum(1)
+    third_sum(0)
+    third_sum(1)
+    second_sum(2)
+    second_sum(3)
     for c in small:
         c.wait()
     small_in[8 + xh] = small_total(4, 4)
     small = small_copy(8 + xh, 6, at_x)
-    ahead = []
-    for h in range(2):
-        third[h].wait()
-        total = buf2[h, rows_at(xh * n3, n3), :].astype(F32) + recv3[h].astype(F32)
-        here = rows_at(bases[h] + xh * n3, n3)
-        out_ref[here, :] = total.astype(BF16)
-        ahead.append(copy(out_ref.at[here], out_ref.at[here], 3, h, 0, at_x))
-    later = []
-    for c in ahead:
-        c.wait()
+    share_second(0)
+    share_second(1)
+    third_sum(2)
+    third_sum(3)
+    share_first(0)
+    share_first(1)
+    share_second(2)
+    share_second(3)
     others.append(near(far_u, other_u, 7, at_cross))
-    others.append(near(far_d, other_d, 8, at_cross))
-    for h in range(2):
-        _, at2 = ways[h][1]
-        here = rows_at(bases[h], n2)
-        for k in range(1, 4):
-            later.append(copy(out_ref.at[here], out_ref.at[here], 4, h, k - 1, at2(k)))
+    share_first(2)
+    share_first(3)
     small.wait()
     small_out_ref[t] = small_total(8, 2)
     small = [
         near(small_out_ref.at[t], small_out_ref.at[t], 9 + i, there)
         for i, there in enumerate((at_swap, at_cross, at_diag))
     ]
-    ended = []
-    for h in range(2):
-        for c in later[3 * h : 3 * h + 3]:
-            c.wait()
-        pos, at = ways[h][0]
-        here = rows_at(h * half + pos * n1, n1)
-        for k in range(1, 4):
-            ended.append(copy(out_ref.at[here], out_ref.at[here], 5, h, k - 1, at(k)))
+    row_sums().wait()
     for c in small + others + ended:
         c.wait()
 
@@ -1104,7 +1240,7 @@
     vm = pltpu.VMEM
     return pl.pallas_call(
         tail_body,
-        in_specs=[whole] * 11 + [free] * 6,
+        in_specs=[free] + [whole] * 8 + [free, whole] + [free] * 6,
         out_specs=[whole] * 4 + [free] * 6,
         out_shape=[
             f(stack.shape, BF16),
@@ -1115,11 +1251,13 @@
         + [f(shape, F32) for shape in shapes]
         + [f(shape, BF16) for shape in shapes],
         scratch_shapes=[
-            vm((2, 3, half // 4, cols), BF16),
-            vm((2, half // 4, cols), BF16),
-            vm((2, 3, half // 16, cols), BF16),
-            vm((2, half // 16, cols), BF16),
-            vm((2, half // 32, cols), BF16),
+            vm((4, half // 8, cols), BF16),
+            vm(returned.shape, BF16),
+            vm((4, 3, half // 8, cols), BF16),
+            vm((4, half // 8, cols), BF16),
+            vm((4, 3, half // 32, cols), BF16),
+            vm((4, half // 32, cols), BF16),
+            vm((4, half // 64, cols), BF16),
             vm((10,) + small.shape, BF16),
             vm((length, 2 * cols), BF16),
             vm((length, 2 * cols), BF16),
@@ -1137,13 +1275,14 @@
             vm((deep, span), BF16),
             vm((deep, span), BF16),
             vm((span, deep), BF16),
-            pltpu.SemaphoreType.DMA((6, 2, 3)),
-            pltpu.SemaphoreType.DMA((6, 2, 3)),
+            pltpu.SemaphoreType.DMA((6, 4, 3)),
+            pltpu.SemaphoreType.DMA((6, 4, 3)),
             pltpu.SemaphoreType.DMA((7,)),
             pltpu.SemaphoreType.DMA((7,)),
             pltpu.SemaphoreType.DMA((12,)),
             pltpu.SemaphoreType.DMA((12,)),
             pltpu.SemaphoreType.DMA((4, 3)),
+            pltpu.SemaphoreType.DMA((5,)),
         ],
         compiler_params=pltpu.CompilerParams(
             collective_id=0, has_side_effects=True, vmem_limit_bytes=62 << 20
@@ -1195,7 +1334,7 @@
     router_by_side = w_router.reshape(width, groups, 2).transpose(2, 1, 0).reshape(experts, width)
     (
         normed_in, first_scale, qpre, kpre, query, key, values, mixed, mid, mids, grads_full, normed_mid, gates,
-        place, rows, grad_rows, *expert_weights,
+        place, rows, late_rows, grad_rows, *expert_weights,
     ) = run_front(
         layer_input, out_grad, gain_1, gain_2, w_query, w_key, w_value, w_output, gain_q, gain_k,
         cosine, sine, labels, routes.T, by_side, router_by_side, w_gate, w_up, w_down, groups,
@@ -1209,7 +1348,7 @@
         .reshape(groups * HALF, length)
     )
 
-    expert_out, back_rows, *pieces = run_experts(rows, grad_rows, expert_weights)
+    expert_out, back_rows, *pieces = run_experts(rows, late_rows, grad_rows, expert_weights)
 
     stack, small, mid_grad, keep, sent, returned = run_middle(
         back_rows, expert_out, place, gates, normed_mid, router_by_side, mid, out_grad, mids,

time: 508 us -> 472 us (0.929)
  the two profiles are of different devices: /device:TPU:2 before, /device:TPU:34 now
where the time goes in v3:
time: 472 us; the launch traced here: 463 us
  Pallas kernels  427 us (90%)
  other arithmetic  22.1 us (5%)
  local copies, waits for them, and re-layouts  13 us (3%)
    pallas_call x1, Pallas kernels, run_tail(): pl.pallas_call(tail_body, in_specs=[free] + [whole] * 8 + [free, whole] +...  149 us
    pallas_call x1, Pallas kernels, run_front(): pl.pallas_call(front_body, in_specs=[whole] * 17 + [free] * 3, out_specs=...  138 us
    pallas_call x1, Pallas kernels, run_experts(): pl.pallas_call(expert_body, in_specs=[free] * 6, out_specs=[whole] + [fre...  72.3 us
    pallas_call x1, Pallas kernels, run_middle(): pl.pallas_call(middle_body, in_specs=[whole, free] + [whole] * 9 + [free]...  67.8 us
    another operation x6, other arithmetic, per_device(): jnp.stack([jnp.where(first_side, mine, other), jnp.where(first_side, othe...  10.2 us

profile of v3, /device:TPU:34, one launch (start us, length us, event | category | flops | bytes accessed | tf_op | source)
XLA Modules:
  0.0 463.3 jit_solution(2498685922068731922)
XLA Ops:
  1.4 0.8 fusion.7
  2.1 0.9 pad_maximum_fusion.3
  3.1 1.1 reshape.113
  4.2 0.8 copy.34
  5.0 0.8 copy.35.col_ref
  6.5 137.6 %front.1 = (bf16[384,2048]{1,0:T(8,128)(2,1)}, f32[384,1]{1,0:T(8,128)}, f32[384,512]{1,0:T(8,128)}, f32[384,512]{1,0:T(8,128)}, bf16[384,512]{1,0:T(8,128)(2,1)...) custom-call(f32[384,512]{1,0:T(8,128)} %x_ref.3, ...), custom_call_target="tpu_custom_call" | custom-call | tf_op jit(solution)/shard_map/front/pallas_call | solution.py:673
  144.1 72.3 %experts.1 = (bf16[32,32,2048]{2,1,0:T(8,128)(2,1)}, bf16[32,32,2176]{2,1,0:T(8,128)(2,1)}, f32[2048,512]{1,0:T(8,128)}, f32[2048,512]{1,0:T(8,128)}, f32[512,20...) custom-call(bf16[32,32,2176]{2,1,0:T(8,128)(2,1)} %get-tuple-element.58.rows_in, ...), custom_call_target="tpu_custom_call" | custom-call | tf_op jit(solution)/shard_map/experts/pallas_call | solution.py:325
  216.5 67.8 %middle.1 = (bf16[8192,512]{1,0:T(8,128)(2,1)}, bf16[80,512]{1,0:T(8,128)(2,1)}, f32[384,512]{1,0:T(8,128)}, f32[384,1024]{1,0:T(8,128)}, bf16[384,1024]{1,0:T(8,128)(2,1)}, /*index=5*/bf16[32,32,2048]{2,1,0:T(8,128)(2,1)}) custom-call(bf16[32,32,2176]{2,1,0:T(8,128)(2,1)} %get-tuple-element.64.rows_ref, bf16[32,32,2048]{2,1,0:T(8,128)(2,1)} %get-tuple-element.65.out_rows, ...), custom_call_target="tpu_custom_call" | custom-call | tf_op jit(solution)/shard_map/middle/pallas_call | solution.py:907
  284.5 1.1 fusion.6.sel_ref
  285.6 1.3 dynamic_slice.7
  286.9 149.4 %sum_over_dp.1 = (bf16[8192,512]{1,0:T(8,128)(2,1)}, bf16[4,80,512]{2,1,0:T(8,128)(2,1)}, f32[384,512]{1,0:T(8,128)}, f32[384,512]{1,0:T(8,128)}, f32[2048,256]{...) custom-call(bf16[8192,512]{1,0:T(8,128)(2,1)} %get-tuple-element.79., ...), custom_call_target="tpu_custom_call" | custom-call | bytes 500000000 | tf_op jit(solution)/shard_map/sum_over_dp/pallas_call | solution.py:1241
  436.3 2.4 fusion.4
  438.7 2.4 pad_maximum_fusion.2
  441.1 0.9 copy-done.3
  442.4 2.4 pad_maximum_fusion.1
  444.8 0.9 copy-done.2
  446.1 2.4 pad_maximum_fusion
  448.5 0.9 slice-done
  449.4 1.4 slice-done.1
  450.9 2.6 maximum_convert_fusion
  453.5 5.2 %slice_convert_fusion = (f32[2048,512]{1,0:T(8,128)}, f32[2048,512]{1,0:T(8,128)}, f32[2048,512]{1,0:T(8,128)}) fusion(bf16[8192,512]{1,0:T(8,128)(2,1)S(1)} %bitcast.46), kind=kLoop, calls=%fused_computation.16 | loop fusion | flops 3145728 | bytes 18874368 | tf_op jit(solution)/shard_map/convert_element_type | solution.py:1374
  459.2 1.0 copy.39
  461.3 0.9 copy.42
  462.2 0.9 copy.43
  (36 shorter events, 3.9 us)
Async XLA Ops:
  0.6 4.3 copy-start.9
  216.5 67.9 %copy-start.7 = (f32[64,384]{1,0:T(8,128)S(1)}, f32[64,384]{1,0:T(8,128)}, u32[]{:S(2)}) copy-start(f32[64,384]{1,0:T(8,128)} %get-tuple-element.67.gates_ref) | copy-start | bytes 294916
  216.5 68.0 %copy-start.8 = (s32[32,384]{1,0:T(8,128)S(1)}, s32[32,384]{1,0:T(8,128)}, u32[]{:S(2)}) copy-start(s32[32,384]{1,0:T(8,128)} %get-tuple-element.66.place_ref) | copy-start | bytes 147460
  438.7 2.4 copy-start.1
  438.7 3.4 copy-start.3
  442.4 2.4 copy-start
  442.4 3.4 copy-start.2
  445.7 3.7 slice-start
  446.0 4.7 %slice-start.1 = ((s8[8388608]{0:T(1024)(128)(4,1)}), s8[4194304]{0:T(1024)(128)(4,1)S(1)}, s32[]{:S(2)}) async-start(s8[8388608]{0:T(1024)(128)(4,1)} %bitcast.45), calls=%async_computation.1 | async-start | bytes 8388608
  453.5 5.3 %copy-start.4 = (bf16[4,80,512]{2,1,0:T(8,128)(2,1)S(1)}, bf16[4,80,512]{2,1,0:T(8,128)(2,1)}, u32[]{:S(2)}) copy-start(bf16[4,80,512]{2,1,0:T(8,128)(2,1)} %get-tuple-element.94) | copy-start | bytes 983044
  458.7 2.6 copy-start.6
  458.8 3.4 copy-start.5

commit v4 on v3

--- a/solution.py
+++ b/solution.py
@@ -1,4 +1,4 @@
-import functools
+import math
 
 import jax
 import jax.numpy as jnp
@@ -35,29 +35,6 @@
 
 def tn(a, b):
     return dot(a, b, ((0,), (0,)))
-
-
-def cross(value):
-    return lax.ppermute(value, "tensor", [(0, 2), (2, 0), (1, 3), (3, 1)])
-
-
-def swap(value):
-    return lax.ppermute(value, "tensor", [(0, 1), (1, 0), (2, 3), (3, 2)])
-
-
-def inv_rms(value):
-    return lax.rsqrt(jnp.mean(value * value, axis=-1, keepdims=True) + EPS)
-
-
-def rope_angles(places):
-    half = HDIM // 2
-    frequency = jnp.exp(jnp.arange(half, dtype=F32) * (-2.0 * jnp.log(10000.0) / HDIM))
-    angle = places.astype(F32)[:, None] * frequency[None, :]
-    cosine, sine = jnp.cos(angle), jnp.sin(angle)
-    return (
-        jnp.concatenate([cosine, cosine], axis=1),
-        jnp.concatenate([-sine, sine], axis=1),
-    )
 
 
 def two_parts(column):
@@ -455,13 +432,18 @@
     def device(self, group):
         return (group, lax.rem(self.side + lax.rem(group // 4, 2), 2) * 2 + self.core)
 
+    def offset(self, e):
+        dz = 3 - lax.rem(e, 4)
+        dx = 1 - lax.rem(e // 4, 2)
+        dy = lax.rem(e // 8 + 1 + dz, 4)
+        return dz, dx, dy
+
     def entry(self, e):
-        o = jnp.where(e == 31, 0, lax.rem(11 * e + 5, 31) + 1)
-        return self.at(o // 8, lax.rem(o // 4, 2), lax.rem(o, 4))
+        return self.at(*self.offset(e))
 
     def source(self, e):
-        o = jnp.where(e == 31, 0, lax.rem(11 * e + 5, 31) + 1)
-        return self.at(4 - o // 8, 2 - lax.rem(o // 4, 2), 4 - lax.rem(o, 4))
+        dz, dx, dy = self.offset(e)
+        return self.at(4 - dz, 2 - dx, 4 - dy)
 
     def greet(self, barrier):
         def one(e, _):
@@ -511,10 +493,21 @@
     return jnp.concatenate([buf[i] for i in range(4)], axis=1)
 
 
+def as_column(row):
+    return jnp.broadcast_to(row.astype(F32), (LANES, row.shape[1])).T[:, :1]
+
+
+def by_side(experts):
+    half = experts // 2
+    r = lax.broadcasted_iota(jnp.int32, (experts, experts), 0)
+    e = lax.broadcasted_iota(jnp.int32, (experts, experts), 1)
+    return jnp.where(e == 2 * lax.rem(r, half) + r // half, 1.0, 0.0)
+
+
 def front_body(
-    x_ref, og_ref, gain1_ref, gain2_ref, wq_ref, wk_ref, wv_ref, wo_ref, qn_ref, kn_ref, cos_ref,
-    sin_ref, col_ref, row_ref, routes_ref, ids_ref, router_ref, wg_ref, wu_ref, wd_ref,
-    normed_ref, fs_ref, qpre_ref, kpre_ref, q_ref, k_ref, v_ref, mixed_ref, mid_ref, mids_ref, ogs_ref,
+    x_ref, og_ref, gain1_ref, gain2_ref, wq_ref, wk_ref, wv_ref, wo_ref, qn_ref, kn_ref, places_ref,
+    row_ref, routes_ref, router_ref, wg_ref, wu_ref, wd_ref,
+    cos_ref, sin_ref, normed_ref, fs_ref, qpre_ref, kpre_ref, q_ref, k_ref, v_ref, mixed_ref, mid_ref, mids_ref, ogs_ref,
     nm_ref, gates_ref, place_ref, rows_in, rows_late, og_in, wg_all, wu_all, wd_all,
     xs, low_s, high_s, sent, got, go, back, og_out, rows_out,
     ts, tr, as_, ar, bs, br, ls, late_sem,
@@ -543,9 +536,12 @@
     ]
     w_cross = [near.send(wg_ref.at[1 - side], wg_all.at[1], near.cross)]
 
-    chosen = routes_ref[0:1, :] == ids_ref[...]
+    experts_all = router_ref.shape[1]
+    number = lax.broadcasted_iota(jnp.int32, (experts_all, length), 0)
+    number = 2 * lax.rem(number, experts_all // 2) + number // (experts_all // 2)
+    chosen = routes_ref[0:1, :] == number
     for k in range(1, TOP):
-        chosen = jnp.logical_or(chosen, routes_ref[k : k + 1, :] == ids_ref[...])
+        chosen = jnp.logical_or(chosen, routes_ref[k : k + 1, :] == number)
     mask = jnp.where(chosen, 1.0, 0.0)
     earlier = lax.broadcasted_iota(jnp.int32, (length, length), 0) < lax.broadcasted_iota(
         jnp.int32, (length, length), 1
@@ -586,9 +582,15 @@
     qpre_ref[...] = qpre
     kpre_ref[...] = kpre
     v_ref[...] = nn(normed, wv_ref[...]).astype(BF16)
-    cosine = cos_ref[...]
-    sine = sin_ref[...]
-    same = col_ref[...] == row_ref[...]
+    lane = lax.broadcasted_iota(jnp.int32, (1, HDIM), 1)
+    half = HDIM // 2
+    step = lax.rem(lane, half).astype(F32) * (-2.0 * math.log(10000.0) / HDIM)
+    angle = as_column(places_ref[...]) * jnp.exp(step)
+    cosine = jnp.cos(angle)
+    sine = jnp.sin(angle) * jnp.where(lane < half, -1.0, 1.0)
+    cos_ref[...] = cosine
+    sin_ref[...] = sine
+    same = as_column(row_ref[...]) == row_ref[...].astype(F32)
     for h in range(q_ref.shape[1] // HDIM):
         at = slice(h * HDIM, (h + 1) * HDIM)
         qh = qpre[:, at]
@@ -614,7 +616,9 @@
     normed = (mid * scale * gain2_ref[...]).astype(BF16)
     nm_ref[...] = normed
 
-    logits = nt(router_ref[...], normed)
+    logits = dot(
+        by_side(experts_all), nn(normed, router_ref[...]), ((1,), (1,)), precision=HIGH
+    )
     masked = jnp.where(chosen, logits, -1e30)
     raised = jnp.where(chosen, jnp.exp(masked - jnp.max(masked, axis=0, keepdims=True)), 0.0)
     gates = raised / jnp.sum(raised, axis=0, keepdims=True)
@@ -659,8 +663,7 @@
 
 
 def run_front(
-    x, og, gain1, gain2, wq, wk, wv, wo, qn, kn, cosine, sine, labels, routes, ids, router, wg, wu,
-    wd, groups,
+    x, og, gain1, gain2, wq, wk, wv, wo, qn, kn, places, labels, routes, router, wg, wu, wd, groups
 ):
     length, quarter = x.shape
     width = 4 * quarter
@@ -672,9 +675,11 @@
     dma = pltpu.SemaphoreType.DMA
     return pl.pallas_call(
         front_body,
-        in_specs=[whole] * 17 + [free] * 3,
-        out_specs=[whole] * 14 + [free] * 6,
+        in_specs=[whole] * 14 + [free] * 3,
+        out_specs=[whole] * 16 + [free] * 6,
         out_shape=[
+            f((length, HDIM), F32),
+            f((length, HDIM), F32),
             f((length, width), BF16),
             f((length, 1), F32),
             f((length, inner), F32),
@@ -720,14 +725,13 @@
         ),
         name="front",
     )(
-        x, og, gain1, gain2, wq, wk, wv, wo, qn, kn, cosine, sine, labels[:, None], labels[None, :],
-        routes, ids, router, wg, wu, wd,
+        x, og, gain1, gain2, wq, wk, wv, wo, qn, kn, places, labels, routes, router, wg, wu, wd
     )
 
 
 def middle_body(
     rows_ref, out_rows, place_ref, gates_ref, nm_ref, router_ref, mid_ref, og_ref, mids_ref, ogs_ref,
-    gain_ref, normed_in, wq_in, wk_in, wv_in, wo_in, qn_ref, kn_ref, cos_ref, sin_ref, col_ref,
+    gain_ref, normed_in, wq_in, wk_in, wv_in, wo_in, qn_ref, kn_ref, cos_ref, sin_ref,
     row_ref, qpre_ref, kpre_ref, q_ref, k_ref, v_ref, mixed_ref,
     stack_ref, small_ref, mid_grad_ref, keep_ref, sent_ref, returned,
     low_s, low_f, high_f, sent, got, go, back, ngs, gg_s, probs_s, normed_ref, wq_ref, wk_ref, wv_ref,
@@ -796,17 +800,18 @@
     gates = gates_ref[...]
     logit_grad = gates * (gate_grad - jnp.sum(gates * gate_grad, axis=0, keepdims=True))
     mine = pl.ds(pl.multiple_of(t * quarter, quarter), quarter)
-    router_back = dot(
-        logit_grad, router_ref[:, mine].astype(F32), ((0,), (0,)), precision=HIGH
+    experts = gates.shape[0]
+    router = dot(
+        by_side(experts), router_ref[mine, :].astype(F32), ((1,), (1,)), precision=HIGH
     )
-    experts = gates.shape[0]
+    router_back = dot(logit_grad, router, ((0,), (0,)), precision=HIGH)
     small_ref[:experts, :] = dot(
         logit_grad, nm_ref[:, mine].astype(F32), ((1,), (0,)), precision=HIGH
     ).astype(BF16)
     mid = wide(mids_ref).astype(F32)
     scale = lax.rsqrt(jnp.mean(mid * mid, axis=1, keepdims=True) + EPS)
     mid_own = mid_ref[...]
-    same = col_ref[...] == row_ref[...]
+    same = as_column(row_ref[...]) == row_ref[...].astype(F32)
     heads = inner // HDIM
 
     def attention_probs(h):
@@ -906,7 +911,7 @@
     dma = pltpu.SemaphoreType.DMA
     return pl.pallas_call(
         middle_body,
-        in_specs=[whole, free] + [whole] * 9 + [free] * 5 + [whole] * 12,
+        in_specs=[whole, free] + [whole] * 9 + [free] * 5 + [whole] * 11,
         out_specs=[whole] * 5 + [free],
         out_shape=[
             f((4 * width, quarter), BF16),
@@ -944,16 +949,17 @@
         name="middle",
     )(
         rows, out_rows, place, gates, nm, router, mid, og, mids, ogs, gain, normed, wq, wk, wv, wo,
-        qn, kn, cosine, sine, labels[:, None], labels[None, :], qpre, kpre, q, k, v, mixed,
+        qn, kn, cosine, sine, labels, qpre, kpre, q, k, v, mixed,
     )
 
 
 def tail_body(
     stack_ref, small_ref, keep_ref, sent_ref, x_ref, mid_grad_ref, fs_ref, gain_ref, mid_ref,
-    ret_ref, sel_ref, kept_g, kept_u, kept_d, got_g, got_u, got_d,
-    out_ref, small_out_ref, input_ref, layer_ref, mine_g, mine_u, mine_d, other_g, other_u, other_d,
+    ret_ref, place_ref, gates_ref, kept_g, kept_u, kept_d, got_g, got_u, got_d,
+    out_ref, small_out_ref, input_ref, layer_ref, full_g, full_u, full_d,
     own_s, ret_s, recv1, buf1, recv2, buf2, recv3, small_in, got, out_sent, out_got, go, back, out_go, out_back,
-    mean_in, kb, gb, nb, kd, gd, far_g, far_u, far_d, ss, rs, sss, srs, ts, tr, ws, ls,
+    mean_in, kb, gb, nb, kd, gd, far_g, far_u, far_d, other_g, other_u,
+    other_d, ss, rs, sss, srs, ts, tr, ws, ls,
 ):
     dp = lax.axis_index("dp")
     t = lax.axis_index("tensor")
@@ -1028,8 +1034,20 @@
         own_loads[-1].start()
 
     swapped = near(sent_ref, got, 0, at_swap)
+    side = lax.rem(t // 2 + xh, 2)
+    groups, slots, width = ret_ref.shape
+    length = x_ref.shape[0]
+    gates = jnp.where(side == 0, gates_ref[:groups, :], gates_ref[groups:, :])
     ret_load.wait()
-    part = tn(sel_ref[...], ret_s[...])
+    part = None
+    for i in range(groups // 8):
+        at = slice(i * 8, (i + 1) * 8)
+        spots = lax.broadcasted_iota(jnp.int32, (8, slots, length), 1) + core * slots
+        hit = jnp.broadcast_to(place_ref[at, :][:, None, :], (8, slots, length)) == spots
+        gate = jnp.broadcast_to(gates[at][:, None, :], (8, slots, length))
+        select = jnp.where(hit, gate, 0.0).reshape(8 * slots, length).astype(BF16)
+        term = tn(select, ret_s[at].reshape(8 * slots, width))
+        part = term if part is None else part + term
     p = [part[:, i * quarter : (i + 1) * quarter] for i in range(4)]
     out_sent[:, :quarter] = jnp.where(first_core, p[1], p[0]).astype(BF16)
     out_sent[:, quarter:] = jnp.where(first_core, p[3], p[2]).astype(BF16)
@@ -1050,7 +1068,7 @@
     in_grad = in_mine + back[...].astype(F32)
     x = x_ref[...]
     fs = fs_ref[...]
-    weighted = in_grad * gain_ref[...]
+    weighted = in_grad * gain_ref[:, pl.ds(pl.multiple_of(t * quarter, quarter), quarter)]
     mean = jnp.sum(weighted * x, axis=1, keepdims=True)
     mean_in[0] = jnp.broadcast_to(mean, mean_in.shape[1:])
     mean_swap = near(mean_in.at[0], mean_in.at[1], 3, at_swap)
@@ -1101,7 +1119,21 @@
                 stores[i - 2].wait()
             nb[slot] = total[:, :span]
             far[at, :] = total[:, span:].astype(BF16)
-            stores.append(pltpu.make_async_copy(nb.at[slot], mine.at[at], ws.at[slot, 2]))
+            stores.append(pltpu.make_async_copy(nb.at[slot], mine.at[side, at], ws.at[slot, 2]))
+            stores[-1].start()
+        for c in stores[-2:]:
+            c.wait()
+
+    def arrived(copy, other, full):
+        copy.wait()
+        stores = []
+        for i in range(other.shape[0] // block):
+            slot = i % 2
+            at = slice(i * block, (i + 1) * block)
+            if i >= 2:
+                stores[i - 2].wait()
+            nb[slot] = other[at, :].astype(F32)
+            stores.append(pltpu.make_async_copy(nb.at[slot], full.at[1 - side, at], ws.at[slot, 2]))
             stores[-1].start()
         for c in stores[-2:]:
             c.wait()
@@ -1124,7 +1156,7 @@
         for c in loads[1]:
             c.wait()
         kd[1] = kd[1] + gd[1].astype(F32)
-        store = pltpu.make_async_copy(kd.at[1], mine_d, ws.at[2, 2])
+        store = pltpu.make_async_copy(kd.at[1], full_d.at[side], ws.at[2, 2])
         store.start()
         return store
 
@@ -1182,11 +1214,11 @@
         for k in range(1, 4):
             ended.append(copy(out_ref.at[here], out_ref.at[here], 5, n, k - 1, at(k)))
 
-    column_sums(kept_g, got_g, far_g, mine_g)
+    column_sums(kept_g, got_g, far_g, full_g)
     others = [near(far_g, other_g, 6, at_cross)]
     first_sum(0)
     first_sum(1)
-    column_sums(kept_u, got_u, far_u, mine_u)
+    column_sums(kept_u, got_u, far_u, full_u)
     first_sum(2)
     first_sum(3)
     for c in small:
@@ -1221,12 +1253,19 @@
         for i, there in enumerate((at_swap, at_cross, at_diag))
     ]
     row_sums().wait()
-    for c in small + others + ended:
+    arrived(others[0], other_g, full_g)
+    arrived(others[1], other_u, full_u)
+    others[2].wait()
+    kd[0] = other_d[...].astype(F32)
+    store = pltpu.make_async_copy(kd.at[0], full_d.at[1 - side], ws.at[2, 2])
+    store.start()
+    store.wait()
+    for c in small + ended:
         c.wait()
 
 
 def run_tail(
-    stack, small, keep, sent, x, mid_grad, fs, gain, mid, returned, select, pieces
+    stack, small, keep, sent, x, mid_grad, fs, gain, mid, returned, place, gates, pieces
 ):
     rows, cols = stack.shape
     half = rows // 2
@@ -1240,16 +1279,15 @@
     vm = pltpu.VMEM
     return pl.pallas_call(
         tail_body,
-        in_specs=[free] + [whole] * 8 + [free, whole] + [free] * 6,
-        out_specs=[whole] * 4 + [free] * 6,
+        in_specs=[free] + [whole] * 8 + [free, whole, whole] + [free] * 6,
+        out_specs=[whole] * 4 + [free] * 3,
         out_shape=[
             f(stack.shape, BF16),
             f((4,) + small.shape, BF16),
             f(x.shape, F32),
             f(x.shape, F32),
         ]
-        + [f(shape, F32) for shape in shapes]
-        + [f(shape, BF16) for shape in shapes],
+        + [f((2,) + shape, F32) for shape in shapes],
         scratch_shapes=[
             vm((4, half // 8, cols), BF16),
             vm(returned.shape, BF16),
@@ -1275,6 +1313,9 @@
             vm((deep, span), BF16),
             vm((deep, span), BF16),
             vm((span, deep), BF16),
+        ]
+        + [vm(shape, BF16) for shape in shapes]
+        + [
             pltpu.SemaphoreType.DMA((6, 4, 3)),
             pltpu.SemaphoreType.DMA((6, 4, 3)),
             pltpu.SemaphoreType.DMA((7,)),
@@ -1289,7 +1330,7 @@
         ),
         cost_estimate=pl.CostEstimate(flops=0, bytes_accessed=500_000_000, transcendentals=0),
         name="sum_over_dp",
-    )(stack, small, keep, sent, x, mid_grad, fs, gain, mid, returned, select, *pieces)
+    )(stack, small, keep, sent, x, mid_grad, fs, gain, mid, returned, place, gates, *pieces)
 
 
 def per_device(
@@ -1314,59 +1355,34 @@
     length, quarter = layer_input.shape
     width = 4 * quarter
     rank_t = lax.axis_index("tensor")
-    core = rank_t % 2
-    low_x = rank_t // 2 == 0
-    high_group = (lax.axis_index("dp") // 4) % 2 == 1
-    first_side = jnp.logical_xor(low_x, high_group)
     groups = lax.axis_size("dp")
     experts = 2 * groups
 
-    def own(vector):
-        return lax.dynamic_slice_in_dim(vector, rank_t * quarter, quarter, 0)
-
-    cosine, sine = rope_angles(positions[0])
-    labels = segments[0]
+    labels = segments
     gain_q = query_norm[None, :]
     gain_k = key_norm[None, :]
     gain_1 = attn_norm[None, :]
     gain_2 = moe_norm[None, :]
-    by_side = jnp.arange(experts, dtype=jnp.int32).reshape(groups, 2).T.reshape(experts, 1)
-    router_by_side = w_router.reshape(width, groups, 2).transpose(2, 1, 0).reshape(experts, width)
     (
-        normed_in, first_scale, qpre, kpre, query, key, values, mixed, mid, mids, grads_full, normed_mid, gates,
+        cosine, sine, normed_in, first_scale, qpre, kpre, query, key, values, mixed, mid, mids, grads_full, normed_mid, gates,
         place, rows, late_rows, grad_rows, *expert_weights,
     ) = run_front(
         layer_input, out_grad, gain_1, gain_2, w_query, w_key, w_value, w_output, gain_q, gain_k,
-        cosine, sine, labels, routes.T, by_side, router_by_side, w_gate, w_up, w_down, groups,
+        positions, labels, routes.T, w_router, w_gate, w_up, w_down, groups,
     )
 
-    gates_side = jnp.where(first_side, gates[:groups], gates[groups:])
-    spots = core * HALF + jnp.arange(HALF, dtype=jnp.int32)
-    select_gated = (
-        jnp.where(place[:, None, :] == spots[None, :, None], gates_side[:, None, :], 0.0)
-        .astype(BF16)
-        .reshape(groups * HALF, length)
-    )
-
     expert_out, back_rows, *pieces = run_experts(rows, late_rows, grad_rows, expert_weights)
 
     stack, small, mid_grad, keep, sent, returned = run_middle(
-        back_rows, expert_out, place, gates, normed_mid, router_by_side, mid, out_grad, mids,
+        back_rows, expert_out, place, gates, normed_mid, w_router, mid, out_grad, mids,
         grads_full, gain_2, normed_in, w_query, w_key, w_value, w_output, gain_q, gain_k, cosine,
         sine, labels, qpre, kpre, query, key, values, mixed,
     )
 
-    big, everywhere, input_grad, layer_output, *halves = run_tail(
-        stack, small, keep, sent, layer_input, mid_grad, first_scale, own(attn_norm)[None, :], mid,
-        returned.reshape(groups * HALF, width), select_gated, pieces,
+    big, everywhere, input_grad, layer_output, *expert_grads = run_tail(
+        stack, small, keep, sent, layer_input, mid_grad, first_scale, gain_1, mid,
+        returned, place, gates, pieces,
     )
-    kept, others = halves[:3], halves[3:]
-    expert_grads = []
-    for mine, other in zip(kept, others):
-        other = other.astype(F32)
-        expert_grads.append(
-            jnp.stack([jnp.where(first_side, mine, other), jnp.where(first_side, other, mine)])
-        )
     small = lax.dynamic_index_in_dim(everywhere, rank_t, 0, keepdims=False)
     everywhere = everywhere.astype(F32)
     rows_w = w_query.shape[0]

time: 472 us -> 457 us (0.968)
  the two profiles are of different devices: /device:TPU:34 before, /device:TPU:0 now
where the time goes in v4:
time: 457 us; the launch traced here: 448 us
  Pallas kernels  419 us (92%)
  local copies, waits for them, and re-layouts  18.9 us (4%)
  other arithmetic  8.52 us (2%)
    pallas_call x1, Pallas kernels, run_tail(): pl.pallas_call(tail_body, in_specs=[free] + [whole] * 8 + [free, whole, w...  141 us
    pallas_call x1, Pallas kernels, run_front(): pl.pallas_call(front_body, in_specs=[whole] * 14 + [free] * 3, out_specs=...  138 us
    pallas_call x1, Pallas kernels, run_experts(): pl.pallas_call(expert_body, in_specs=[free] * 6, out_specs=[whole] + [fre...  75.9 us
    pallas_call x1, Pallas kernels, run_middle(): pl.pallas_call(middle_body, in_specs=[whole, free] + [whole] * 9 + [free]...  65.1 us
    unnamed x19, local copies, waits for them, and re-layouts  16.1 us

profile of v4, /device:TPU:0, one launch (start us, length us, event | category | flops | bytes accessed | tf_op | source)
XLA Modules:
  0.0 447.9 jit_solution(17589333803455503795)
XLA Ops:
  0.6 2.0 copy.31.router_ref
  2.6 137.9 %front.1 = (f32[384,128]{1,0:T(8,128)}, f32[384,128]{1,0:T(8,128)}, bf16[384,2048]{1,0:T(8,128)(2,1)}, f32[384,1]{1,0:T(8,128)}, f32[384,512]{1,0:T(8,128)}, /*i...) custom-call(f32[384,512]{1,0:T(8,128)} %x_ref.3, ...), custom_call_target="tpu_custom_call" | custom-call | tf_op jit(solution)/shard_map/front/pallas_call | solution.py:676
  140.5 75.9 %experts.1 = (bf16[32,32,2048]{2,1,0:T(8,128)(2,1)}, bf16[32,32,2176]{2,1,0:T(8,128)(2,1)}, f32[2048,512]{1,0:T(8,128)}, f32[2048,512]{1,0:T(8,128)}, f32[512,20...) custom-call(bf16[32,32,2176]{2,1,0:T(8,128)(2,1)} %get-tuple-element.57.rows_in, ...), custom_call_target="tpu_custom_call" | custom-call | tf_op jit(solution)/shard_map/experts/pallas_call | solution.py:302
  216.4 65.1 %middle.1 = (bf16[8192,512]{1,0:T(8,128)(2,1)}, bf16[80,512]{1,0:T(8,128)(2,1)}, f32[384,512]{1,0:T(8,128)}, f32[384,1024]{1,0:T(8,128)}, bf16[384,1024]{1,0:T(8,128)(2,1)}, /*index=5*/bf16[32,32,2048]{2,1,0:T(8,128)(2,1)}) custom-call(bf16[32,32,2176]{2,1,0:T(8,128)(2,1)} %get-tuple-element.63.rows_ref, bf16[32,32,2048]{2,1,0:T(8,128)(2,1)} %get-tuple-element.64.out_rows, ...), custom_call_target="tpu_custom_call" | custom-call | tf_op jit(solution)/shard_map/middle/pallas_call | solution.py:912
  281.5 140.5 %sum_over_dp.1 = (bf16[8192,512]{1,0:T(8,128)(2,1)}, bf16[4,80,512]{2,1,0:T(8,128)(2,1)}, f32[384,512]{1,0:T(8,128)}, f32[384,512]{1,0:T(8,128)}, f32[2,2048,256...) custom-call(bf16[8192,512]{1,0:T(8,128)(2,1)} %get-tuple-element.80.stack_ref, ...), custom_call_target="tpu_custom_call" | custom-call | bytes 500000000 | tf_op jit(solution)/shard_map/sum_over_dp/pallas_call | solution.py:1280
  422.0 0.0 copy-start
  422.0 1.8 fusion
  423.8 2.7 maximum_convert_fusion
  426.5 1.0 copy-done
  427.5 5.2 %slice_convert_fusion = (f32[2048,512]{1,0:T(8,128)}, f32[2048,512]{1,0:T(8,128)}, f32[2048,512]{1,0:T(8,128)}) fusion(bf16[8192,512]{1,0:T(8,128)(2,1)S(1)} %copy-done), kind=kLoop, calls=%fused_computation.1 | loop fusion | flops 3145728 | bytes 18874368 | tf_op jit(solution)/shard_map/convert_element_type | solution.py:1390
  432.8 0.0 copy-done.3
  432.8 0.3 copy.33
  433.2 1.0 copy.34
  434.2 0.6 fusion.1
  434.8 0.6 dynamic-slice_convert_fusion
  435.4 0.0 copy-done.5
  435.4 0.9 copy.40
  436.2 0.0 copy-done.4
  436.2 0.9 copy.41
  437.1 4.6 %copy.42 = f32[2,2048,256]{2,1,0:T(8,128)} copy(f32[2,2048,256]{2,1,0:T(8,128)} %get-tuple-element.136) | data formatting | bytes 8388608
  441.8 0.0 copy-done.2
  441.8 2.1 copy.43
  443.9 1.6 copy-done.1
  445.5 2.0 copy.44
  (6 shorter events, 0.1 us)
Async XLA Ops:
  422.0 5.5 %copy-start = (bf16[8192,512]{1,0:T(8,128)(2,1)S(1)}, bf16[8192,512]{1,0:T(8,128)(2,1)}, u32[]{:S(2)}) copy-start(bf16[8192,512]{1,0:T(8,128)(2,1)} %get-tuple-element.96) | copy-start | bytes 25165828
  427.5 5.3 %copy-start.3 = (bf16[4,80,512]{2,1,0:T(8,128)(2,1)S(1)}, bf16[4,80,512]{2,1,0:T(8,128)(2,1)}, u32[]{:S(2)}) copy-start(bf16[4,80,512]{2,1,0:T(8,128)(2,1)} %get-tuple-element.95) | copy-start | bytes 983044
  427.5 7.8 %copy-start.5 = (f32[384,512]{1,0:T(8,128)S(1)}, f32[384,512]{1,0:T(8,128)}, u32[]{:S(2)}) copy-start(f32[384,512]{1,0:T(8,128)} %get-tuple-element.125) | copy-start | bytes 2359300
  432.8 3.5 copy-start.4
  437.1 4.6 %copy-start.2 = (f32[2,2048,256]{2,1,0:T(8,128)S(1)}, f32[2,2048,256]{2,1,0:T(8,128)}, u32[]{:S(2)}) copy-start(f32[2,2048,256]{2,1,0:T(8,128)} %get-tuple-element.137) | copy-start | bytes 12582916
  441.8 3.7 copy-start.1

commit v5 on v4

--- a/solution.py
+++ b/solution.py
@@ -53,9 +53,9 @@
 
 def expert_body(
     rows_in, rows_late, og_in, wg_all, wu_all, wd_all,
-    out_ref, back_in, kept_g, kept_u, kept_d, got_g, got_u, got_d,
+    out_rows, back_in, kept_g, kept_u, kept_d, got_g, got_u, got_d,
     rows_s, og_s, wgu_s, wd_s, back_s, gu_s, hid_s, keep_s, move_s, down_keep, down_move,
-    rs_sem, og_sem, w_sem, bs, br, ls, ks, ms, mr, late_s, late_r,
+    rs_sem, og_sem, w_sem, bs, br, ls, ks, ms, mr, late_s, late_r, out_ref, out_sem,
 ):
     plane = Plane()
     swap = (plane.dp, lax.axis_index("tensor") + 1 - 2 * plane.core)
@@ -179,6 +179,7 @@
 
         low = nn(hid.astype(BF16), wd_s[...]).astype(BF16)
         out_ref[part] = low.reshape(per, slots, width)
+        pltpu.make_async_copy(out_ref.at[part], out_rows.at[part], out_sem.at[k]).start()
         pltpu.make_async_copy(og_in.at[pl.ds(0, per)], og_s.at[part], og_sem.at[k]).wait()
         grads = og_s[part].reshape(tile, width)
         slot = jnp.sum(grads.astype(F32) * low.astype(F32), axis=1, keepdims=True)
@@ -286,6 +287,13 @@
     lax.fori_loop(0, groups - 1, finish, 0)
     own_back.wait()
 
+    def stored(k, _):
+        part = pl.ds(pl.multiple_of(k * per, per), per)
+        pltpu.make_async_copy(out_ref.at[part], out_rows.at[part], out_sem.at[k]).wait()
+        return 0
+
+    lax.fori_loop(0, 4, stored, 0)
+
 
 def run_experts(rows, late, grads, weights):
     groups, slots, more = rows.shape
@@ -294,7 +302,6 @@
     half = hidden // 2
     count = groups * slots
     block = 256
-    whole = pl.BlockSpec(memory_space=pltpu.VMEM)
     free = pl.BlockSpec(memory_space=pl.ANY)
     f = jax.ShapeDtypeStruct
     vm = pltpu.VMEM
@@ -302,7 +309,7 @@
     return pl.pallas_call(
         expert_body,
         in_specs=[free] * 6,
-        out_specs=[whole] + [free] * 7,
+        out_specs=[free] * 8,
         out_shape=[
             f((groups, slots, width), BF16),
             f((groups, slots, more), BF16),
@@ -336,6 +343,8 @@
             dma((width // block + 1, 2)),
             dma((late.shape[0],)),
             dma((late.shape[0],)),
+            vm((groups, slots, width), BF16),
+            dma((4,)),
         ],
         compiler_params=pltpu.CompilerParams(
             collective_id=2, has_side_effects=True, vmem_limit_bytes=61 << 20
@@ -505,13 +514,33 @@
 
 
 def front_body(
-    x_ref, og_ref, gain1_ref, gain2_ref, wq_ref, wk_ref, wv_ref, wo_ref, qn_ref, kn_ref, places_ref,
+    x_ref, og_ref, gain1_ref, gain2_ref, wq_in, wk_in, wv_in, wo_in, qn_ref, kn_ref, places_ref,
     row_ref, routes_ref, router_ref, wg_ref, wu_ref, wd_ref,
-    cos_ref, sin_ref, normed_ref, fs_ref, qpre_ref, kpre_ref, q_ref, k_ref, v_ref, mixed_ref, mid_ref, mids_ref, ogs_ref,
-    nm_ref, gates_ref, place_ref, rows_in, rows_late, og_in, wg_all, wu_all, wd_all,
-    xs, low_s, high_s, sent, got, go, back, og_out, rows_out,
-    ts, tr, as_, ar, bs, br, ls, late_sem,
+    *rest,
 ):
+    cos_ref, sin_ref, fs_ref, gates_ref, place_ref = rest[:5]
+    outs, (rows_in, rows_late, og_in, wg_all, wu_all, wd_all), rest = rest[5:16], rest[16:22], rest[22:]
+    held, rest = rest[:11], rest[11:]
+    normed_ref, qpre_ref, kpre_ref, q_ref, k_ref, v_ref, mixed_ref, mid_ref, mids_ref, ogs_ref, nm_ref = held
+    wq_ref, wk_ref, wv_ref, wo_ref, w_sem, out_sem, *rest = rest
+    (
+        xs, low_s, high_s, sent, got, go, back, og_out, rows_out, ts, tr, as_, ar, bs, br, ls, late_sem,
+    ) = rest
+    loads = [
+        pltpu.make_async_copy(source, target, w_sem.at[i])
+        for i, (source, target) in enumerate(
+            ((wq_in, wq_ref), (wk_in, wk_ref), (wv_in, wv_ref), (wo_in, wo_ref))
+        )
+    ]
+    saves = [
+        pltpu.make_async_copy(source, target, out_sem.at[i])
+        for i, (source, target) in enumerate(zip(held, outs))
+    ]
+
+    def save(*which):
+        for i in which:
+            saves[i].start()
+
     near = Near(ts, tr)
     plane = Plane()
     side = plane.side
@@ -535,6 +564,8 @@
         for i, (w, w_all) in enumerate(weights)
     ]
     w_cross = [near.send(wg_ref.at[1 - side], wg_all.at[1], near.cross)]
+    for c in loads:
+        c.start()
 
     experts_all = router_ref.shape[1]
     number = lax.broadcasted_iota(jnp.int32, (experts_all, length), 0)
@@ -562,6 +593,7 @@
     for c in og_copies[1:]:
         c.wait()
     og = wide(ogs_ref)
+    save(9)
     for i in range(experts // 8):
         select = jnp.where(hits(i), 1.0, 0.0).reshape(8 * HALF, length).astype(BF16)
         og_out[i * 8 : (i + 1) * 8] = nn(select, og).astype(BF16).reshape(8, HALF, width)
@@ -577,6 +609,9 @@
     fs_ref[...] = scale
     normed = (x * scale * gain1_ref[...]).astype(BF16)
     normed_ref[...] = normed
+    for c in loads:
+        c.wait()
+    save(0)
     qpre = nn(normed, wq_ref[...])
     kpre = nn(normed, wk_ref[...])
     qpre_ref[...] = qpre
@@ -602,6 +637,7 @@
         probs = softmax_rows(query, key, same).astype(BF16)
         mixed_ref[:, at] = nn(probs, v_ref[:, at]).astype(BF16)
     near.split(nn(mixed_ref[...], wo_ref[...]), low_s, high_s, sent)
+    save(1, 2, 3, 4, 5, 6)
     mid = x_ref[...] + near.sum_parts(low_s, high_s, sent, got, go, back)
     mid_ref[...] = mid
     mids_ref[t] = mid.astype(BF16)
@@ -611,10 +647,12 @@
     near.gather_relay(mids_ref, mid_copies)
     for c in mid_copies[1:]:
         c.wait()
+    save(7, 8)
     mid = wide(mids_ref).astype(F32)
     scale = lax.rsqrt(jnp.mean(mid * mid, axis=1, keepdims=True) + EPS)
     normed = (mid * scale * gain2_ref[...]).astype(BF16)
     nm_ref[...] = normed
+    save(10)
 
     logits = dot(
         by_side(experts_all), nn(normed, router_ref[...]), ((1,), (1,)), precision=HIGH
@@ -658,7 +696,7 @@
     og_wait()
     rows_wait()
     lax.fori_loop(0, 32 - early, late_wait, 0)
-    for c in w_swap + kept:
+    for c in w_swap + kept + saves:
         c.wait()
 
 
@@ -673,27 +711,32 @@
     f = jax.ShapeDtypeStruct
     vm = pltpu.VMEM
     dma = pltpu.SemaphoreType.DMA
+    held = [
+        f((length, width), BF16),
+        f((length, inner), F32),
+        f((length, inner), F32),
+        f((length, inner), BF16),
+        f((length, inner), BF16),
+        f((length, inner), BF16),
+        f((length, inner), BF16),
+        f((length, quarter), F32),
+        f((4, length, quarter), BF16),
+        f((4, length, quarter), BF16),
+        f((length, width), BF16),
+    ]
     return pl.pallas_call(
         front_body,
-        in_specs=[whole] * 14 + [free] * 3,
-        out_specs=[whole] * 16 + [free] * 6,
+        in_specs=[whole] * 4 + [free] * 4 + [whole] * 6 + [free] * 3,
+        out_specs=[whole] * 5 + [free] * 17,
         out_shape=[
             f((length, HDIM), F32),
             f((length, HDIM), F32),
-            f((length, width), BF16),
             f((length, 1), F32),
-            f((length, inner), F32),
-            f((length, inner), F32),
-            f((length, inner), BF16),
-            f((length, inner), BF16),
-            f((length, inner), BF16),
-            f((length, inner), BF16),
-            f((length, quarter), F32),
-            f((4, length, quarter), BF16),
-            f((4, length, quarter), BF16),
-            f((length, width), BF16),
             f((2 * groups, length), F32),
             f((groups, length), jnp.int32),
+        ]
+        + held
+        + [
             f((groups, HALF, width + LANES), BF16),
             f((LATE, HALF, width + LANES), BF16),
             f((groups, HALF, width), BF16),
@@ -701,7 +744,11 @@
             f((4,) + wu.shape[1:], BF16),
             f((4,) + wd.shape[1:], BF16),
         ],
-        scratch_shapes=[
+        scratch_shapes=[vm(h.shape, h.dtype) for h in held]
+        + [vm(w.shape, BF16) for w in (wq, wk, wv, wo)]
+        + [
+            dma((4,)),
+            dma((11,)),
             vm((4, length, quarter), BF16),
             vm((length, quarter), F32),
             vm((length, quarter), F32),
@@ -733,8 +780,8 @@
     rows_ref, out_rows, place_ref, gates_ref, nm_ref, router_ref, mid_ref, og_ref, mids_ref, ogs_ref,
     gain_ref, normed_in, wq_in, wk_in, wv_in, wo_in, qn_ref, kn_ref, cos_ref, sin_ref,
     row_ref, qpre_ref, kpre_ref, q_ref, k_ref, v_ref, mixed_ref,
-    stack_ref, small_ref, mid_grad_ref, keep_ref, sent_ref, returned,
-    low_s, low_f, high_f, sent, got, go, back, ngs, gg_s, probs_s, normed_ref, wq_ref, wk_ref, wv_ref,
+    stack_out, small_ref, mid_grad_ref, keep_ref, sent_ref, returned,
+    low_s, low_f, high_f, sent, got, go, back, ngs, gg_s, stack_ref, probs_s, normed_ref, wq_ref, wk_ref, wv_ref,
     wo_ref, ts, tr, os, orr, ls,
 ):
     near = Near(ts, tr)
@@ -841,6 +888,15 @@
     wo_grad = tn(mixed_ref[...], attn_grad).astype(BF16)
     for i in range(4):
         stack_ref[i * inner : (i + 1) * inner, :] = wo_grad[:, i * quarter : (i + 1) * quarter]
+    saves = [
+        pltpu.make_async_copy(
+            stack_ref.at[i * width : (i + 1) * width],
+            stack_out.at[i * width : (i + 1) * width],
+            ls.at[6 + i],
+        )
+        for i in range(4)
+    ]
+    saves[0].start()
     mixed_grad = nt(attn_grad, wo_ref[...]).astype(BF16)
     cosine = cos_ref[...]
     sine = sin_ref[...]
@@ -892,8 +948,11 @@
         stack_ref[(i + 1) * width : (i + 2) * width, :] = tn(
             normed, low_s[:, i * inner : (i + 1) * inner]
         ).astype(BF16)
+        saves[i + 1].start()
 
     out_wait()
+    for c in saves:
+        c.wait()
 
 
 def run_middle(
@@ -912,7 +971,7 @@
     return pl.pallas_call(
         middle_body,
         in_specs=[whole, free] + [whole] * 9 + [free] * 5 + [whole] * 11,
-        out_specs=[whole] * 5 + [free],
+        out_specs=[free] + [whole] * 4 + [free],
         out_shape=[
             f((4 * width, quarter), BF16),
             f((SMALL, quarter), BF16),
@@ -931,6 +990,7 @@
             vm((length, quarter), BF16),
             vm((4, length, quarter), BF16),
             vm((4, groups, length), F32),
+            vm((4 * width, quarter), BF16),
             vm((inner // HDIM, length, length), F32),
             vm(normed.shape, BF16),
             vm(wq.shape, BF16),
@@ -941,7 +1001,7 @@
             dma((8,)),
             dma((31,)),
             dma((31,)),
-            dma((6,)),
+            dma((10,)),
         ],
         compiler_params=pltpu.CompilerParams(
             collective_id=3, has_side_effects=True, vmem_limit_bytes=61 << 20
@@ -1364,8 +1424,8 @@
     gain_1 = attn_norm[None, :]
     gain_2 = moe_norm[None, :]
     (
-        cosine, sine, normed_in, first_scale, qpre, kpre, query, key, values, mixed, mid, mids, grads_full, normed_mid, gates,
-        place, rows, late_rows, grad_rows, *expert_weights,
+        cosine, sine, first_scale, gates, place, normed_in, qpre, kpre, query, key, values, mixed, mid,
+        mids, grads_full, normed_mid, rows, late_rows, grad_rows, *expert_weights,
     ) = run_front(
         layer_input, out_grad, gain_1, gain_2, w_query, w_key, w_value, w_output, gain_q, gain_k,
         positions, labels, routes.T, w_router, w_gate, w_up, w_down, groups,

time: 457 us -> 442 us (0.967); the launches traced: 448 us -> 438 us
  Pallas kernels: 419 us -> 410 us
    pallas_call x2, Pallas kernels: 214 us -> 207 us  [the longest x1 133 us: run_front(): pl.pallas_call(front_body, in_specs=[whole] * 4 + [free] * 4 + [whole] *...]
where the time goes in v5:
time: 442 us; the launch traced here: 438 us
  Pallas kernels  410 us (93%)
  local copies, waits for them, and re-layouts  18.9 us (4%)
  other arithmetic  8.52 us (2%)
    pallas_call x1, Pallas kernels, run_tail(): pl.pallas_call(tail_body, in_specs=[free] + [whole] * 8 + [free, whole, w...  140 us
    pallas_call x1, Pallas kernels, run_front(): pl.pallas_call(front_body, in_specs=[whole] * 4 + [free] * 4 + [whole] *...  133 us
    pallas_call x1, Pallas kernels, run_experts(): pl.pallas_call(expert_body, in_specs=[free] * 6, out_specs=[free] * 8, ou...  73.8 us
    pallas_call x1, Pallas kernels, run_middle(): pl.pallas_call(middle_body, in_specs=[whole, free] + [whole] * 9 + [free]...  62.5 us
    unnamed x19, local copies, waits for them, and re-layouts  16.1 us

profile of v5, /device:TPU:0, one launch (start us, length us, event | category | flops | bytes accessed | tf_op | source)
XLA Modules:
  0.0 437.8 jit_solution(13458975557007861919)
XLA Ops:
  0.6 2.0 copy.31.router_ref
  2.6 132.9 %front.1 = (f32[384,128]{1,0:T(8,128)}, f32[384,128]{1,0:T(8,128)}, f32[384,1]{1,0:T(8,128)}, f32[64,384]{1,0:T(8,128)}, s32[32,384]{1,0:T(8,128)}, /*index=5*/b...) custom-call(f32[384,512]{1,0:T(8,128)} %x_ref.3, ...), custom_call_target="tpu_custom_call" | custom-call | tf_op jit(solution)/shard_map/front/pallas_call | solution.py:727
  135.5 73.8 %experts.1 = (bf16[32,32,2048]{2,1,0:T(8,128)(2,1)}, bf16[32,32,2176]{2,1,0:T(8,128)(2,1)}, f32[2048,512]{1,0:T(8,128)}, f32[2048,512]{1,0:T(8,128)}, f32[512,20...) custom-call(bf16[32,32,2176]{2,1,0:T(8,128)(2,1)} %get-tuple-element.57.rows_in, ...), custom_call_target="tpu_custom_call" | custom-call | tf_op jit(solution)/shard_map/experts/pallas_call | solution.py:309
  209.4 62.5 %middle.1 = (bf16[8192,512]{1,0:T(8,128)(2,1)}, bf16[80,512]{1,0:T(8,128)(2,1)}, f32[384,512]{1,0:T(8,128)}, f32[384,1024]{1,0:T(8,128)}, bf16[384,1024]{1,0:T(8,128)(2,1)}, /*index=5*/bf16[32,32,2048]{2,1,0:T(8,128)(2,1)}) custom-call(bf16[32,32,2176]{2,1,0:T(8,128)(2,1)} %get-tuple-element.63.rows_ref, bf16[32,32,2048]{2,1,0:T(8,128)(2,1)} %get-tuple-element.64.out_rows, ...), custom_call_target="tpu_custom_call" | custom-call | tf_op jit(solution)/shard_map/middle/pallas_call | solution.py:971
  271.9 140.3 %sum_over_dp.1 = (bf16[8192,512]{1,0:T(8,128)(2,1)}, bf16[4,80,512]{2,1,0:T(8,128)(2,1)}, f32[384,512]{1,0:T(8,128)}, f32[384,512]{1,0:T(8,128)}, f32[2,2048,256...) custom-call(bf16[8192,512]{1,0:T(8,128)(2,1)} %get-tuple-element.80.stack_ref, ...), custom_call_target="tpu_custom_call" | custom-call | bytes 500000000 | tf_op jit(solution)/shard_map/sum_over_dp/pallas_call | solution.py:1340
  412.1 0.0 copy-start
  412.2 1.8 fusion
  414.0 2.7 maximum_convert_fusion
  416.7 1.0 copy-done
  417.7 5.2 %slice_convert_fusion = (f32[2048,512]{1,0:T(8,128)}, f32[2048,512]{1,0:T(8,128)}, f32[2048,512]{1,0:T(8,128)}) fusion(bf16[8192,512]{1,0:T(8,128)(2,1)S(1)} %copy-done), kind=kLoop, calls=%fused_computation.1 | loop fusion | flops 3145728 | bytes 18874368 | tf_op jit(solution)/shard_map/convert_element_type | solution.py:1450
  422.9 0.0 copy-done.3
  423.0 0.3 copy.33
  423.3 1.0 copy.34
  424.3 0.6 fusion.1
  424.9 0.6 dynamic-slice_convert_fusion
  425.5 0.0 copy-done.5
  425.5 0.9 copy.40
  426.4 0.0 copy-done.4
  426.4 0.9 copy.41
  427.3 4.6 %copy.42 = f32[2,2048,256]{2,1,0:T(8,128)} copy(f32[2,2048,256]{2,1,0:T(8,128)} %get-tuple-element.136) | data formatting | bytes 8388608
  431.9 0.0 copy-done.2
  431.9 2.1 copy.43
  434.0 1.6 copy-done.1
  435.6 2.0 copy.44
  (6 shorter events, 0.1 us)
Async XLA Ops:
  412.1 5.5 %copy-start = (bf16[8192,512]{1,0:T(8,128)(2,1)S(1)}, bf16[8192,512]{1,0:T(8,128)(2,1)}, u32[]{:S(2)}) copy-start(bf16[8192,512]{1,0:T(8,128)(2,1)} %get-tuple-element.96) | copy-start | bytes 25165828
  417.7 5.3 %copy-start.3 = (bf16[4,80,512]{2,1,0:T(8,128)(2,1)S(1)}, bf16[4,80,512]{2,1,0:T(8,128)(2,1)}, u32[]{:S(2)}) copy-start(bf16[4,80,512]{2,1,0:T(8,128)(2,1)} %get-tuple-element.95) | copy-start | bytes 983044
  417.7 7.8 %copy-start.5 = (f32[384,512]{1,0:T(8,128)S(1)}, f32[384,512]{1,0:T(8,128)}, u32[]{:S(2)}) copy-start(f32[384,512]{1,0:T(8,128)} %get-tuple-element.125) | copy-start | bytes 2359300
  422.9 3.5 copy-start.4
  427.3 4.6 %copy-start.2 = (f32[2,2048,256]{2,1,0:T(8,128)S(1)}, f32[2,2048,256]{2,1,0:T(8,128)}, u32[]{:S(2)}) copy-start(f32[2,2048,256]{2,1,0:T(8,128)} %get-tuple-element.137) | copy-start | bytes 12582916
  431.9 3.7 copy-start.1

commit v6 on v5

--- a/solution.py
+++ b/solution.py
@@ -1017,7 +1017,7 @@
     stack_ref, small_ref, keep_ref, sent_ref, x_ref, mid_grad_ref, fs_ref, gain_ref, mid_ref,
     ret_ref, place_ref, gates_ref, kept_g, kept_u, kept_d, got_g, got_u, got_d,
     out_ref, small_out_ref, input_ref, layer_ref, full_g, full_u, full_d,
-    own_s, ret_s, recv1, buf1, recv2, buf2, recv3, small_in, got, out_sent, out_got, go, back, out_go, out_back,
+    fin_s, own_s, ret_s, recv1, buf1, recv2, buf2, recv3, small_in, got, out_sent, out_got, go, back, out_go, out_back,
     mean_in, kb, gb, nb, kd, gd, far_g, far_u, far_d, other_g, other_u,
     other_d, ss, rs, sss, srs, ts, tr, ws, ls,
 ):
@@ -1256,11 +1256,14 @@
         third[n].wait()
         total = buf2[n, rows_at(xh * n3, n3), :].astype(F32) + recv3[n].astype(F32)
         here = rows_at(bases[n] + xh * n3, n3)
-        out_ref[here, :] = total.astype(BF16)
-        ahead.append(copy(out_ref.at[here], out_ref.at[here], 3, n, 0, at_x))
+        fin_s[n] = total.astype(BF16)
+        ahead.append(copy(fin_s.at[n], out_ref.at[here], 3, n, 0, at_x))
+        own_loads.append(pltpu.make_async_copy(fin_s.at[n], out_ref.at[here], ls.at[n]))
+        own_loads[-1].start()
 
     def share_second(n):
         ahead[n].wait()
+        own_loads[4 + n].wait()
         here = rows_at(bases[n], n2)
         _, (_, at) = streams[n][0]
         for k in range(1, 4):
@@ -1340,7 +1343,7 @@
     return pl.pallas_call(
         tail_body,
         in_specs=[free] + [whole] * 8 + [free, whole, whole] + [free] * 6,
-        out_specs=[whole] * 4 + [free] * 3,
+        out_specs=[free] + [whole] * 3 + [free] * 3,
         out_shape=[
             f(stack.shape, BF16),
             f((4,) + small.shape, BF16),
@@ -1349,6 +1352,7 @@
         ]
         + [f((2,) + shape, F32) for shape in shapes],
         scratch_shapes=[
+            vm((4, half // 64, cols), BF16),
             vm((4, half // 8, cols), BF16),
             vm(returned.shape, BF16),
             vm((4, 3, half // 8, cols), BF16),

time: 442 us -> 441 us (level)
  no operation moved by 1% of the time
where the time goes in v6:
time: 441 us; the launch traced here: 436 us
  Pallas kernels  408 us (93%)
  local copies, waits for them, and re-layouts  18.9 us (4%)
  other arithmetic  8.52 us (2%)
    pallas_call x1, Pallas kernels, run_tail(): pl.pallas_call(tail_body, in_specs=[free] + [whole] * 8 + [free, whole, w...  139 us
    pallas_call x1, Pallas kernels, run_front(): pl.pallas_call(front_body, in_specs=[whole] * 4 + [free] * 4 + [whole] *...  133 us
    pallas_call x1, Pallas kernels, run_experts(): pl.pallas_call(expert_body, in_specs=[free] * 6, out_specs=[free] * 8, ou...  73.8 us
    pallas_call x1, Pallas kernels, run_middle(): pl.pallas_call(middle_body, in_specs=[whole, free] + [whole] * 9 + [free]...  62.5 us
    unnamed x19, local copies, waits for them, and re-layouts  16.1 us

profile of v6, /device:TPU:0, one launch (start us, length us, event | category | flops | bytes accessed | tf_op | source)
XLA Modules:
  0.0 436.2 jit_solution(10854755216375455427)
XLA Ops:
  0.6 2.0 copy.31.router_ref
  2.6 132.9 %front.1 = (f32[384,128]{1,0:T(8,128)}, f32[384,128]{1,0:T(8,128)}, f32[384,1]{1,0:T(8,128)}, f32[64,384]{1,0:T(8,128)}, s32[32,384]{1,0:T(8,128)}, /*index=5*/b...) custom-call(f32[384,512]{1,0:T(8,128)} %x_ref.3, ...), custom_call_target="tpu_custom_call" | custom-call | tf_op jit(solution)/shard_map/front/pallas_call | solution.py:727
  135.5 73.8 %experts.1 = (bf16[32,32,2048]{2,1,0:T(8,128)(2,1)}, bf16[32,32,2176]{2,1,0:T(8,128)(2,1)}, f32[2048,512]{1,0:T(8,128)}, f32[2048,512]{1,0:T(8,128)}, f32[512,20...) custom-call(bf16[32,32,2176]{2,1,0:T(8,128)(2,1)} %get-tuple-element.57.rows_in, ...), custom_call_target="tpu_custom_call" | custom-call | tf_op jit(solution)/shard_map/experts/pallas_call | solution.py:309
  209.4 62.5 %middle.1 = (bf16[8192,512]{1,0:T(8,128)(2,1)}, bf16[80,512]{1,0:T(8,128)(2,1)}, f32[384,512]{1,0:T(8,128)}, f32[384,1024]{1,0:T(8,128)}, bf16[384,1024]{1,0:T(8,128)(2,1)}, /*index=5*/bf16[32,32,2048]{2,1,0:T(8,128)(2,1)}) custom-call(bf16[32,32,2176]{2,1,0:T(8,128)(2,1)} %get-tuple-element.63.rows_ref, bf16[32,32,2048]{2,1,0:T(8,128)(2,1)} %get-tuple-element.64.out_rows, ...), custom_call_target="tpu_custom_call" | custom-call | tf_op jit(solution)/shard_map/middle/pallas_call | solution.py:971
  271.9 138.7 %sum_over_dp.1 = (bf16[8192,512]{1,0:T(8,128)(2,1)}, bf16[4,80,512]{2,1,0:T(8,128)(2,1)}, f32[384,512]{1,0:T(8,128)}, f32[384,512]{1,0:T(8,128)}, f32[2,2048,256...) custom-call(bf16[8192,512]{1,0:T(8,128)(2,1)} %get-tuple-element.80.stack_ref, ...), custom_call_target="tpu_custom_call" | custom-call | bytes 500000000 | tf_op jit(solution)/shard_map/sum_over_dp/pallas_call | solution.py:1343
  410.5 0.0 copy-start
  410.6 1.8 fusion
  412.4 2.7 maximum_convert_fusion
  415.0 1.0 copy-done
  416.1 5.2 %slice_convert_fusion = (f32[2048,512]{1,0:T(8,128)}, f32[2048,512]{1,0:T(8,128)}, f32[2048,512]{1,0:T(8,128)}) fusion(bf16[8192,512]{1,0:T(8,128)(2,1)S(1)} %copy-done), kind=kLoop, calls=%fused_computation.1 | loop fusion | flops 3145728 | bytes 18874368 | tf_op jit(solution)/shard_map/convert_element_type | solution.py:1454
  421.3 0.0 copy-done.3
  421.4 0.3 copy.33
  421.7 1.0 copy.34
  422.7 0.6 fusion.1
  423.3 0.6 dynamic-slice_convert_fusion
  423.9 0.0 copy-done.5
  423.9 0.9 copy.40
  424.8 0.0 copy-done.4
  424.8 0.9 copy.41
  425.7 4.6 %copy.42 = f32[2,2048,256]{2,1,0:T(8,128)} copy(f32[2,2048,256]{2,1,0:T(8,128)} %get-tuple-element.136) | data formatting | bytes 8388608
  430.3 0.0 copy-done.2
  430.3 2.1 copy.43
  432.4 1.6 copy-done.1
  434.0 2.0 copy.44
  (6 shorter events, 0.1 us)
Async XLA Ops:
  410.5 5.5 %copy-start = (bf16[8192,512]{1,0:T(8,128)(2,1)S(1)}, bf16[8192,512]{1,0:T(8,128)(2,1)}, u32[]{:S(2)}) copy-start(bf16[8192,512]{1,0:T(8,128)(2,1)} %get-tuple-element.96) | copy-start | bytes 25165828
  416.1 5.3 %copy-start.3 = (bf16[4,80,512]{2,1,0:T(8,128)(2,1)S(1)}, bf16[4,80,512]{2,1,0:T(8,128)(2,1)}, u32[]{:S(2)}) copy-start(bf16[4,80,512]{2,1,0:T(8,128)(2,1)} %get-tuple-element.95) | copy-start | bytes 983044
  416.1 7.8 %copy-start.5 = (f32[384,512]{1,0:T(8,128)S(1)}, f32[384,512]{1,0:T(8,128)}, u32[]{:S(2)}) copy-start(f32[384,512]{1,0:T(8,128)} %get-tuple-element.125) | copy-start | bytes 2359300
  421.3 3.5 copy-start.4
  425.7 4.6 %copy-start.2 = (f32[2,2048,256]{2,1,0:T(8,128)S(1)}, f32[2,2048,256]{2,1,0:T(8,128)}, u32[]{:S(2)}) copy-start(f32[2,2048,256]{2,1,0:T(8,128)} %get-tuple-element.137) | copy-start | bytes 12582916
  430.3 3.7 copy-start.1
